TPU v7x, 32 devices: a whole 2x2x4 slice. The times are simulated.
32 devices in a mesh: dp: 4 (over x, core), ctx: 2 (over y), tensor: 4 (over z).
Axes of the slice: x: 2, y: 2, z: 4, core: 2. Of those that a mesh axis runs over, the one named last changes fastest.
Arguments:
- hidden_in: bfloat16 [4, 1024, 1536], P('dp', 'ctx'), may hold values from -6 to 6
- segment_ids: int32 [4, 1024], P('dp'), may hold values from 0 to 5, never falling along the last dimension, each value on 1 to 512 neighbouring positions
- out_grad: bfloat16 [4, 1024, 1536], P('dp', 'ctx'), may hold values from -6 to 6
- norm_gains: bfloat16 [2, 2, 1536], P(None, None, ('dp', 'ctx')), may hold values from 0.5 to 1.5
- query_weight: bfloat16 [2, 1536, 1536], P(None, ('dp', 'ctx'), 'tensor'), may hold values from -0.15625 to 0.15625
- query_bias: bfloat16 [2, 12, 128], P(None, 'tensor', ('dp', 'ctx')), may hold values from -3 to 3
- kv_weight: bfloat16 [2, 1536, 512], P(None, ('dp', 'ctx')), may hold values from -0.15625 to 0.15625
- kv_bias: bfloat16 [2, 512], P(None, ('dp', 'ctx')), may hold values from -3 to 3
- out_weight: bfloat16 [2, 1536, 1536], P(None, 'tensor', ('dp', 'ctx')), may hold values from -1.25 to 1.25
- gate_up_weight: bfloat16 [2, 1536, 2, 8960], P(None, ('dp', 'ctx'), None, 'tensor'), may hold values from -0.15625 to 0.15625
- down_weight: bfloat16 [2, 8960, 1536], P(None, 'tensor', ('dp', 'ctx')), may hold values from -0.0625 to 0.0625
- norm_gains_first: float32 [2, 2, 1536], P(None, None, ('dp', 'ctx')), may hold values from -235.15102 to 235.15102
- query_weight_first: float32 [2, 1536, 1536], P(None, ('dp', 'ctx'), 'tensor'), may hold values from -71.55418 to 71.55418
- query_bias_first: float32 [2, 12, 128], P(None, 'tensor', ('dp', 'ctx')), may hold values from -71.55418 to 71.55418
- kv_weight_first: float32 [2, 1536, 512], P(None, ('dp', 'ctx')), may hold values from -175.27122 to 175.27122
- kv_bias_first: float32 [2, 512], P(None, ('dp', 'ctx')), may hold values from -175.27122 to 175.27122
- out_weight_first: float32 [2, 1536, 1536], P(None, 'tensor', ('dp', 'ctx')), may hold values from -39.191837 to 39.191837
- gate_up_weight_first: float32 [2, 1536, 2, 8960], P(None, ('dp', 'ctx'), None, 'tensor'), may hold values from -10.119288 to 10.119288
- down_weight_first: float32 [2, 8960, 1536], P(None, 'tensor', ('dp', 'ctx')), may hold values from -30.357866 to 30.357866
- norm_gains_second: float32 [2, 2, 1536], P(None, None, ('dp', 'ctx')), may hold values from 1105.92 to 17694.72
- query_weight_second: float32 [2, 1536, 1536], P(None, ('dp', 'ctx'), 'tensor'), may hold values from 102.4 to 1638.4
- query_bias_second: float32 [2, 12, 128], P(None, 'tensor', ('dp', 'ctx')), may hold values from 102.4 to 1638.4
- kv_weight_second: float32 [2, 1536, 512], P(None, ('dp', 'ctx')), may hold values from 614.4 to 9830.4
- kv_bias_second: float32 [2, 512], P(None, ('dp', 'ctx')), may hold values from 614.4 to 9830.4
- out_weight_second: float32 [2, 1536, 1536], P(None, 'tensor', ('dp', 'ctx')), may hold values from 30.72 to 491.52
- gate_up_weight_second: float32 [2, 1536, 2, 8960], P(None, ('dp', 'ctx'), None, 'tensor'), may hold values from 2.048 to 32.768
- down_weight_second: float32 [2, 8960, 1536], P(None, 'tensor', ('dp', 'ctx')), may hold values from 18.432 to 294.912
Outputs:
- block_out: bfloat16 [4, 1024, 1536], P('dp', 'ctx')
- input_grad: float32 [4, 1024, 1536], P('dp', 'ctx')
- norm_gains_grad: float32 [2, 2, 1536], P(None, None, ('dp', 'ctx'))
- query_weight_grad: float32 [2, 1536, 1536], P(None, ('dp', 'ctx'), 'tensor')
- query_bias_grad: float32 [2, 12, 128], P(None, 'tensor', ('dp', 'ctx'))
- kv_weight_grad: float32 [2, 1536, 512], P(None, ('dp', 'ctx'))
- kv_bias_grad: float32 [2, 512], P(None, ('dp', 'ctx'))
- out_weight_grad: float32 [2, 1536, 1536], P(None, 'tensor', ('dp', 'ctx'))
- gate_up_weight_grad: float32 [2, 1536, 2, 8960], P(None, ('dp', 'ctx'), None, 'tensor')
- down_weight_grad: float32 [2, 8960, 1536], P(None, 'tensor', ('dp', 'ctx'))
- norm_gains_first_new: float32 [2, 2, 1536], P(None, None, ('dp', 'ctx'))
- query_weight_first_new: float32 [2, 1536, 1536], P(None, ('dp', 'ctx'), 'tensor')
- query_bias_first_new: float32 [2, 12, 128], P(None, 'tensor', ('dp', 'ctx'))
- kv_weight_first_new: float32 [2, 1536, 512], P(None, ('dp', 'ctx'))
- kv_bias_first_new: float32 [2, 512], P(None, ('dp', 'ctx'))
- out_weight_first_new: float32 [2, 1536, 1536], P(None, 'tensor', ('dp', 'ctx'))
- gate_up_weight_first_new: float32 [2, 1536, 2, 8960], P(None, ('dp', 'ctx'), None, 'tensor')
- down_weight_first_new: float32 [2, 8960, 1536], P(None, 'tensor', ('dp', 'ctx'))
- norm_gains_second_new: float32 [2, 2, 1536], P(None, None, ('dp', 'ctx'))
- query_weight_second_new: float32 [2, 1536, 1536], P(None, ('dp', 'ctx'), 'tensor')
- query_bias_second_new: float32 [2, 12, 128], P(None, 'tensor', ('dp', 'ctx'))
- kv_weight_second_new: float32 [2, 1536, 512], P(None, ('dp', 'ctx'))
- kv_bias_second_new: float32 [2, 512], P(None, ('dp', 'ctx'))
- out_weight_second_new: float32 [2, 1536, 1536], P(None, 'tensor', ('dp', 'ctx'))
- gate_up_weight_second_new: float32 [2, 1536, 2, 8960], P(None, ('dp', 'ctx'), None, 'tensor')
- down_weight_second_new: float32 [2, 8960, 1536], P(None, 'tensor', ('dp', 'ctx'))
- norm_gains_new: float32 [2, 2, 1536], P(None, None, ('dp', 'ctx'))
- query_weight_new: float32 [2, 1536, 1536], P(None, ('dp', 'ctx'), 'tensor')
- query_bias_new: float32 [2, 12, 128], P(None, 'tensor', ('dp', 'ctx'))
- kv_weight_new: float32 [2, 1536, 512], P(None, ('dp', 'ctx'))
- kv_bias_new: float32 [2, 512], P(None, ('dp', 'ctx'))
- out_weight_new: float32 [2, 1536, 1536], P(None, 'tensor', ('dp', 'ctx'))
- gate_up_weight_new: float32 [2, 1536, 2, 8960], P(None, ('dp', 'ctx'), None, 'tensor')
- down_weight_new: float32 [2, 8960, 1536], P(None, 'tensor', ('dp', 'ctx'))
Inputs may be any that keep to these rules, and one draw needn't show every extreme that they name: `segment_ids`: within each sequence the numbers never fall; each document holds 1 to 512 tokens, and one holds exactly that many.
All inputs are finite; a program needn't handle non-finite values.
Results may differ from a plain program's by a relative error of at most 0.03.
Values may be sent and summed in bfloat16 or wider, within the bound.
A program may use at most 320 MiB of HBM per device.

v0:
```python
import jax
import jax.numpy as jnp
from jax import lax
from jax.sharding import PartitionSpec as P

H = 12
KV = 2
HD = 128
LAYERS = 2


NORM_EPS = 1e-06
ROPE_BASE = 1000000.0
MASK_FILL = -1e30
beta_first = 0.9
beta_second = 0.95
adam_eps = 1e-08
decay_rate = 0.1
adam_step = 3.0


def rotate(values, cosine, sine):
    half_width = values.shape[-1] // 2
    first_half = values[..., :half_width]
    second_half = values[..., half_width:]
    return jnp.concatenate(
        [first_half * cosine - second_half * sine, second_half * cosine + first_half * sine],
        axis=-1,
    )


def rotate_back(grad_rows, cosine, sine):
    half_width = grad_rows.shape[-1] // 2
    first_half = grad_rows[..., :half_width]
    second_half = grad_rows[..., half_width:]
    return jnp.concatenate(
        [first_half * cosine + second_half * sine, second_half * cosine - first_half * sine],
        axis=-1,
    )


def norm_back(values, norm_scale, gain, grad_rows):
    weighted = grad_rows * gain
    inner_mean = jnp.mean(weighted * values, axis=-1, keepdims=True)
    grad_values = (
        norm_scale * weighted - values * (norm_scale * norm_scale * norm_scale) * inner_mean
    )
    return (grad_values, jnp.sum(grad_rows * values * norm_scale, axis=0))


def adam_update(weight, gradient, first_old, second_old, decayed, step_rate):
    first_new = beta_first * first_old + (1.0 - beta_first) * gradient
    second_new = beta_second * second_old + (1.0 - beta_second) * gradient * gradient
    mean_hat = first_new / (1.0 - beta_first**adam_step)
    square_hat = second_new / (1.0 - beta_second**adam_step)
    new_weight = weight - step_rate * (
        mean_hat / (jnp.sqrt(square_hat) + adam_eps) + decayed * decay_rate * weight
    )
    return (first_new, second_new, new_weight)


def gather_layer(gains, w_query, b_query, w_kv, b_kv, w_out, w_gate_up, w_down):
    return (
        lax.all_gather(gains, ("dp", "ctx"), axis=1, tiled=True),
        lax.all_gather(w_query, ("dp", "ctx"), axis=0, tiled=True),
        lax.all_gather(b_query, ("dp", "ctx"), axis=1, tiled=True),
        lax.all_gather(w_kv, ("dp", "ctx"), axis=0, tiled=True),
        lax.all_gather(b_kv, ("dp", "ctx"), axis=0, tiled=True),
        lax.all_gather(w_out, ("dp", "ctx"), axis=1, tiled=True),
        lax.all_gather(w_gate_up, ("dp", "ctx"), axis=0, tiled=True),
        lax.all_gather(w_down, ("dp", "ctx"), axis=1, tiled=True),
    )


def scatter_layer(gains, w_query, b_query, w_kv, b_kv, w_out, w_gate_up, w_down):
    return (
        lax.psum_scatter(
            gains.astype(jnp.bfloat16), ("dp", "ctx"), scatter_dimension=1, tiled=True
        ).astype(jnp.float32),
        lax.psum_scatter(
            w_query.astype(jnp.bfloat16), ("dp", "ctx"), scatter_dimension=0, tiled=True
        ).astype(jnp.float32),
        lax.psum_scatter(
            b_query.astype(jnp.bfloat16), ("dp", "ctx"), scatter_dimension=1, tiled=True
        ).astype(jnp.float32),
        lax.psum_scatter(
            w_kv.astype(jnp.bfloat16), ("dp", "ctx"), scatter_dimension=0, tiled=True
        ).astype(jnp.float32),
        lax.psum_scatter(
            b_kv.astype(jnp.bfloat16), ("dp", "ctx"), scatter_dimension=0, tiled=True
        ).astype(jnp.float32),
        lax.psum_scatter(
            w_out.astype(jnp.bfloat16), ("dp", "ctx"), scatter_dimension=1, tiled=True
        ).astype(jnp.float32),
        lax.psum_scatter(
            w_gate_up.astype(jnp.bfloat16), ("dp", "ctx"), scatter_dimension=0, tiled=True
        ).astype(jnp.float32),
        lax.psum_scatter(
            w_down.astype(jnp.bfloat16), ("dp", "ctx"), scatter_dimension=1, tiled=True
        ).astype(jnp.float32),
    )


def tensor_sum(values):
    return lax.psum(values.astype(jnp.bfloat16), "tensor").astype(jnp.float32)


def masked_scores(queries, all_keys, allowed, score_scale):
    scores = (
        jnp.einsum("sqhd,skd->shqk", queries, all_keys, preferred_element_type=jnp.float32)
        * score_scale
    )
    return jnp.where(allowed, scores, MASK_FILL)


def local(
    hidden_in,
    segment_ids,
    out_grad,
    norm_gains,
    query_weight,
    query_bias,
    kv_weight,
    kv_bias,
    out_weight,
    gate_up_weight,
    down_weight,
    norm_gains_first,
    query_weight_first,
    query_bias_first,
    kv_weight_first,
    kv_bias_first,
    out_weight_first,
    gate_up_weight_first,
    down_weight_first,
    norm_gains_second,
    query_weight_second,
    query_bias_second,
    kv_weight_second,
    kv_bias_second,
    out_weight_second,
    gate_up_weight_second,
    down_weight_second,
):
    seq_count, local_len, model_width = hidden_in.shape
    seq_length = segment_ids.shape[1]
    row_count = seq_count * local_len
    heads_here = query_weight.shape[2] // HD
    local_start = lax.axis_index("ctx") * local_len
    kv_head = lax.axis_index("tensor") * heads_here // (H // KV)
    score_scale = HD ** (-0.5)
    own_segments = lax.dynamic_slice_in_dim(segment_ids, local_start, local_len, 1)
    earlier = jnp.sum(
        (segment_ids[:, None, :] < own_segments[:, :, None]).astype(jnp.int32), axis=-1
    )
    token_index = local_start + jnp.arange(local_len, dtype=jnp.int32)
    position = (token_index[None, :] - earlier).astype(jnp.float32)
    frequency = ROPE_BASE ** (-jnp.arange(HD // 2, dtype=jnp.float32) / (HD // 2))
    angles = position[..., None] * frequency
    cosine = jnp.cos(angles).reshape(row_count, 1, HD // 2)
    sine = jnp.sin(angles).reshape(row_count, 1, HD // 2)
    key_index = jnp.arange(seq_length, dtype=jnp.int32)
    allowed = (own_segments[:, :, None] == segment_ids[:, None, :]) & (
        key_index[None, None, :] <= token_index[None, :, None]
    )
    allowed = allowed[:, None]
    hidden = hidden_in.astype(jnp.float32).reshape(row_count, model_width)
    stored = []
    for layer_index in range(LAYERS):
        current = gather_layer(
            norm_gains[layer_index],
            query_weight[layer_index],
            query_bias[layer_index],
            kv_weight[layer_index],
            kv_bias[layer_index],
            out_weight[layer_index],
            gate_up_weight[layer_index],
            down_weight[layer_index],
        )
        gain_rows, w_query, b_query, w_kv, b_kv, w_out, w_gate_up, w_down = current
        gain_rows = gain_rows.astype(jnp.float32)
        scale_one = lax.rsqrt(jnp.mean(hidden * hidden, axis=-1, keepdims=True) + NORM_EPS)
        normed = (hidden * scale_one * gain_rows[0]).astype(jnp.bfloat16)
        query_lin = jnp.dot(normed, w_query, preferred_element_type=jnp.float32) + b_query.reshape(
            heads_here * HD
        ).astype(jnp.float32)
        kv_columns = jnp.concatenate(
            [
                lax.dynamic_slice_in_dim(w_kv, kv_head * HD, HD, 1),
                lax.dynamic_slice_in_dim(w_kv, (KV + kv_head) * HD, HD, 1),
            ],
            axis=1,
        )
        kv_offsets = jnp.concatenate(
            [
                lax.dynamic_slice_in_dim(b_kv, kv_head * HD, HD, 0),
                lax.dynamic_slice_in_dim(b_kv, (KV + kv_head) * HD, HD, 0),
            ],
            axis=0,
        )
        kv_lin = jnp.dot(
            normed, kv_columns, preferred_element_type=jnp.float32
        ) + kv_offsets.astype(jnp.float32)
        queries = (
            rotate(query_lin.reshape(row_count, heads_here, HD), cosine, sine)
            .astype(jnp.bfloat16)
            .reshape(seq_count, local_len, heads_here, HD)
        )
        key_rows = (
            rotate(kv_lin[:, :HD], cosine[:, 0], sine[:, 0])
            .astype(jnp.bfloat16)
            .reshape(seq_count, local_len, HD)
        )
        value_rows = kv_lin[:, HD:].astype(jnp.bfloat16).reshape(seq_count, local_len, HD)
        all_keys, all_values = (
            lax.all_gather(key_rows, "ctx", axis=1, tiled=True),
            lax.all_gather(value_rows, "ctx", axis=1, tiled=True),
        )
        scores = masked_scores(queries, all_keys, allowed, score_scale)
        row_max = jnp.max(scores, axis=-1, keepdims=True)
        exp_scores = jnp.exp(scores - row_max)
        row_total = jnp.sum(exp_scores, axis=-1, keepdims=True)
        weights = exp_scores / row_total
        log_total = row_max + jnp.log(row_total)
        mixture = jnp.einsum(
            "shqk,skd->sqhd",
            weights.astype(jnp.bfloat16),
            all_values,
            preferred_element_type=jnp.float32,
        )
        mixed_low = mixture.reshape(row_count, heads_here * HD).astype(jnp.bfloat16)
        middle = hidden + tensor_sum(jnp.dot(mixed_low, w_out, preferred_element_type=jnp.float32))
        scale_two = lax.rsqrt(jnp.mean(middle * middle, axis=-1, keepdims=True) + NORM_EPS)
        normed_two = (middle * scale_two * gain_rows[1]).astype(jnp.bfloat16)
        gate_up = jnp.einsum(
            "rd,dgf->rgf", normed_two, w_gate_up, preferred_element_type=jnp.float32
        )
        inner_low = (jax.nn.silu(gate_up[:, 0]) * gate_up[:, 1]).astype(jnp.bfloat16)
        stored.append(
            (
                hidden,
                scale_one,
                normed,
                queries,
                all_keys,
                all_values,
                log_total,
                mixed_low,
                middle,
                scale_two,
                normed_two,
                gate_up,
                inner_low,
            )
        )
        hidden = middle + tensor_sum(jnp.dot(inner_low, w_down, preferred_element_type=jnp.float32))
    block_out = hidden.astype(jnp.bfloat16).reshape(seq_count, local_len, model_width)
    grad_hidden = out_grad.astype(jnp.float32).reshape(row_count, model_width)
    layer_grads = [None] * LAYERS
    for layer_index in reversed(range(LAYERS)):
        (
            layer_input,
            scale_one,
            normed,
            queries,
            all_keys,
            all_values,
            log_total,
            mixed_low,
            middle,
            scale_two,
            normed_two,
            gate_up,
            inner_low,
        ) = stored[layer_index]
        current = gather_layer(
            norm_gains[layer_index],
            query_weight[layer_index],
            query_bias[layer_index],
            kv_weight[layer_index],
            kv_bias[layer_index],
            out_weight[layer_index],
            gate_up_weight[layer_index],
            down_weight[layer_index],
        )
        gain_rows, w_query, b_query, w_kv, b_kv, w_out, w_gate_up, w_down = current
        gain_rows = gain_rows.astype(jnp.float32)
        grad_low = grad_hidden.astype(jnp.bfloat16)
        grad_down_w = jnp.einsum(
            "rf,rd->fd", inner_low, grad_low, preferred_element_type=jnp.float32
        )
        grad_inner = jnp.einsum("rd,fd->rf", grad_low, w_down, preferred_element_type=jnp.float32)
        gate_lin = gate_up[:, 0]
        up_lin = gate_up[:, 1]
        sigmoid_gate = jax.nn.sigmoid(gate_lin)
        grad_gate = grad_inner * up_lin * sigmoid_gate * (1.0 + gate_lin * (1.0 - sigmoid_gate))
        grad_upper = grad_inner * gate_lin * sigmoid_gate
        grad_pair = jnp.stack([grad_gate, grad_upper], axis=1).astype(jnp.bfloat16)
        grad_gate_up_w = jnp.einsum(
            "rd,rgf->dgf", normed_two, grad_pair, preferred_element_type=jnp.float32
        )
        grad_normed_two = lax.psum(
            jnp.einsum(
                "rgf,dgf->rd", grad_pair, w_gate_up, preferred_element_type=jnp.float32
            ).astype(jnp.bfloat16),
            "tensor",
        ).astype(jnp.float32)
        back_two, grad_gain_two = norm_back(middle, scale_two, gain_rows[1], grad_normed_two)
        grad_middle = grad_hidden + back_two
        grad_mid_low = grad_middle.astype(jnp.bfloat16)
        grad_out_w = jnp.einsum(
            "re,rd->ed", mixed_low, grad_mid_low, preferred_element_type=jnp.float32
        )
        grad_mixed = (
            jnp.einsum("rd,ed->re", grad_mid_low, w_out, preferred_element_type=jnp.float32)
            .astype(jnp.bfloat16)
            .reshape(seq_count, local_len, heads_here, HD)
        )
        scores = masked_scores(queries, all_keys, allowed, score_scale)
        probabilities = jnp.exp(scores - log_total)
        grad_probs = jnp.einsum(
            "sqhd,skd->shqk", grad_mixed, all_values, preferred_element_type=jnp.float32
        )
        row_delta = jnp.sum(probabilities * grad_probs, axis=-1, keepdims=True)
        grad_scores = (probabilities * (grad_probs - row_delta)).astype(jnp.bfloat16)
        grad_queries = (
            jnp.einsum("shqk,skd->sqhd", grad_scores, all_keys, preferred_element_type=jnp.float32)
            * score_scale
        )
        grad_keys = (
            jnp.einsum("shqk,sqhd->skd", grad_scores, queries, preferred_element_type=jnp.float32)
            * score_scale
        )
        grad_values = jnp.einsum(
            "shqk,sqhd->skd",
            probabilities.astype(jnp.bfloat16),
            grad_mixed,
            preferred_element_type=jnp.float32,
        )
        own_grads = lax.psum_scatter(
            jnp.stack([grad_keys, grad_values], axis=2).astype(jnp.bfloat16),
            "ctx",
            scatter_dimension=1,
            tiled=True,
        ).astype(jnp.float32)
        head_mask = (jnp.arange(KV, dtype=jnp.int32) == kv_head).astype(jnp.float32)
        summed = lax.psum(
            (own_grads[:, :, :, None, :] * head_mask[:, None]).astype(jnp.bfloat16), "tensor"
        ).astype(jnp.float32)
        grad_key_lin = rotate_back(
            summed[:, :, 0].reshape(row_count, KV, HD), cosine, sine
        ).reshape(row_count, KV * HD)
        grad_kv = jnp.concatenate(
            [grad_key_lin, summed[:, :, 1].reshape(row_count, KV * HD)], axis=1
        ).astype(jnp.bfloat16)
        grad_query_lin = (
            rotate_back(grad_queries.reshape(row_count, heads_here, HD), cosine, sine)
            .reshape(row_count, heads_here * HD)
            .astype(jnp.bfloat16)
        )
        grad_query_w = jnp.einsum(
            "rd,re->de", normed, grad_query_lin, preferred_element_type=jnp.float32
        )
        grad_query_b = jnp.sum(grad_query_lin.astype(jnp.float32), axis=0).reshape(heads_here, HD)
        grad_kv_w = jnp.einsum("rd,re->de", normed, grad_kv, preferred_element_type=jnp.float32)
        grad_kv_b = jnp.sum(grad_kv.astype(jnp.float32), axis=0)
        grad_normed = lax.psum(
            jnp.einsum(
                "re,de->rd", grad_query_lin, w_query, preferred_element_type=jnp.float32
            ).astype(jnp.bfloat16),
            "tensor",
        ).astype(jnp.float32)
        grad_normed = grad_normed + jnp.einsum(
            "re,de->rd", grad_kv, w_kv, preferred_element_type=jnp.float32
        )
        back_one, grad_gain_one = norm_back(layer_input, scale_one, gain_rows[0], grad_normed)
        grad_hidden = grad_middle + back_one
        grad_gains = jnp.stack([grad_gain_one, grad_gain_two])
        grad_tuple = (
            grad_gains,
            grad_query_w,
            grad_query_b,
            grad_kv_w,
            grad_kv_b,
            grad_out_w,
            grad_gate_up_w,
            grad_down_w,
        )
        grad_tuple = scatter_layer(
            grad_gains,
            grad_query_w,
            grad_query_b,
            grad_kv_w,
            grad_kv_b,
            grad_out_w,
            grad_gate_up_w,
            grad_down_w,
        )
        layer_grads[layer_index] = grad_tuple
    stacked = [
        jnp.stack([layer_grads[layer_index][param_index] for layer_index in range(LAYERS)])
        for param_index in range(8)
    ]
    params = (
        norm_gains,
        query_weight,
        query_bias,
        kv_weight,
        kv_bias,
        out_weight,
        gate_up_weight,
        down_weight,
    )
    firsts = (
        norm_gains_first,
        query_weight_first,
        query_bias_first,
        kv_weight_first,
        kv_bias_first,
        out_weight_first,
        gate_up_weight_first,
        down_weight_first,
    )
    seconds = (
        norm_gains_second,
        query_weight_second,
        query_bias_second,
        kv_weight_second,
        kv_bias_second,
        out_weight_second,
        gate_up_weight_second,
        down_weight_second,
    )
    decays = (0.0, 1.0, 0.0, 1.0, 0.0, 1.0, 1.0, 1.0)
    rates = (0.5, 0.02, 0.5, 0.02, 0.5, 0.1, 0.02, 0.02)
    moved = [
        adam_update(
            params[param_index].astype(jnp.float32),
            stacked[param_index],
            firsts[param_index],
            seconds[param_index],
            decays[param_index],
            rates[param_index],
        )
        for param_index in range(8)
    ]
    input_grad = grad_hidden.reshape(seq_count, local_len, model_width)
    return (
        block_out,
        input_grad,
        stacked[0],
        stacked[1],
        stacked[2],
        stacked[3],
        stacked[4],
        stacked[5],
        stacked[6],
        stacked[7],
        moved[0][0],
        moved[1][0],
        moved[2][0],
        moved[3][0],
        moved[4][0],
        moved[5][0],
        moved[6][0],
        moved[7][0],
        moved[0][1],
        moved[1][1],
        moved[2][1],
        moved[3][1],
        moved[4][1],
        moved[5][1],
        moved[6][1],
        moved[7][1],
        moved[0][2],
        moved[1][2],
        moved[2][2],
        moved[3][2],
        moved[4][2],
        moved[5][2],
        moved[6][2],
        moved[7][2],
    )


def solution(mesh):
    in_specs = (
        P("dp", "ctx", None),
        P("dp", None),
        P("dp", "ctx", None),
        P(None, None, ("dp", "ctx")),
        P(None, ("dp", "ctx"), "tensor"),
        P(None, "tensor", ("dp", "ctx")),
        P(None, ("dp", "ctx"), None),
        P(None, ("dp", "ctx")),
        P(None, "tensor", ("dp", "ctx")),
        P(None, ("dp", "ctx"), None, "tensor"),
        P(None, "tensor", ("dp", "ctx")),
        P(None, None, ("dp", "ctx")),
        P(None, ("dp", "ctx"), "tensor"),
        P(None, "tensor", ("dp", "ctx")),
        P(None, ("dp", "ctx"), None),
        P(None, ("dp", "ctx")),
        P(None, "tensor", ("dp", "ctx")),
        P(None, ("dp", "ctx"), None, "tensor"),
        P(None, "tensor", ("dp", "ctx")),
        P(None, None, ("dp", "ctx")),
        P(None, ("dp", "ctx"), "tensor"),
        P(None, "tensor", ("dp", "ctx")),
        P(None, ("dp", "ctx"), None),
        P(None, ("dp", "ctx")),
        P(None, "tensor", ("dp", "ctx")),
        P(None, ("dp", "ctx"), None, "tensor"),
        P(None, "tensor", ("dp", "ctx")),
    )
    out_specs = (
        P("dp", "ctx", None),
        P("dp", "ctx", None),
        P(None, None, ("dp", "ctx")),
        P(None, ("dp", "ctx"), "tensor"),
        P(None, "tensor", ("dp", "ctx")),
        P(None, ("dp", "ctx"), None),
        P(None, ("dp", "ctx")),
        P(None, "tensor", ("dp", "ctx")),
        P(None, ("dp", "ctx"), None, "tensor"),
        P(None, "tensor", ("dp", "ctx")),
        P(None, None, ("dp", "ctx")),
        P(None, ("dp", "ctx"), "tensor"),
        P(None, "tensor", ("dp", "ctx")),
        P(None, ("dp", "ctx"), None),
        P(None, ("dp", "ctx")),
        P(None, "tensor", ("dp", "ctx")),
        P(None, ("dp", "ctx"), None, "tensor"),
        P(None, "tensor", ("dp", "ctx")),
        P(None, None, ("dp", "ctx")),
        P(None, ("dp", "ctx"), "tensor"),
        P(None, "tensor", ("dp", "ctx")),
        P(None, ("dp", "ctx"), None),
        P(None, ("dp", "ctx")),
        P(None, "tensor", ("dp", "ctx")),
        P(None, ("dp", "ctx"), None, "tensor"),
        P(None, "tensor", ("dp", "ctx")),
        P(None, None, ("dp", "ctx")),
        P(None, ("dp", "ctx"), "tensor"),
        P(None, "tensor", ("dp", "ctx")),
        P(None, ("dp", "ctx"), None),
        P(None, ("dp", "ctx")),
        P(None, "tensor", ("dp", "ctx")),
        P(None, ("dp", "ctx"), None, "tensor"),
        P(None, "tensor", ("dp", "ctx")),
    )
    return jax.shard_map(local, mesh=mesh, in_specs=in_specs, out_specs=out_specs, check_vma=False)
```

profile of v0, /device:TPU:0, one launch (start us, length us, event | category | flops | bytes accessed | tf_op | source)
XLA Modules:
  0.0 1993.0 jit_solution(1517739611447411412)
XLA Ops:
  17.6 18.1 all-gather.5
  36.5 20.0 %all-gather = bf16[1,2,1536]{1,0,2:T(2,128)(2,1)S(1)} all-gather(bf16[1,2,192]{1,0,2:T(2,128)(2,1)S(1)} %copy.379), channel_id=2, replica_groups=mesh['dp'=4,'ctx'=2,'tensor'=4] {'dp','ctx'}, dimensions={2}, use_global_device_ids=true | all-gather | bytes 6912 | tf_op jit(solution)/shard_map/all_gather | solution.py:64
  57.3 25.1 %slice_reduce_fusion.2 = (f32[1536]{0:T(1024)S(1)}, f32[1536]{0:T(1024)S(1)}) fusion(f32[1,2,1536]{1,0,2:T(1,128)S(1)} %convert_element_type.473), kind=kLoop, calls=%fused_computation.232 | loop fusion | bytes 24576 | tf_op jit(solution)/shard_map/slice | solution.py:234
  84.2 14.3 all-reduce.5
  141.9 58.9 %all-reduce.16.cloned.1.call-done = bf16[512,1536]{1,0:T(8,128)(2,1)} async-done(((bf16[512,1536]{1,0:T(8,128)(2,1)}), bf16[512,1536]{1,0:T(8,128)(2,1)}) %all-reduce.16.cloned.1.call-update) | async-done | bytes 1572880 | tf_op jit(solution)/shard_map/psum | solution.py:105
  203.4 77.6 %all-gather.35.cloned.1.call-done = bf16[1,1536,2,2240]{3,2,0,1:T(2,128)(2,1)} async-done(((bf16[1,192,2,2240]{3,2,0,1:T(2,128)(2,1)}), bf16[1,1536,2,2240]{3,2,0,1:T(2,128)(2,1)}) %all-gather.35.cloned.1.call-update) | async-done | bytes 13762576 | tf_op jit(solution)/shard_map/all_gather | solution.py:70
  281.0 35.1 %copy.309 = bf16[1,1536,2,2240]{1,3,2,0:T(8,128)(2,1)} copy(bf16[1,1536,2,2240]{3,2,0,1:T(2,128)(2,1)} %all-gather.35.cloned.1.call-done) | data formatting | bytes 27525120 | tf_op jit(solution)/shard_map/all_gather | solution.py:70
  344.1 16.0 all-gather.14
  360.4 18.3 all-gather.9
  380.1 25.4 %slice_reduce_fusion = (f32[1536]{0:T(1024)S(1)}, f32[1536]{0:T(1024)S(1)}) fusion(f32[1,2,1536]{1,0,2:T(1,128)S(1)} %convert_element_type.474), kind=kLoop, calls=%fused_computation.230 | loop fusion | bytes 24576 | tf_op jit(solution)/shard_map/slice | solution.py:234
  407.6 25.2 %all-reduce.18.cloned.1.call-done = bf16[512,1536]{1,0:T(8,128)(2,1)} async-done(((bf16[512,1536]{1,0:T(8,128)(2,1)}), bf16[512,1536]{1,0:T(8,128)(2,1)}) %all-reduce.18.cloned.1.call-update) | async-done | bytes 1572880 | tf_op jit(solution)/shard_map/psum | solution.py:105
  437.4 21.0 %all-gather.41.cloned.1.call-done = bf16[1,1536,384]{2,1,0:T(8,128)(2,1)} async-done(((bf16[1,192,384]{2,1,0:T(8,128)(2,1)}), bf16[1,1536,384]{2,1,0:T(8,128)(2,1)}) %all-gather.41.cloned.1.call-update) | async-done | bytes 1179664 | tf_op jit(solution)/shard_map/all_gather | solution.py:65
  489.7 77.0 %all-gather.45.cloned.1.call-done = bf16[1,1536,2,2240]{3,2,0,1:T(2,128)(2,1)} async-done(((bf16[1,192,2,2240]{3,2,0,1:T(2,128)(2,1)}), bf16[1,1536,2,2240]{3,2,0,1:T(2,128)(2,1)}) %all-gather.45.cloned.1.call-update) | async-done | bytes 13762576 | tf_op jit(solution)/shard_map/all_gather | solution.py:70
  566.7 35.3 %copy.318 = bf16[1,1536,2,2240]{1,3,2,0:T(8,128)(2,1)} copy(bf16[1,1536,2,2240]{3,2,0,1:T(2,128)(2,1)} %all-gather.45.cloned.1.call-done) | data formatting | bytes 27525120 | tf_op jit(solution)/shard_map/all_gather | solution.py:70
  601.9 36.7 %all-reduce.20.cloned.1.call-done = bf16[512,1536]{1,0:T(8,128)(2,1)} async-done(((bf16[512,1536]{1,0:T(8,128)(2,1)}), bf16[512,1536]{1,0:T(8,128)(2,1)}) %all-reduce.20.cloned.1.call-update) | async-done | bytes 1572880 | tf_op jit(solution)/shard_map/psum | solution.py:105
  655.6 33.5 %all-gather.47.cloned.1.call-done = bf16[1,2240,1536]{1,2,0:T(8,128)(2,1)} async-done(((bf16[1,2240,192]{1,2,0:T(8,128)(2,1)}), bf16[1,2240,1536]{1,2,0:T(8,128)(2,1)}) %all-gather.47.cloned.1.call-update) | async-done | bytes 6881296 | tf_op jit(solution)/shard_map/all_gather | solution.py:71
  714.6 69.2 %all-reduce.22.cloned.1.call-done = bf16[512,1536]{1,0:T(8,128)(2,1)} async-done(((bf16[512,1536]{1,0:T(8,128)(2,1)}), bf16[512,1536]{1,0:T(8,128)(2,1)}) %all-reduce.22.cloned.1.call-update) | async-done | bytes 1572880 | tf_op jit(solution)/shard_map/psum | solution.py:302
  814.1 87.9 %all-reduce.28.cloned.1.call-done = (bf16[1,512,2,2,128]{4,3,1,2,0:T(2,128)(2,1)}, bf16[512,1536]{1,0:T(8,128)(2,1)}) async-done(((bf16[1,512,2,2,128]{4,3,1,2,0:T(2,128)(2,1)}, bf16[512,1536]{1,0:T(8,128)(2,1)}), (bf16[1,512,2,2,128]{4,3,1,2,0:T(2,128)(2,1)}, bf16[512,1536]{1,0:T(8,128)(2,1)})) %all-reduce.28.cloned.1.call-update) | async-done | bytes 2097168 | tf_op jit(solution)/shard_map/psum | solution.py:347
  937.9 68.1 %all-reduce.24.cloned.1.call-done = bf16[512,1536]{1,0:T(8,128)(2,1)} async-done(((bf16[512,1536]{1,0:T(8,128)(2,1)}), bf16[512,1536]{1,0:T(8,128)(2,1)}) %all-reduce.24.cloned.1.call-update) | async-done | bytes 1572880 | tf_op jit(solution)/shard_map/psum | solution.py:302
  1058.5 120.7 %all-reduce.26.cloned.1.call-done = (bf16[512,1536]{1,0:T(8,128)(2,1)}, bf16[1,512,2,2,128]{4,3,1,2,0:T(2,128)(2,1)}, bf16[512,1536]{1,0:T(8,128)(2,1)}) async-done(((bf16[512,1536]{1,0:T(8,128)(2,1)}, bf16[1,512,2,2,128]{4,3,1,2,0:T(2,128)(2,1)}, bf16[512,1536]{1,0:T(8,128)(2,1)}), (bf16[512,1536]{1,0:T(8,128)(2,1)}, bf16[1,512,2,2,128]{4,3,1,2,0:T(2,128)(2,1)}, ...) | async-done | bytes 3670032 | tf_op jit(solution)/shard_map/psum | solution.py:105
  1251.6 34.0 %reduce-scatter.53.cloned.1.call-done = bf16[16,3]{1,0:T(8,128)(2,1)} async-done(((bf16[128,3]{1,0:T(8,128)(2,1)}), bf16[16,3]{1,0:T(8,128)(2,1)}) %reduce-scatter.53.cloned.1.call-update) | async-done | bytes 112
  1288.7 37.3 %reduce-scatter.39.cloned.1.call-done = bf16[384,192]{0,1:T(8,128)(2,1)} async-done(((bf16[384,1536]{0,1:T(8,128)(2,1)}), bf16[384,192]{0,1:T(8,128)(2,1)}) %reduce-scatter.39.cloned.1.call-update) | async-done | bytes 147472 | tf_op jit(solution)/shard_map/reduce_scatter | solution.py:92
  1326.0 39.9 %reduce-scatter.37.cloned.1.call-done = bf16[384,192]{0,1:T(8,128)(2,1)} async-done(((bf16[384,1536]{0,1:T(8,128)(2,1)}), bf16[384,192]{0,1:T(8,128)(2,1)}) %reduce-scatter.37.cloned.1.call-update) | async-done | bytes 147472 | tf_op jit(solution)/shard_map/reduce_scatter | solution.py:92
  1368.7 37.5 %reduce-scatter.31.cloned.1.call-done = bf16[192,384]{1,0:T(8,128)(2,1)} async-done(((bf16[1536,384]{1,0:T(8,128)(2,1)}), bf16[192,384]{1,0:T(8,128)(2,1)}) %reduce-scatter.31.cloned.1.call-update) | async-done | bytes 147472 | tf_op jit(solution)/shard_map/reduce_scatter | solution.py:80
  1406.3 39.9 %reduce-scatter.29.cloned.1.call-done = bf16[192,384]{1,0:T(8,128)(2,1)} async-done(((bf16[1536,384]{1,0:T(8,128)(2,1)}), bf16[192,384]{1,0:T(8,128)(2,1)}) %reduce-scatter.29.cloned.1.call-update) | async-done | bytes 147472 | tf_op jit(solution)/shard_map/reduce_scatter | solution.py:80
  1485.3 41.2 %reduce-scatter.35.cloned.1.call-done = bf16[192,512]{1,0:T(8,128)(2,1)} async-done(((bf16[1536,512]{1,0:T(8,128)(2,1)}), bf16[192,512]{1,0:T(8,128)(2,1)}) %reduce-scatter.35.cloned.1.call-update) | async-done | bytes 196624 | tf_op jit(solution)/shard_map/reduce_scatter | solution.py:86
  1526.5 42.1 %reduce-scatter.33.cloned.1.call-done = bf16[192,512]{1,0:T(8,128)(2,1)} async-done(((bf16[1536,512]{1,0:T(8,128)(2,1)}), bf16[192,512]{1,0:T(8,128)(2,1)}) %reduce-scatter.33.cloned.1.call-update) | async-done | bytes 196624 | tf_op jit(solution)/shard_map/reduce_scatter | solution.py:86
  1571.9 66.6 %reduce-scatter.47.cloned.1.call-done = bf16[2240,192]{0,1:T(8,128)(2,1)} async-done(((bf16[2240,1536]{0,1:T(8,128)(2,1)}), bf16[2240,192]{0,1:T(8,128)(2,1)}) %reduce-scatter.47.cloned.1.call-update) | async-done | bytes 860176 | tf_op jit(solution)/shard_map/reduce_scatter | solution.py:98
  1638.5 69.6 %reduce-scatter.45.cloned.1.call-done = bf16[2240,192]{0,1:T(8,128)(2,1)} async-done(((bf16[2240,1536]{0,1:T(8,128)(2,1)}), bf16[2240,192]{0,1:T(8,128)(2,1)}) %reduce-scatter.45.cloned.1.call-update) | async-done | bytes 860176 | tf_op jit(solution)/shard_map/reduce_scatter | solution.py:98
  1716.9 96.0 %reduce-scatter.43.cloned.1.call-done = bf16[192,2,2240]{2,0,1:T(8,128)(2,1)} async-done(((bf16[1536,2,2240]{2,0,1:T(8,128)(2,1)}), bf16[192,2,2240]{2,0,1:T(8,128)(2,1)}) %reduce-scatter.43.cloned.1.call-update) | async-done | bytes 1720336 | tf_op jit(solution)/shard_map/reduce_scatter | solution.py:95
  1812.9 104.6 %reduce-scatter.41.cloned.1.call-done = bf16[192,2,2240]{2,0,1:T(8,128)(2,1)} async-done(((bf16[1536,2,2240]{2,0,1:T(8,128)(2,1)}), bf16[192,2,2240]{2,0,1:T(8,128)(2,1)}) %reduce-scatter.41.cloned.1.call-update) | async-done | bytes 1720336 | tf_op jit(solution)/shard_map/reduce_scatter | solution.py:95
  1934.6 16.9 convert_subtract_fusion
  (490 shorter events, 466.1 us)
Async XLA Ops:
  9.2 95.4 %all-gather.29.cloned.1.call-start = ((), (), s32[]{:S(2)}) async-start(), calls=%async_computation.33 | async-start | bytes 1769472 | tf_op jit(solution)/shard_map/all_gather | solution.py:67
  11.0 117.2 %all-gather.33.cloned.1.call-start = ((), (), s32[]{:S(2)}) async-start(), calls=%async_computation.35 | async-start | bytes 1327104 | tf_op jit(solution)/shard_map/all_gather | solution.py:69
  12.8 188.0 %all-reduce.16.cloned.1.call-start = ((), (), s32[]{:S(2)}) async-start(), calls=%async_computation.16 | async-start | bytes 3145728 | tf_op jit(solution)/shard_map/psum | solution.py:105
  131.8 149.2 %all-gather.35.cloned.1.call-start = ((), (), s32[]{:S(2)}) async-start(), calls=%async_computation.36 | async-start | bytes 15925248 | tf_op jit(solution)/shard_map/all_gather | solution.py:70
  138.1 195.1 %all-gather.37.cloned.1.call-start = ((), (), s32[]{:S(2)}) async-start(), calls=%async_computation.37 | async-start | bytes 7962624 | tf_op jit(solution)/shard_map/all_gather | solution.py:71
  140.9 264.6 %all-gather.39.cloned.1.call-start = ((), (), s32[]{:S(2)}) async-start(), calls=%async_computation.38 | async-start | bytes 1769472 | tf_op jit(solution)/shard_map/all_gather | solution.py:67
  141.7 291.2 %all-reduce.18.cloned.1.call-start = ((), (), s32[]{:S(2)}) async-start(), calls=%async_computation.17 | async-start | bytes 3145728 | tf_op jit(solution)/shard_map/psum | solution.py:105
  341.9 116.5 %all-gather.41.cloned.1.call-start = ((), (), s32[]{:S(2)}) async-start(), calls=%async_computation.39 | async-start | bytes 1327104 | tf_op jit(solution)/shard_map/all_gather | solution.py:65
  342.7 142.7 %all-gather.43.cloned.1.call-start = ((), (), s32[]{:S(2)}) async-start(), calls=%async_computation.40 | async-start | bytes 1327104 | tf_op jit(solution)/shard_map/all_gather | solution.py:69
  343.3 223.4 %all-gather.45.cloned.1.call-start = ((), (), s32[]{:S(2)}) async-start(), calls=%async_computation.41 | async-start | bytes 15925248 | tf_op jit(solution)/shard_map/all_gather | solution.py:70
  344.0 294.7 %all-reduce.20.cloned.1.call-start = ((), (), s32[]{:S(2)}) async-start(), calls=%async_computation.18 | async-start | bytes 3145728 | tf_op jit(solution)/shard_map/psum | solution.py:105
  488.9 200.2 %all-gather.47.cloned.1.call-start = ((), (), s32[]{:S(2)}) async-start(), calls=%async_computation.42 | async-start | bytes 7962624 | tf_op jit(solution)/shard_map/all_gather | solution.py:71
  489.6 294.1 %all-reduce.22.cloned.1.call-start = ((), (), s32[]{:S(2)}) async-start(), calls=%async_computation.19 | async-start | bytes 3145728 | tf_op jit(solution)/shard_map/psum | solution.py:302
  714.5 97.3 %reduce-scatter.25.cloned.1.call-start = ((), (), s32[]{:S(2)}) async-start(), calls=%async_computation.20 | async-start | bytes 786432 | tf_op jit(solution)/shard_map/reduce_scatter | solution.py:340
  798.0 103.9 %all-reduce.28.cloned.1.call-start = ((), (), s32[]{:S(2)}) async-start(), calls=%async_computation.48 | async-start | bytes 4194304 | tf_op jit(solution)/shard_map/psum | solution.py:347
  814.1 192.0 %all-reduce.24.cloned.1.call-start = ((), (), s32[]{:S(2)}) async-start(), calls=%async_computation.21 | async-start | bytes 3145728 | tf_op jit(solution)/shard_map/psum | solution.py:302
  937.8 101.4 %reduce-scatter.27.cloned.1.call-start = ((), (), s32[]{:S(2)}) async-start(), calls=%async_computation.22 | async-start | bytes 786432 | tf_op jit(solution)/shard_map/reduce_scatter | solution.py:340
  1022.1 157.1 %all-reduce.26.cloned.1.call-start = ((), (), s32[]{:S(2)}) async-start(), calls=%async_computation.47 | async-start | bytes 7340032 | tf_op jit(solution)/shard_map/psum | solution.py:105
  1041.5 201.8 %reduce-scatter.55.cloned.1.call-start = ((), (), s32[]{:S(2)}) async-start(), calls=%async_computation.46 | async-start | bytes 36864
  1042.3 208.5 %reduce-scatter.51.cloned.1.call-start = ((), (), s32[]{:S(2)}) async-start(), calls=%async_computation.44 | async-start | bytes 442368
  1043.4 242.2 %reduce-scatter.53.cloned.1.call-start = ((), (), s32[]{:S(2)}) async-start(), calls=%async_computation.45 | async-start | bytes 36864
  1044.2 281.9 %reduce-scatter.39.cloned.1.call-start = ((), (), s32[]{:S(2)}) async-start(), calls=%async_computation.28 | async-start | bytes 1327104 | tf_op jit(solution)/shard_map/reduce_scatter | solution.py:92
  1048.8 317.1 %reduce-scatter.37.cloned.1.call-start = ((), (), s32[]{:S(2)}) async-start(), calls=%async_computation.27 | async-start | bytes 1327104 | tf_op jit(solution)/shard_map/reduce_scatter | solution.py:92
  1051.9 354.3 %reduce-scatter.31.cloned.1.call-start = ((), (), s32[]{:S(2)}) async-start(), calls=%async_computation.24 | async-start | bytes 1327104 | tf_op jit(solution)/shard_map/reduce_scatter | solution.py:80
  1055.7 390.5 %reduce-scatter.29.cloned.1.call-start = ((), (), s32[]{:S(2)}) async-start(), calls=%async_computation.23 | async-start | bytes 1327104 | tf_op jit(solution)/shard_map/reduce_scatter | solution.py:80
  1058.0 425.8 %reduce-scatter.49.cloned.1.call-start = ((), (), s32[]{:S(2)}) async-start(), calls=%async_computation.43 | async-start | bytes 442368
  1186.6 340.0 %reduce-scatter.35.cloned.1.call-start = ((), (), s32[]{:S(2)}) async-start(), calls=%async_computation.26 | async-start | bytes 1769472 | tf_op jit(solution)/shard_map/reduce_scatter | solution.py:86
  1190.2 378.4 %reduce-scatter.33.cloned.1.call-start = ((), (), s32[]{:S(2)}) async-start(), calls=%async_computation.25 | async-start | bytes 1769472 | tf_op jit(solution)/shard_map/reduce_scatter | solution.py:86
  1193.8 444.7 %reduce-scatter.47.cloned.1.call-start = ((), (), s32[]{:S(2)}) async-start(), calls=%async_computation.32 | async-start | bytes 7962624 | tf_op jit(solution)/shard_map/reduce_scatter | solution.py:98
  1203.7 504.4 %reduce-scatter.45.cloned.1.call-start = ((), (), s32[]{:S(2)}) async-start(), calls=%async_computation.31 | async-start | bytes 7962624 | tf_op jit(solution)/shard_map/reduce_scatter | solution.py:98
  1213.2 599.8 %reduce-scatter.43.cloned.1.call-start = ((), (), s32[]{:S(2)}) async-start(), calls=%async_computation.30 | async-start | bytes 15925248 | tf_op jit(solution)/shard_map/reduce_scatter | solution.py:95
  1228.4 689.1 %reduce-scatter.41.cloned.1.call-start = ((), (), s32[]{:S(2)}) async-start(), calls=%async_computation.29 | async-start | bytes 15925248 | tf_op jit(solution)/shard_map/reduce_scatter | solution.py:95
  (115 other events, 3163.2 us)
Sparse Core Ops, SparseCore 0:
  10.6 26.9 all-gather.30
  40.0 27.6 all-gather.28
  70.2 24.2 all-gather.32
  131.9 68.8 all-reduce.15
  203.2 77.8 all-gather.34
  283.3 48.8 all-gather.36
  334.7 26.0 all-gather.38
  363.7 69.1 all-reduce.17
  435.3 23.1 all-gather.40
  460.8 24.5 all-gather.42
  487.9 78.7 all-gather.44
  569.5 69.1 all-reduce.19
  641.1 47.8 all-gather.46
  714.6 69.1 all-reduce.21
  798.2 13.5 reduce-scatter.24
  814.8 87.1 all-reduce.27
  938.0 68.0 all-reduce.23
  1041.6 137.5 all-reduce.25
  1182.9 30.2 reduce-scatter.54
  1216.9 33.8 reduce-scatter.50
  1254.3 31.2 reduce-scatter.52
  1289.2 36.8 reduce-scatter.38
  1329.1 36.7 reduce-scatter.36
  1369.5 36.7 reduce-scatter.30
  1409.4 36.7 reduce-scatter.28
  1449.9 33.8 reduce-scatter.48
  1488.0 38.4 reduce-scatter.34
  1530.2 38.4 reduce-scatter.32
  1573.0 65.4 reduce-scatter.46
  1642.6 65.4 reduce-scatter.44
  1712.2 100.7 reduce-scatter.42
  1816.8 100.7 reduce-scatter.40
  (1 shorter events, 13.5 us)
where the time goes:
time: 2000 us; the launch traced here: 1990 us
  waiting for transfers between devices  1320 us (66%)
  local copies, waits for them, and re-layouts  222 us (11%)
  matrix products  202 us (10%)
  blocking collectives  125 us (6%)
  other arithmetic  107 us (5%)
    psum x4, waiting for transfers between devices, tensor_sum(): return lax.psum(values.astype(jnp.bfloat16), 'tensor').astype(jnp.float32)  242 us
    reduce_scatter x2, waiting for transfers between devices, scatter_layer(): lax.psum_scatter(w_gate_up.astype(jnp.bfloat16), ('dp', 'ctx'), scatter_d...  201 us
    all_gather x2, waiting for transfers between devices, gather_layer(): lax.all_gather(w_gate_up, ('dp', 'ctx'), axis=0, tiled=True)  155 us
    psum x2, waiting for transfers between devices, local(): lax.psum(jnp.einsum('rgf,dgf->rd', grad_pair, w_gate_up, preferred_elemen...  137 us
    reduce_scatter x2, waiting for transfers between devices, scatter_layer(): lax.psum_scatter(w_down.astype(jnp.bfloat16), ('dp', 'ctx'), scatter_dime...  136 us
    psum x1, waiting for transfers between devices, local(): lax.psum((own_grads[:, :, :, None, :] * head_mask[:, None]).astype(jnp.bf...  87.9 us
    unnamed x261, local copies, waits for them, and re-layouts  86.2 us
    reduce_scatter x2, waiting for transfers between devices, scatter_layer(): lax.psum_scatter(w_kv.astype(jnp.bfloat16), ('dp', 'ctx'), scatter_dimens...  83.3 us
  transfers between devices with their start and end apart: 33, of which 26 were waited for; matrix products, arithmetic and copies ran while one was open for 18% of the time, Pallas kernels for 0%

commit v1 on v0

v1 whole, which is shorter than its diff:
```python
import functools

import jax
import jax.numpy as jnp
from jax import lax
from jax.experimental import pallas as pl
from jax.experimental.pallas import tpu as pltpu
from jax.sharding import PartitionSpec as P

H = 12
KV = 2
HD = 128
LAYERS = 2

NORM_EPS = 1e-06
ROPE_BASE = 1000000.0
MASK_FILL = -1e30
beta_first = 0.9
beta_second = 0.95
adam_eps = 1e-08
decay_rate = 0.1
adam_step = 3.0

MESH = pl.DeviceIdType.MESH
ROW_TILE = 16
Z_CHUNKS = 8


class Place:
    def __init__(self, sizes):
        self.dps, self.ctxs, self.tensors = sizes
        self.xs = self.dps // 2
        self.dp = lax.axis_index("dp")
        self.ctx = lax.axis_index("ctx")
        self.tensor = lax.axis_index("tensor")
        self.x = self.dp // 2
        self.core = self.dp % 2

    def x_at(self, step):
        return lax.rem(self.x + step, self.xs)

    def ctx_at(self, step):
        return lax.rem(self.ctx + step, self.ctxs)

    def shard(self, x, core, ctx):
        return (x * 2 + core) * self.ctxs + ctx

    def to_x(self, x):
        return {"dp": x * 2 + self.core}

    def to_ctx(self, ctx):
        return {"ctx": ctx}

    def to_core(self):
        return {"dp": self.x * 2 + 1 - self.core}

    def to_tensor(self, tensor):
        return {"tensor": tensor}


class Sems:
    def __init__(self, send, recv):
        self.send, self.recv, self.used = send, recv, 0

    def take(self, count=1):
        first = self.used
        self.used += count
        return first

    def remote(self, src, dst, device, slot=None):
        slot = self.take() if slot is None else slot
        return pltpu.make_async_remote_copy(
            src_ref=src,
            dst_ref=dst,
            send_sem=self.send.at[slot],
            recv_sem=self.recv.at[slot],
            device_id=device,
            device_id_type=MESH,
        )

    def local(self, src, dst):
        return pltpu.make_async_copy(src, dst, self.send.at[self.take()])


def half_rows(rows):
    return min(rows, (rows // 2 + ROW_TILE - 1) // ROW_TILE * ROW_TILE)


def gather_steps(place, sems, shard, whole):
    rows = shard.shape[0]
    cut = half_rows(rows)
    spans = [(0, cut), (cut, rows - cut)]
    xs, ctxs = range(1, place.xs), range(1, place.ctxs)
    me = place.shard(place.x, place.core, place.ctx)
    sent, kept = [], {}

    def part(index, span):
        return whole.at[index, pl.ds(span[0], span[1])]

    def first():
        for step in xs:
            kept["x", step] = sems.remote(shard, whole.at[me], place.to_x(place.x_at(step)))
        for step in ctxs:
            kept["ctx", step] = sems.remote(shard, whole.at[me], place.to_ctx(place.ctx_at(step)))
        kept["core"] = sems.remote(shard, whole.at[me], place.to_core())
        kept["own"] = sems.local(shard, whole.at[me])
        for copy in kept.values():
            copy.start()

    def forward(index, span, device):
        copy = sems.remote(part(index, span), part(index, span), device)
        copy.start()
        sent.append(copy)
        return copy

    def second():
        for step in xs:
            kept["x", step].wait_recv()
            index = place.shard(place.x_at(place.xs - step), place.core, place.ctx)
            for other in ctxs:
                kept["far", step, other, 0] = forward(index, spans[0], place.to_ctx(place.ctx_at(other)))
            forward(index, (0, rows), place.to_core())
        for step in ctxs:
            kept["ctx", step].wait_recv()
            index = place.shard(place.x, place.core, place.ctx_at(place.ctxs - step))
            if spans[1][1] > 0:
                for other in xs:
                    kept["far", other, step, 1] = forward(
                        index, spans[1], place.to_x(place.x_at(other))
                    )
            forward(index, (0, rows), place.to_core())

    def third():
        for step in xs:
            for other in ctxs:
                index = place.shard(
                    place.x_at(place.xs - step), place.core, place.ctx_at(place.ctxs - other)
                )
                kept["far", step, other, 0].wait_recv()
                if spans[1][1] > 0:
                    kept["far", step, other, 1].wait_recv()
                forward(index, (0, rows), place.to_core())

    def last():
        for name, copy in kept.items():
            if name == "own":
                copy.wait()
            elif name[0] in ("x", "ctx"):
                copy.wait_send()
        kept["core"].wait()
        far = [copy for name, copy in kept.items() if name[0] == "far"]
        for copy in sent:
            if any(copy is other for other in far):
                copy.wait_send()
            else:
                copy.wait()

    return [first, second, third, last]


def gather_sems(sizes):
    xs, ctxs = sizes[0] // 2 - 1, sizes[1] - 1
    return 2 + 2 * (xs + ctxs) + 3 * xs * ctxs


def add_rows(rows, body):
    @pl.loop(0, rows // ROW_TILE)
    def _(block):
        body(pl.ds(pl.multiple_of(block * ROW_TILE, ROW_TILE), ROW_TILE))


def scatter_buffers(sizes, shape, dtype):
    n, rows, cols = shape
    xs, ctxs = sizes[0] // 2, sizes[1]
    cut = half_rows(rows)
    far = max(1, (xs - 1) * (ctxs - 1))
    return [
        pltpu.VMEM((xs, ctxs, rows, cols), dtype),
        pltpu.VMEM((xs, ctxs, rows, cols), dtype),
        pltpu.VMEM((far, cut, cols), dtype),
        pltpu.VMEM((far, max(ROW_TILE, rows - cut), cols), dtype),
        pltpu.VMEM((max(1, xs - 1 + ctxs - 1), rows, cols), dtype),
    ]


def scatter_sems(sizes):
    xs, ctxs = sizes[0] // 2 - 1, sizes[1] - 1
    return 2 * (xs + 1) + (xs + ctxs) + 2 * xs * ctxs


def scatter_steps(place, sems, whole, out, mine, other, far_x, far_ctx, near):
    rows = out.shape[0]
    cut = half_rows(rows)
    xs, ctxs = range(1, place.xs), range(1, place.ctxs)
    ahead = lambda step, turn: (step - 1) * len(ctxs) + turn - 1
    loads, swaps, sent = {}, {}, []
    far, close = {}, {}
    wide = lambda ref, *at: ref[at].astype(jnp.float32)

    def first():
        for step in list(xs) + [0]:
            to = place.x_at(step)
            at = place.shard(to, 1 - place.core, 0)
            swaps[step] = sems.remote(
                whole.at[pl.ds(at, place.ctxs)], other.at[step], place.to_core()
            )
            swaps[step].start()
            at = place.shard(to, place.core, 0)
            loads[step] = sems.local(whole.at[pl.ds(at, place.ctxs)], mine.at[step])
            loads[step].start()

    def second():
        for step in xs:
            loads[step].wait()
            swaps[step].wait_recv()
            for turn in ctxs:
                ctx = place.ctx_at(turn)

                def add(span):
                    total = wide(mine, step, ctx, span) + wide(other, step, ctx, span)
                    mine[step, ctx, span] = total.astype(mine.dtype)

                add_rows(rows, add)
                slot = ahead(step, turn)
                far[step, turn, 0] = sems.remote(
                    mine.at[step, ctx, pl.ds(0, cut)], far_x.at[slot], place.to_ctx(ctx)
                )
                far[step, turn, 0].start()
                if rows > cut:
                    far[step, turn, 1] = sems.remote(
                        mine.at[step, ctx, pl.ds(cut, rows - cut)],
                        far_ctx.at[slot],
                        place.to_x(place.x_at(step)),
                    )
                    far[step, turn, 1].start()
        loads[0].wait()
        swaps[0].wait_recv()

    def third():
        for turn in ctxs:
            ctx = place.ctx_at(turn)
            if rows > cut:
                for step in xs:
                    far[step, turn, 1].wait_recv()

            def add_near(span):
                total = wide(mine, 0, ctx, span) + wide(other, 0, ctx, span)
                mine[0, ctx, span] = total.astype(mine.dtype)

            def add_far(block):
                span = pl.ds(pl.multiple_of(cut + block * ROW_TILE, ROW_TILE), ROW_TILE)
                here = pl.ds(pl.multiple_of(block * ROW_TILE, ROW_TILE), ROW_TILE)
                total = wide(mine, 0, ctx, span) + wide(other, 0, ctx, span)
                for step in xs:
                    total = total + wide(far_ctx, ahead(step, turn), here)
                mine[0, ctx, span] = total.astype(mine.dtype)

            add_rows(cut, add_near)
            if rows > cut:
                pl.loop(0, (rows - cut) // ROW_TILE)(add_far)
            slot = len(xs) + turn - 1
            close["ctx", turn] = sems.remote(mine.at[0, ctx], near.at[slot], place.to_ctx(ctx))
            close["ctx", turn].start()
        for step in xs:
            for turn in ctxs:
                far[step, turn, 0].wait_recv()

            def add_cut(span):
                total = wide(mine, step, place.ctx, span) + wide(other, step, place.ctx, span)
                for turn in ctxs:
                    total = total + wide(far_x, ahead(step, turn), span)
                mine[step, place.ctx, span] = total.astype(mine.dtype)

            def add_rest(block):
                span = pl.ds(pl.multiple_of(cut + block * ROW_TILE, ROW_TILE), ROW_TILE)
                total = wide(mine, step, place.ctx, span) + wide(other, step, place.ctx, span)
                mine[step, place.ctx, span] = total.astype(mine.dtype)

            add_rows(cut, add_cut)
            if rows > cut:
                pl.loop(0, (rows - cut) // ROW_TILE)(add_rest)
            close["x", step] = sems.remote(
                mine.at[step, place.ctx], near.at[step - 1], place.to_x(place.x_at(step))
            )
            close["x", step].start()

    def last():
        for copy in close.values():
            copy.wait_recv()

        def add_own(span):
            total = wide(mine, 0, place.ctx, span) + wide(other, 0, place.ctx, span)
            for slot in range(len(xs) + len(ctxs)):
                total = total + wide(near, slot, span)
            out[span] = total.astype(out.dtype)

        add_rows(rows, add_own)
        for copy in (*far.values(), *close.values(), *swaps.values()):
            copy.wait_send()

    return [first, second, third, last]


def line_steps(place, sems, part, out, recv, acc):
    rows = part.shape[0]
    size = rows // (2 * Z_CHUNKS)
    line = place.tensors
    me = place.tensor
    left = me < (line + 1) // 2
    hops = jnp.where(left, me, line - 1 - me)
    ahead = jnp.where(left, 1, -1)
    near = jnp.where(left, 0, 1)
    far = 1 - near
    onward = place.to_tensor(lax.clamp(0, me + ahead, line - 1))
    back = place.to_tensor(lax.clamp(0, me - ahead, line - 1))
    base = sems.take(4 * Z_CHUNKS)
    inner = hops > 0

    def span(flow, chunk):
        return pl.ds(pl.multiple_of((flow * Z_CHUNKS + chunk) * size, size), size)

    def summing(flow, chunk, src, device):
        return sems.remote(
            src.at[span(flow, chunk)],
            recv.at[span(flow, chunk)],
            device,
            base + flow * Z_CHUNKS + chunk,
        )

    def sharing(flow, chunk, device):
        return sems.remote(
            out.at[span(flow, chunk)],
            out.at[span(flow, chunk)],
            device,
            base + (2 + flow) * Z_CHUNKS + chunk,
        )

    def add(flow, chunk, into):
        at = span(flow, chunk)
        total = part[at].astype(jnp.float32) + recv[at].astype(jnp.float32)
        into[at] = total.astype(into.dtype)

    def begin():
        @pl.when(hops == 0)
        def _():
            for chunk in range(Z_CHUNKS):
                summing(near, chunk, part, onward).start()

    def step(turn):
        def run():
            chunk = turn
            if chunk < Z_CHUNKS:

                @pl.when(inner)
                def _():
                    summing(near, chunk, part, onward).wait_recv()
                    add(near, chunk, acc)
                    summing(near, chunk, acc, onward).start()

                summing(far, chunk, acc, back).wait_recv()

                @pl.when(inner)
                def _():
                    add(far, chunk, acc)
                    summing(far, chunk, acc, back).start()

                @pl.when(hops == 0)
                def _():
                    add(far, chunk, out)
                    sharing(far, chunk, onward).start()

            chunk = turn - 2
            if 0 <= chunk < Z_CHUNKS:

                @pl.when(inner)
                def _():
                    sharing(far, chunk, onward).wait_recv()
                    sharing(far, chunk, onward).start()

            chunk = turn - 3
            if 0 <= chunk < Z_CHUNKS:
                sharing(near, chunk, back).wait_recv()

                @pl.when(inner)
                def _():
                    sharing(near, chunk, back).start()

        return run

    def end():
        for chunk in range(Z_CHUNKS):
            summing(near, chunk, acc, onward).wait_send()
            sharing(far, chunk, onward).wait_send()

            @pl.when(inner)
            def _():
                summing(far, chunk, acc, back).wait_send()
                sharing(near, chunk, back).wait_send()

    return [begin] + [step(turn) for turn in range(Z_CHUNKS + 3)] + [end]


def transfer_kernel(sizes, counts, plan, *refs):
    z_count, g_count, s_count, p_count, w_count = counts
    inputs = sum(counts)
    ins, outs, rest = refs[:inputs], refs[inputs : 2 * inputs], list(refs[2 * inputs :])
    place = Place(sizes)
    sems = Sems(rest.pop(), rest.pop())

    barrier = pltpu.get_barrier_semaphore()
    partners = []
    arrived = 0
    if g_count or s_count:
        partners.append(place.to_core())
        partners += [place.to_x(place.x_at(step)) for step in range(1, place.xs)]
    if g_count or s_count or p_count or w_count:
        partners += [place.to_ctx(place.ctx_at(step)) for step in range(1, place.ctxs)]
    for partner in partners:
        pl.semaphore_signal(barrier, inc=1, device_id=partner, device_id_type=MESH)
    arrived = len(partners)
    if z_count:
        above = place.tensor < place.tensors - 1
        below = place.tensor > 0

        @pl.when(above)
        def _():
            pl.semaphore_signal(
                barrier, inc=1, device_id=place.to_tensor(place.tensor + 1), device_id_type=MESH
            )

        @pl.when(below)
        def _():
            pl.semaphore_signal(
                barrier, inc=1, device_id=place.to_tensor(place.tensor - 1), device_id_type=MESH
            )

        arrived = arrived + above.astype(jnp.int32) + below.astype(jnp.int32)
    pl.semaphore_wait(barrier, arrived)

    ins, outs = list(ins), list(outs)
    lines, planes, ends = [], [], []
    for _ in range(z_count):
        lines.append(line_steps(place, sems, ins.pop(0), outs.pop(0), rest.pop(0), rest.pop(0)))
    for _ in range(g_count):
        planes.append(gather_steps(place, sems, ins.pop(0), outs.pop(0)))
    for _ in range(s_count):
        buffers = [rest.pop(0) for _ in range(5)]
        planes.append(scatter_steps(place, sems, ins.pop(0), outs.pop(0), *buffers))
    small = []
    for index in range(p_count + w_count):
        src, dst = ins.pop(0), outs.pop(0)
        mine = place.ctx
        for step in range(1, place.ctxs):
            to = place.ctx_at(step)
            block = src if index < p_count else src.at[to]
            small.append(sems.remote(block, dst.at[mine], place.to_ctx(to)))
        block = src if index < p_count else src.at[mine]
        small.append(sems.local(block, dst.at[mine]))
    for copy in small:
        copy.start()
    stages = [[plane[stage] for plane in planes] for stage in range(4)]
    for run in stages[0]:
        run()
    turns = max([len(line) for line in lines], default=0)
    for turn in range(turns + 1):
        for stage in (1, 2):
            if (plan[stage - 1] == turn) or (turn == turns and plan[stage - 1] > turns):
                for run in stages[stage]:
                    run()
        for line in lines:
            if turn < len(line):
                line[turn]()
    for run in stages[3]:
        run()
    for copy in small:
        copy.wait()


def transfer(sizes, number, z_sums=(), gathers=(), scatters=(), pieces=(), swaps=(), plan=(99, 99)):
    n = sizes[0] * sizes[1]
    any_space = pl.BlockSpec(memory_space=pl.ANY)
    in_vmem = pl.BlockSpec(memory_space=pltpu.VMEM)
    args = (*z_sums, *gathers, *scatters, *pieces, *swaps)
    in_specs = [in_vmem] * len(z_sums) + [any_space] * (len(args) - len(z_sums))
    out_specs = (
        [in_vmem] * len(z_sums)
        + [any_space] * len(gathers)
        + [in_vmem] * len(scatters)
        + [any_space] * (len(pieces) + len(swaps))
    )
    out_shape = (
        [jax.ShapeDtypeStruct(a.shape, a.dtype) for a in z_sums]
        + [jax.ShapeDtypeStruct((n, *a.shape), a.dtype) for a in gathers]
        + [jax.ShapeDtypeStruct(a.shape[1:], jnp.float32) for a in scatters]
        + [jax.ShapeDtypeStruct((sizes[1], *a.shape), a.dtype) for a in pieces]
        + [jax.ShapeDtypeStruct(a.shape, a.dtype) for a in swaps]
    )
    scratch = []
    for a in z_sums:
        scratch += [pltpu.VMEM(a.shape, a.dtype)] * 2
    for a in scatters:
        scratch += scatter_buffers(sizes, a.shape, a.dtype)
    count = (
        4 * Z_CHUNKS * len(z_sums)
        + gather_sems(sizes) * len(gathers)
        + scatter_sems(sizes) * len(scatters)
        + sizes[1] * (len(pieces) + len(swaps))
    )
    scratch += [pltpu.SemaphoreType.DMA((count,)), pltpu.SemaphoreType.DMA((count,))]
    counts = (len(z_sums), len(gathers), len(scatters), len(pieces), len(swaps))
    return pl.pallas_call(
        functools.partial(transfer_kernel, sizes, counts, plan),
        out_shape=out_shape,
        in_specs=in_specs,
        out_specs=out_specs,
        scratch_shapes=scratch,
        compiler_params=pltpu.CompilerParams(
            collective_id=number, has_side_effects=True, vmem_limit_bytes=56 << 20
        ),
        name="transfer%d" % number,
    )(*args)


def rotate(values, cosine, sine):
    half_width = values.shape[-1] // 2
    first_half = values[..., :half_width]
    second_half = values[..., half_width:]
    return jnp.concatenate(
        [first_half * cosine - second_half * sine, second_half * cosine + first_half * sine],
        axis=-1,
    )


def rotate_back(grad_rows, cosine, sine):
    return rotate(grad_rows, cosine, -sine)


def norm_back(values, norm_scale, gain, grad_rows):
    weighted = grad_rows * gain
    inner_mean = jnp.mean(weighted * values, axis=-1, keepdims=True)
    grad_values = (
        norm_scale * weighted - values * (norm_scale * norm_scale * norm_scale) * inner_mean
    )
    return (grad_values, jnp.sum(grad_rows * values * norm_scale, axis=0))


def adam_update(weight, gradient, first_old, second_old, decayed, step_rate):
    first_new = beta_first * first_old + (1.0 - beta_first) * gradient
    second_new = beta_second * second_old + (1.0 - beta_second) * gradient * gradient
    mean_hat = first_new / (1.0 - beta_first**adam_step)
    square_hat = second_new / (1.0 - beta_second**adam_step)
    new_weight = weight - step_rate * (
        mean_hat / (jnp.sqrt(square_hat) + adam_eps) + decayed * decay_rate * weight
    )
    return (first_new, second_new, new_weight)


def dot(lhs, rhs, over):
    return lax.dot_general(lhs, rhs, ((over[0:1], over[1:2]), ((), ())), preferred_element_type=jnp.float32)


def masked_scores(queries, all_keys, allowed, score_scale):
    scores = (
        jnp.einsum("sqhd,skd->shqk", queries, all_keys, preferred_element_type=jnp.float32)
        * score_scale
    )
    return jnp.where(allowed, scores, MASK_FILL)


def local(
    sizes,
    hidden_in,
    segment_ids,
    out_grad,
    norm_gains,
    query_weight,
    query_bias,
    kv_weight,
    kv_bias,
    out_weight,
    gate_up_weight,
    down_weight,
    *moments,
):
    low = jnp.bfloat16
    wide = jnp.float32
    dps, ctxs, tensors = sizes
    n = dps * ctxs
    seq_count, local_len, model_width = hidden_in.shape
    seq_length = segment_ids.shape[1]
    row_count = seq_count * local_len
    shard_rows = query_weight.shape[1]
    heads_here = query_weight.shape[2] // HD
    q_width = heads_here * HD
    hidden_units = down_weight.shape[1]
    local_start = lax.axis_index("ctx") * local_len
    kv_head = lax.axis_index("tensor") * heads_here // (H // KV)
    score_scale = HD ** (-0.5)
    numbers = iter(range(1, 100))

    def move(**what):
        return transfer(sizes, next(numbers), **what)

    attention_shards = [
        jnp.concatenate(
            [
                query_weight[layer],
                lax.dynamic_slice_in_dim(kv_weight[layer], kv_head * HD, HD, 1),
                lax.dynamic_slice_in_dim(kv_weight[layer], (KV + kv_head) * HD, HD, 1),
                out_weight[layer].T,
            ],
            axis=1,
        )
        for layer in range(LAYERS)
    ]
    gate_shards = [gate_up_weight[layer, :, 0] for layer in range(LAYERS)]
    up_shards = [gate_up_weight[layer, :, 1] for layer in range(LAYERS)]
    down_shards = [down_weight[layer].T for layer in range(LAYERS)]

    bias_part = kv_bias.shape[1]
    head_part = query_bias.shape[2]
    small_width = -(-max(shard_rows, bias_part) // 128) * 128
    pad = lambda a: jnp.pad(a, ((0, 0), (0, small_width - a.shape[1])))
    small_rows = LAYERS * (2 + heads_here + 1)
    small_shard = jnp.pad(
        jnp.concatenate(
            [
                pad(norm_gains.reshape(LAYERS * 2, shard_rows)),
                pad(query_bias.reshape(LAYERS * heads_here, head_part)),
                pad(kv_bias),
            ],
            axis=0,
        ),
        ((0, -small_rows % ROW_TILE), (0, 0)),
    )

    small, attention_weights = move(gathers=[small_shard, attention_shards[0]])
    at = LAYERS * 2
    gains = (
        small[:, :at, :shard_rows]
        .transpose(1, 0, 2)
        .reshape(LAYERS, 2, model_width)
        .astype(wide)
    )
    q_biases = (
        small[:, at : at + LAYERS * heads_here, :head_part]
        .transpose(1, 0, 2)
        .reshape(LAYERS, q_width)
        .astype(wide)
    )
    at += LAYERS * heads_here
    kv_biases = small[:, at : at + LAYERS, :bias_part].transpose(1, 0, 2).reshape(LAYERS, 2 * KV, HD)
    kv_biases = jnp.concatenate(
        [
            lax.dynamic_slice_in_dim(kv_biases, kv_head, 1, 1)[:, 0],
            lax.dynamic_slice_in_dim(kv_biases, KV + kv_head, 1, 1)[:, 0],
        ],
        axis=1,
    ).astype(wide)

    own_segments = lax.dynamic_slice_in_dim(segment_ids, local_start, local_len, 1)
    earlier = jnp.sum(
        (segment_ids[:, None, :] < own_segments[:, :, None]).astype(jnp.int32), axis=-1
    )
    token_index = local_start + jnp.arange(local_len, dtype=jnp.int32)
    position = (token_index[None, :] - earlier).astype(wide)
    frequency = ROPE_BASE ** (-jnp.arange(HD // 2, dtype=wide) / (HD // 2))
    angles = position[..., None] * frequency
    cosine = jnp.cos(angles).reshape(row_count, 1, HD // 2)
    sine = jnp.sin(angles).reshape(row_count, 1, HD // 2)
    key_index = jnp.arange(seq_length, dtype=jnp.int32)
    allowed = (own_segments[:, :, None] == segment_ids[:, None, :]) & (
        key_index[None, None, :] <= token_index[None, :, None]
    )
    allowed = allowed[:, None]

    hidden = hidden_in.astype(wide).reshape(row_count, model_width)
    stored = []
    gate_weights = up_weights = down_weights = None
    for layer in range(LAYERS):
        w_attention = attention_weights.reshape(model_width, q_width + 2 * HD + q_width)
        w_in = w_attention[:, : q_width + 2 * HD]
        w_out = w_attention[:, q_width + 2 * HD :]
        scale_one = lax.rsqrt(jnp.mean(hidden * hidden, axis=-1, keepdims=True) + NORM_EPS)
        normed = (hidden * scale_one * gains[layer, 0]).astype(low)
        lin = dot(normed, w_in, (1, 0)) + jnp.concatenate([q_biases[layer], kv_biases[layer]])
        lin_heads = lin[:, : q_width + HD].reshape(row_count, heads_here + 1, HD)
        turned = rotate(lin_heads, cosine, sine).astype(low)
        queries = turned[:, :heads_here].reshape(seq_count, local_len, heads_here, HD)
        pair = jnp.concatenate([turned[:, heads_here], lin[:, q_width + HD :].astype(low)], axis=1)
        if layer == 0:
            down_weights, pairs = move(gathers=[down_shards[0]], pieces=[pair])
        else:
            (pairs,) = move(pieces=[pair])
        pairs = (
            pairs.reshape(ctxs, seq_count, local_len, 2 * HD)
            .transpose(1, 0, 2, 3)
            .reshape(seq_count, seq_length, 2 * HD)
        )
        all_keys, all_values = pairs[..., :HD], pairs[..., HD:]
        scores = masked_scores(queries, all_keys, allowed, score_scale)
        row_max = jnp.max(scores, axis=-1, keepdims=True)
        exp_scores = jnp.exp(scores - row_max)
        row_total = jnp.sum(exp_scores, axis=-1, keepdims=True)
        weights = exp_scores / row_total
        log_total = row_max + jnp.log(row_total)
        mixture = jnp.einsum(
            "shqk,skd->sqhd", weights.astype(low), all_values, preferred_element_type=wide
        )
        mixed_low = mixture.reshape(row_count, q_width).astype(low)
        part = dot(mixed_low, w_out, (1, 1)).astype(low)
        total, gate_weights, up_weights = move(
            z_sums=[part], gathers=[gate_shards[layer], up_shards[layer]]
        )
        w_gate = gate_weights.reshape(model_width, hidden_units)
        w_up = up_weights.reshape(model_width, hidden_units)
        w_down = down_weights.reshape(model_width, hidden_units)
        middle = hidden + total.astype(wide)
        scale_two = lax.rsqrt(jnp.mean(middle * middle, axis=-1, keepdims=True) + NORM_EPS)
        normed_two = (middle * scale_two * gains[layer, 1]).astype(low)
        gate = dot(normed_two, w_gate, (1, 0))
        up = dot(normed_two, w_up, (1, 0))
        inner_low = (jax.nn.silu(gate) * up).astype(low)
        stored.append(
            (
                hidden,
                scale_one,
                normed,
                queries,
                all_keys,
                all_values,
                log_total,
                mixed_low,
                middle,
                scale_two,
                normed_two,
                gate,
                up,
                inner_low,
                w_in,
                w_out,
                w_gate,
                w_up,
                w_down,
            )
        )
        part = dot(inner_low, w_down, (1, 1)).astype(low)
        if layer + 1 < LAYERS:
            total, attention_weights, down_weights = move(
                z_sums=[part], gathers=[attention_shards[layer + 1], down_shards[layer + 1]]
            )
            hidden = middle + total.astype(wide)
        else:
            last_part = part

    def split(gradient):
        return gradient.astype(low).reshape(n, shard_rows, gradient.shape[1])

    def by_owner(row, width):
        return jnp.pad(row.reshape(n, 1, width), ((0, 0), (0, 0), (0, small_width - width)))

    grad_hidden = out_grad.astype(wide).reshape(row_count, model_width)
    done = [{} for _ in range(LAYERS)]
    small_grads = [None] * LAYERS
    waiting = []
    for layer in reversed(range(LAYERS)):
        (
            layer_input,
            scale_one,
            normed,
            queries,
            all_keys,
            all_values,
            log_total,
            mixed_low,
            middle,
            scale_two,
            normed_two,
            gate,
            up,
            inner_low,
            w_in,
            w_out,
            w_gate,
            w_up,
            w_down,
        ) = stored[layer]
        grad_low = grad_hidden.astype(low)
        grad_down_w = split(dot(grad_low, inner_low, (0, 0)))
        grad_inner = dot(grad_low, w_down, (1, 0))
        sigmoid_gate = jax.nn.sigmoid(gate)
        grad_gate = (
            grad_inner * up * sigmoid_gate * (1.0 + gate * (1.0 - sigmoid_gate))
        ).astype(low)
        grad_upper = (grad_inner * gate * sigmoid_gate).astype(low)
        grad_gate_w = split(dot(normed_two, grad_gate, (0, 0)))
        grad_up_w = split(dot(normed_two, grad_upper, (0, 0)))
        part = (dot(grad_gate, w_gate, (1, 1)) + dot(grad_upper, w_up, (1, 1))).astype(low)
        total, done[layer]["down"], done[layer]["gate"], *rest = move(
            z_sums=[part], scatters=[grad_down_w, grad_gate_w] + [a for _, _, a in waiting]
        )
        for (name, owner, _), result in zip(waiting, rest):
            done[owner][name] = result
        back_two, grad_gain_two = norm_back(middle, scale_two, gains[layer, 1], total.astype(wide))
        grad_middle = grad_hidden + back_two
        grad_mid_low = grad_middle.astype(low)
        grad_out_w = split(dot(grad_mid_low, mixed_low, (0, 0)))
        grad_mixed = (
            dot(grad_mid_low, w_out, (1, 0))
            .astype(low)
            .reshape(seq_count, local_len, heads_here, HD)
        )
        scores = masked_scores(queries, all_keys, allowed, score_scale)
        probabilities = jnp.exp(scores - log_total)
        grad_probs = jnp.einsum(
            "sqhd,skd->shqk", grad_mixed, all_values, preferred_element_type=wide
        )
        row_delta = jnp.sum(probabilities * grad_probs, axis=-1, keepdims=True)
        grad_scores = (probabilities * (grad_probs - row_delta)).astype(low)
        grad_queries = (
            jnp.einsum("shqk,skd->sqhd", grad_scores, all_keys, preferred_element_type=wide)
            * score_scale
        )
        grad_keys = (
            jnp.einsum("shqk,sqhd->skd", grad_scores, queries, preferred_element_type=wide)
            * score_scale
        )
        grad_values = jnp.einsum(
            "shqk,sqhd->skd", probabilities.astype(low), grad_mixed, preferred_element_type=wide
        )
        grad_pair = jnp.concatenate([grad_keys, grad_values], axis=2).astype(low)
        grad_pair = (
            grad_pair.reshape(seq_count, ctxs, local_len, 2 * HD)
            .transpose(1, 0, 2, 3)
            .reshape(ctxs, row_count, 2 * HD)
        )
        (grad_pair,) = move(swaps=[grad_pair])
        grad_pair = jnp.sum(grad_pair.astype(wide), axis=0)
        grad_heads = jnp.concatenate(
            [grad_queries.reshape(row_count, heads_here, HD), grad_pair[:, None, :HD]], axis=1
        )
        grad_lin = jnp.concatenate(
            [
                rotate_back(grad_heads, cosine, sine).reshape(row_count, q_width + HD),
                grad_pair[:, HD:],
            ],
            axis=1,
        ).astype(low)
        grad_in_w = split(dot(normed, grad_lin, (0, 0)))
        grad_bias = jnp.sum(grad_lin.astype(wide), axis=0)
        part = dot(grad_lin, w_in, (1, 1)).astype(low)
        zeros = jnp.zeros((2 * KV, HD), wide)
        kv_bias_grad = lax.dynamic_update_slice_in_dim(
            zeros, grad_bias[q_width : q_width + HD][None], kv_head, 0
        )
        kv_bias_grad = lax.dynamic_update_slice_in_dim(
            kv_bias_grad, grad_bias[q_width + HD :][None], KV + kv_head, 0
        )
        head_rows = grad_bias[:q_width].reshape(heads_here, HD)
        small_grads[layer] = [grad_gain_two, head_rows, kv_bias_grad.reshape(-1)]
        if layer > 0:
            total, done[layer]["up"] = move(z_sums=[part], scatters=[grad_up_w])
            waiting = [("out", layer, grad_out_w), ("in", layer, grad_in_w)]
        else:
            total, block_sum, done[layer]["up"], done[layer]["in"], done[layer]["out"] = move(
                z_sums=[part, last_part], scatters=[grad_up_w, grad_in_w, grad_out_w]
            )
        back_one, grad_gain_one = norm_back(
            layer_input, scale_one, gains[layer, 0], total.astype(wide)
        )
        small_grads[layer].insert(0, grad_gain_one)
        grad_hidden = grad_middle + back_one

    block_out = (stored[-1][8] + block_sum.astype(wide)).astype(low)
    block_out = block_out.reshape(seq_count, local_len, model_width)
    input_grad = grad_hidden.reshape(seq_count, local_len, model_width)

    small_part = []
    for layer in range(LAYERS):
        gain_one, gain_two, head_rows, kv_row = small_grads[layer]
        small_part += [by_owner(gain_one, shard_rows), by_owner(gain_two, shard_rows)]
        small_part += [by_owner(head_rows[head], head_part) for head in range(heads_here)]
        small_part.append(by_owner(kv_row, bias_part))
    small_part = jnp.pad(
        jnp.concatenate(small_part, axis=1), ((0, 0), (0, -small_rows % ROW_TILE), (0, 0))
    ).astype(low)
    (small_sum,) = move(scatters=[small_part])
    small_sum = small_sum[:small_rows].reshape(LAYERS, 2 + heads_here + 1, small_width)
    gains_grad = small_sum[:, :2, :shard_rows]
    query_bias_grad = small_sum[:, 2 : 2 + heads_here, :head_part]

    kv_part = jnp.stack([done[layer]["in"][:, q_width:] for layer in range(LAYERS)])
    kv_full = jnp.zeros((LAYERS, shard_rows, 2 * KV * HD), wide)
    kv_full = lax.dynamic_update_slice_in_dim(kv_full, kv_part[..., :HD], kv_head * HD, 2)
    kv_full = lax.dynamic_update_slice_in_dim(kv_full, kv_part[..., HD:], (KV + kv_head) * HD, 2)
    kv_weight_grad, kv_bias_grad = lax.psum(
        (kv_full, small_sum[:, 2 + heads_here, :bias_part]), "tensor"
    )

    stack = lambda name, f=lambda a: a: jnp.stack([f(done[layer][name]) for layer in range(LAYERS)])
    grads = (
        gains_grad,
        stack("in", lambda a: a[:, :q_width]),
        query_bias_grad,
        kv_weight_grad,
        kv_bias_grad,
        stack("out", lambda a: a.T),
        jnp.stack([stack("gate"), stack("up")], axis=2),
        stack("down", lambda a: a.T),
    )
    params = (
        norm_gains,
        query_weight,
        query_bias,
        kv_weight,
        kv_bias,
        out_weight,
        gate_up_weight,
        down_weight,
    )
    firsts, seconds = moments[:8], moments[8:]
    decays = (0.0, 1.0, 0.0, 1.0, 0.0, 1.0, 1.0, 1.0)
    rates = (0.5, 0.02, 0.5, 0.02, 0.5, 0.1, 0.02, 0.02)
    moved = [
        adam_update(
            params[i].astype(wide), grads[i], firsts[i], seconds[i], decays[i], rates[i]
        )
        for i in range(8)
    ]
    return (
        block_out,
        input_grad,
        *grads,
        *[moved[i][0] for i in range(8)],
        *[moved[i][1] for i in range(8)],
        *[moved[i][2] for i in range(8)],
    )


def solution(mesh):
    params = (
        P(None, None, ("dp", "ctx")),
        P(None, ("dp", "ctx"), "tensor"),
        P(None, "tensor", ("dp", "ctx")),
        P(None, ("dp", "ctx"), None),
        P(None, ("dp", "ctx")),
        P(None, "tensor", ("dp", "ctx")),
        P(None, ("dp", "ctx"), None, "tensor"),
        P(None, "tensor", ("dp", "ctx")),
    )
    rows = P("dp", "ctx", None)
    sizes = (mesh.shape["dp"], mesh.shape["ctx"], mesh.shape["tensor"])
    return jax.shard_map(
        functools.partial(local, sizes),
        mesh=mesh,
        in_specs=(rows, P("dp", None), rows, *params, *params, *params),
        out_specs=(rows, rows, *params, *params, *params, *params),
        check_vma=False,
    )
```

time: 2000 us -> 1390 us (0.69)
  waiting for transfers between devices: 1320 us -> 0.02 us
  Pallas kernels: 0 us -> 876 us
  blocking collectives: 125 us -> 10.4 us
  local copies, waits for them, and re-layouts: 222 us -> 166 us
    pallas_call x0 -> x13, Pallas kernels: none -> 876 us  [transfer(): pl.pallas_call(functools.partial(transfer_kernel, sizes, counts, plan), o...]
    reduce_scatter x12 -> x0, waiting for transfers between devices: 581 us -> none  [the longest x2 201 us: scatter_layer(): lax.psum_scatter(w_gate_up.astype(jnp.bfloat16), ('dp', 'ctx'), scatter_d...]
    psum x7 -> x1, waiting for transfers between devices: 467 us -> 0.01 us  [local(): lax.psum((kv_full, small_sum[:, 2 + heads_here, :bias_part]), 'tensor')]
    all_gather x10 -> x0, waiting for transfers between devices: 213 us -> none  [the longest x2 155 us: gather_layer(): lax.all_gather(w_gate_up, ('dp', 'ctx'), axis=0, tiled=True)]
    all_gather x8 -> x0, blocking collectives: 96.7 us -> none  [the longest x2 38.2 us: gather_layer(): lax.all_gather(gains, ('dp', 'ctx'), axis=1, tiled=True)]
    all_gather x4 -> x0, local copies, waits for them, and re-layouts: 70.6 us -> none  [the longest x2 70.4 us: gather_layer(): lax.all_gather(w_gate_up, ('dp', 'ctx'), axis=0, tiled=True)]
    convert_element_type x2 -> x8, local copies, waits for them, and re-layouts: 0.36 us -> 61.6 us  [the longest x6 61.5 us: split(): return gradient.astype(low).reshape(n, shard_rows, gradient.shape[1])]
    unnamed x37 -> x1, waiting for transfers between devices: 54.9 us -> 0.02 us
  transfers between devices with their start and end apart: 33 -> 1, of which waited for: 26 -> 0; matrix products, arithmetic and copies ran while one was open for 18% -> 8% of each run, Pallas kernels for 0% -> 1%
where the time goes in v1:
time: 1390 us; the launch traced here: 1380 us
  Pallas kernels  876 us (63%)
  matrix products  206 us (15%)
  local copies, waits for them, and re-layouts  166 us (12%)
  other arithmetic  104 us (7%)
  between operations  15.9 us (1%)
    pallas_call x13, Pallas kernels, transfer(): pl.pallas_call(functools.partial(transfer_kernel, sizes, counts, plan), o...  876 us
    dot_general x30, matrix products, dot(): lax.dot_general(lhs, rhs, ((over[0:1], over[1:2]), ((), ())), preferred_e...  184 us
    unnamed x252, local copies, waits for them, and re-layouts  62.5 us
    convert_element_type x6, local copies, waits for them, and re-layouts, split(): return gradient.astype(low).reshape(n, shard_rows, gradient.shape[1])  61.5 us
    sub x8, other arithmetic, adam_update(): weight - step_rate * (mean_hat / (jnp.sqrt(square_hat) + adam_eps) + deca...  34.2 us
  transfers between devices with their start and end apart: 1, of which 0 were waited for; matrix products, arithmetic and copies ran while one was open for 8% of the time, Pallas kernels for 1%

profile of v1, /device:TPU:0, one launch (start us, length us, event | category | flops | bytes accessed | tf_op | source)
XLA Modules:
  0.0 1377.4 jit_solution(5097135735522870717)
XLA Ops:
  14.2 21.6 %transfer1.1 = (bf16[8,16,256]{2,1,0:T(8,128)(2,1)}, bf16[8,192,1024]{2,1,0:T(8,128)(2,1)}) custom-call(bf16[16,256]{1,0:T(8,128)(2,1)} %pad.75.refs_0_, bf16[192,1024]{1,0:T(8,128)(2,1)} %get-tuple-element.312.refs_1_), custom_call_target="tpu_custom_call" | custom-call | tf_op jit(solution)/shard_map/transfer1/pallas_call | solution.py:511
  54.1 41.2 %transfer2.1 = (bf16[8,192,2240]{2,1,0:T(8,128)(2,1)}, bf16[2,512,256]{2,1,0:T(8,128)(2,1)}) custom-call(bf16[192,2240]{1,0:T(8,128)(2,1)} %get-tuple-element.255.refs_0_, bf16[512,256]{1,0:T(8,128)(2,1)} %pad_maximum_fusion.16.refs_1_), custom_call_target="tpu_custom_call" | custom-call | tf_op jit(solution)/shard_map/transfer2/pallas_call | solution.py:511
  113.2 88.2 %transfer3.1 = (bf16[512,1536]{1,0:T(8,128)(2,1)}, bf16[8,192,2240]{2,1,0:T(8,128)(2,1)}, bf16[8,192,2240]{2,1,0:T(8,128)(2,1)}) custom-call(bf16[512,1536]{1,0:T(8,128)(2,1)} %convolution_convert_fusion.13.refs_0_, bf16[192,2240]{1,0:T(8,128)(2,1)} %get-tuple-element.319.refs_1_, bf16[192,2240]{1,0:T(8,128)(2,1)} %get-tuple-element.318.refs_2_), custom_call_target="tpu_custom_call" | custom-call | tf_op jit(solution)/shard_map/transfer3/pallas_call | solution.py:511
  204.7 10.8 fusion.154
  215.5 11.1 multiply_convert_fusion.5
  231.7 83.2 %transfer4.1 = (bf16[512,1536]{1,0:T(8,128)(2,1)}, bf16[8,192,1024]{2,1,0:T(8,128)(2,1)}, bf16[8,192,2240]{2,1,0:T(8,128)(2,1)}) custom-call(bf16[512,1536]{1,0:T(8,128)(2,1)} %convolution_convert_fusion.12.refs_0_, bf16[192,1024]{1,0:T(8,128)(2,1)} %get-tuple-element.313.refs_1_, bf16[192,2240]{1,0:T(8,128)(2,1)} %get-tuple-element.254.refs_2_), custom_call_target="tpu_custom_call" | custom-call | tf_op jit(solution)/shard_map/transfer4/pallas_call | solution.py:511
  328.0 10.4 transfer5.1
  349.9 88.2 %transfer6.1 = (bf16[512,1536]{1,0:T(8,128)(2,1)}, bf16[8,192,2240]{2,1,0:T(8,128)(2,1)}, bf16[8,192,2240]{2,1,0:T(8,128)(2,1)}) custom-call(bf16[512,1536]{1,0:T(8,128)(2,1)} %convolution_convert_fusion.11.refs_0_, bf16[192,2240]{1,0:T(8,128)(2,1)} %get-tuple-element.317.refs_1_, bf16[192,2240]{1,0:T(8,128)(2,1)} %get-tuple-element.316.refs_2_), custom_call_target="tpu_custom_call" | custom-call | tf_op jit(solution)/shard_map/transfer6/pallas_call | solution.py:511
  455.3 12.7 multiply_convert_fusion.2
  468.1 9.4 fusion.156
  488.8 10.2 copy.188
  499.0 10.2 copy.189
  509.2 9.6 fusion.56.refs_0_
  518.8 122.7 %transfer7.1 = (bf16[512,1536]{1,0:T(8,128)(2,1)}, f32[192,2240]{1,0:T(8,128)}, f32[192,2240]{1,0:T(8,128)}) custom-call(bf16[512,1536]{1,0:T(8,128)(2,1)} %fusion.56.refs_0_, bf16[8,192,2240]{2,1,0:T(8,128)(2,1)} %bitcast.351, bf16[8,192,2240]{2,1,0:T(8,128)(2,1)} %bitcast.352), custom_call_target="tpu_custom_call" | custom-call | tf_op jit(solution)/shard_map/transfer7/pallas_call | solution.py:511
  663.3 9.1 transfer8.1
  684.5 10.4 copy.197
  699.0 97.5 %transfer9.1 = (bf16[512,1536]{1,0:T(8,128)(2,1)}, f32[192,2240]{1,0:T(8,128)}) custom-call(bf16[512,1536]{1,0:T(8,128)(2,1)} %convolution_convert_fusion.10.refs_0_, bf16[8,192,2240]{2,1,0:T(8,128)(2,1)} %bitcast.353), custom_call_target="tpu_custom_call" | custom-call | tf_op jit(solution)/shard_map/transfer9/pallas_call | solution.py:511
  807.0 12.5 multiply_convert_fusion
  819.5 9.4 fusion.157
  839.7 10.2 copy.198
  849.9 10.3 copy.199
  868.8 138.4 %transfer10.1 = (bf16[512,1536]{1,0:T(8,128)(2,1)}, f32[192,2240]{1,0:T(8,128)}, f32[192,2240]{1,0:T(8,128)}, f32[192,384]{1,0:T(8,128)}, f32[192,640]{1,0:T(8,128)}) custom-call(bf16[512,1536]{1,0:T(8,128)(2,1)} %fusion.57.refs_0_, bf16[8,192,2240]{2,1,0:T(8,128)(2,1)} %bitcast.348, bf16[8,192,2240]{2,1,0:T(8,128)(2,1)} %bitcast.349, ...), custom_call_target="tpu_custom_call" | custom-call | tf_op jit(solution)/shard_map/transfer10/pallas_call | solution.py:511
  1028.9 9.1 transfer11.1
  1067.6 10.2 copy.207
  1077.8 158.2 %transfer12.1 = (bf16[512,1536]{1,0:T(8,128)(2,1)}, bf16[512,1536]{1,0:T(8,128)(2,1)}, f32[192,2240]{1,0:T(8,128)}, f32[192,640]{1,0:T(8,128)}, f32[192,384]{1,0:T(8,128)}) custom-call(bf16[512,1536]{1,0:T(8,128)(2,1)} %convolution_convert_fusion.9.refs_0_, bf16[512,1536]{1,0:T(8,128)(2,1)} %convolution_convert_fusion.8.refs_1_, ...), custom_call_target="tpu_custom_call" | custom-call | tf_op jit(solution)/shard_map/transfer12/pallas_call | solution.py:511
  1266.3 10.4 psum.15
  1287.7 16.1 %convert_subtract_fusion = (f32[2,192,2,2240]{3,1,0,2:T(8,128)}, f32[2,192,2,2240]{3,1,0,2:T(8,128)}, f32[2,192,2,2240]{3,1,0,2:T(8,128)}, f32[2,192,2,2240]{3,1,0,2:T(8,128)}) fusion(bf16[2,192,2,2240]{3,2,1,0:T(2,128)(2,1)S(1)} %copy-done.14, f32[2,192,1,2240]{3,1,0,2:T(8,128)S(1)} %maximum_bitcast_fusion.1, ...), kind=kLoop, calls=%fused_computation.8 | loop fusion | flops 29245440 | bytes 51609600 | tf_op jit(solution)/shard_map/sub | solution.py:552
  1303.8 8.9 convert_subtract_fusion.1
  1313.8 11.4 copy.227
  1325.9 11.4 copy.229
  1337.9 11.6 copy.231
  1350.0 11.4 copy.233
  (441 shorter events, 275.4 us)
Async XLA Ops:
  7.2 31.3 %copy-start.2 = (bf16[1,512,1536]{2,1,0:T(8,128)(2,1)S(1)}, bf16[1,512,1536]{2,1,0:T(8,128)(2,1)}, u32[]{:S(2)}) copy-start(bf16[1,512,1536]{2,1,0:T(8,128)(2,1)} %param.27) | copy-start | bytes 4718596
  7.2 1358.7 %all-reduce.19.cloned.1.call-start = ((), (), s32[]{:S(2)}) async-start(), calls=%async_computation | async-start | bytes 1572864 | tf_op jit(solution)/shard_map/psum | solution.py:896
  38.6 165.6 %copy-start.81 = (f32[1536]{0:T(1024)}, f32[1536]{0:T(1024)S(1)}, u32[]{:S(2)}) copy-start(f32[1536]{0:T(1024)S(1)} %get-tuple-element.202) | copy-start | bytes 18436
  50.9 44.4 %copy-start.34 = (pred[512,1024]{0,1:T(8,128)(4,1)}, pred[512,1024]{0,1:T(8,128)(4,1)S(1)}, u32[]{:S(2)}) copy-start(pred[512,1024]{0,1:T(8,128)(4,1)S(1)} %fusion.58) | copy-start | bytes 1572868
  52.7 42.6 %copy-start.27 = (f32[512,64]{1,0:T(8,128)}, f32[512,64]{1,0:T(8,128)S(1)}, u32[]{:S(2)}) copy-start(f32[512,64]{1,0:T(8,128)S(1)} %get-tuple-element.279) | copy-start | bytes 393220
  52.7 42.6 %copy-start.45 = (f32[512,64]{1,0:T(8,128)}, f32[512,64]{1,0:T(8,128)S(1)}, u32[]{:S(2)}) copy-start(f32[512,64]{1,0:T(8,128)S(1)} %get-tuple-element.278) | copy-start | bytes 393220
  53.0 44.8 %copy-start.17 = (bf16[512,4,64]{2,0,1:T(8,128)(2,1)}, bf16[512,4,64]{2,0,1:T(8,128)(2,1)S(1)}, u32[]{:S(2)}) copy-start(bf16[512,4,64]{2,0,1:T(8,128)(2,1)S(1)} %get-tuple-element.252) | copy-start | bytes 786436
  53.0 44.8 %copy-start.19 = (bf16[512,4,64]{2,0,1:T(8,128)(2,1)}, bf16[512,4,64]{2,0,1:T(8,128)(2,1)S(1)}, u32[]{:S(2)}) copy-start(bf16[512,4,64]{2,0,1:T(8,128)(2,1)S(1)} %get-tuple-element.253) | copy-start | bytes 786436
  204.1 11.4 copy-start.86
  204.7 10.8 copy-start.55
  204.7 21.9 %slice-start.6 = ((s8[7077888]{0:T(1024)(128)(4,1)}), s8[4194304]{0:T(1024)(128)(4,1)S(1)}, s32[]{:S(2)}) async-start(s8[7077888]{0:T(1024)(128)(4,1)} %bitcast.415), calls=%async_computation.7 | async-start | bytes 8388608
  215.5 11.1 slice-start.7
  326.6 11.8 copy-start.35
  327.0 14.0 %copy-start.21 = (bf16[512,4,64]{2,0,1:T(8,128)(2,1)}, bf16[512,4,64]{2,0,1:T(8,128)(2,1)S(1)}, u32[]{:S(2)}) copy-start(bf16[512,4,64]{2,0,1:T(8,128)(2,1)S(1)} %get-tuple-element.250) | copy-start | bytes 786436
  327.0 14.0 %copy-start.23 = (bf16[512,4,64]{2,0,1:T(8,128)(2,1)}, bf16[512,4,64]{2,0,1:T(8,128)(2,1)S(1)}, u32[]{:S(2)}) copy-start(bf16[512,4,64]{2,0,1:T(8,128)(2,1)S(1)} %get-tuple-element.251) | copy-start | bytes 786436
  348.5 89.6 %copy-start.5 = (f32[512,1536]{1,0:T(8,128)S(1)}, f32[512,1536]{1,0:T(8,128)}, u32[]{:S(2)}) copy-start(f32[512,1536]{1,0:T(8,128)} %get-tuple-element.235) | copy-start | bytes 9437188
  440.2 204.5 %copy-start.4 = (f32[512,1536]{1,0:T(8,128)}, f32[512,1536]{1,0:T(8,128)S(1)}, u32[]{:S(2)}) copy-start(f32[512,1536]{1,0:T(8,128)S(1)} %get-tuple-element.233) | copy-start | bytes 9437188
  440.3 9.6 slice-start.4
  440.6 36.9 %copy-start.58 = (bf16[512,1536]{1,0:T(8,128)(2,1)}, bf16[512,1536]{1,0:T(8,128)(2,1)S(1)}, u32[]{:S(2)}) copy-start(bf16[512,1536]{1,0:T(8,128)(2,1)S(1)} %multiply_convert_fusion.6) | copy-start | bytes 4718596
  468.1 15.1 %copy-start.106 = (bf16[512,2240]{0,1:T(8,128)(2,1)}, bf16[512,2240]{0,1:T(8,128)(2,1)S(1)}, u32[]{:S(2)}) copy-start(bf16[512,2240]{0,1:T(8,128)(2,1)S(1)} %get-tuple-element.238) | copy-start | bytes 6881284
  684.5 10.4 copy-start.49
  699.0 97.5 %copy-start.6 = (f32[512,1536]{1,0:T(8,128)S(1)}, f32[512,1536]{1,0:T(8,128)}, u32[]{:S(2)}) copy-start(f32[512,1536]{1,0:T(8,128)} %get-tuple-element.235) | copy-start | bytes 9437188
  849.9 10.3 copy-start.108
  868.8 138.4 %copy-start.3 = (bf16[1,512,1536]{2,1,0:T(8,128)(2,1)S(1)}, bf16[1,512,1536]{2,1,0:T(8,128)(2,1)}, u32[]{:S(2)}) copy-start(bf16[1,512,1536]{2,1,0:T(8,128)(2,1)} %param.27) | copy-start | bytes 4718596
  868.8 138.4 %copy-start.12 = (bf16[512,1536]{1,0:T(8,128)(2,1)S(1)}, bf16[512,1536]{1,0:T(8,128)(2,1)}, u32[]{:S(2)}) copy-start(bf16[512,1536]{1,0:T(8,128)(2,1)} %get-tuple-element.65) | copy-start | bytes 4718596
  868.8 138.5 %copy-start.82 = (f32[1536]{0:T(1024)S(1)}, f32[1536]{0:T(1024)}, u32[]{:S(2)}) copy-start(f32[1536]{0:T(1024)} %copy-done.81) | copy-start | bytes 18436
  868.8 138.5 %copy-start.87 = (f32[512]{0:T(512)S(1)}, f32[512]{0:T(512)}, u32[]{:S(2)}) copy-start(f32[512]{0:T(512)} %copy-done.86) | copy-start | bytes 6148
  1027.0 13.0 copy-start.68
  1287.7 16.1 %copy-start.25 = (bf16[2,2240,192]{1,2,0:T(8,128)(2,1)S(1)}, bf16[2,2240,192]{1,2,0:T(8,128)(2,1)}, u32[]{:S(2)}) copy-start(bf16[2,2240,192]{1,2,0:T(8,128)(2,1)} %param.37) | copy-start | bytes 5160964
  1287.7 16.1 %copy-start.38 = (f32[2,2240,192]{1,2,0:T(8,128)S(1)}, f32[2,2240,192]{1,2,0:T(8,128)}, u32[]{:S(2)}) copy-start(f32[2,2240,192]{1,2,0:T(8,128)} %param.53) | copy-start | bytes 10321924
  1350.0 11.4 copy-start.91
  1350.0 11.4 copy-start.98
  (89 other events, 356.8 us)
Sparse Core Ops, SparseCore 0:
  1239.1 42.6 all-reduce.18

commit v2 on v1

--- a/solution.py
+++ b/solution.py
@@ -4,6 +4,7 @@
 import jax.numpy as jnp
 from jax import lax
 from jax.experimental import pallas as pl
+from jax.experimental.layout import Layout, with_layout_constraint
 from jax.experimental.pallas import tpu as pltpu
 from jax.sharding import PartitionSpec as P
 
@@ -24,6 +25,7 @@
 MESH = pl.DeviceIdType.MESH
 ROW_TILE = 16
 Z_CHUNKS = 8
+NEAR_LEAD, FAR_LAG, NEAR_LAG = 2, 6, 8
 
 
 class Place:
@@ -348,8 +350,8 @@
 
     def step(turn):
         def run():
-            chunk = turn
-            if chunk < Z_CHUNKS:
+            chunk = turn + NEAR_LEAD
+            if 0 <= chunk < Z_CHUNKS:
 
                 @pl.when(inner)
                 def _():
@@ -357,6 +359,8 @@
                     add(near, chunk, acc)
                     summing(near, chunk, acc, onward).start()
 
+            chunk = turn
+            if 0 <= chunk < Z_CHUNKS:
                 summing(far, chunk, acc, back).wait_recv()
 
                 @pl.when(inner)
@@ -369,7 +373,7 @@
                     add(far, chunk, out)
                     sharing(far, chunk, onward).start()
 
-            chunk = turn - 2
+            chunk = turn - FAR_LAG
             if 0 <= chunk < Z_CHUNKS:
 
                 @pl.when(inner)
@@ -377,7 +381,7 @@
                     sharing(far, chunk, onward).wait_recv()
                     sharing(far, chunk, onward).start()
 
-            chunk = turn - 3
+            chunk = turn - NEAR_LAG
             if 0 <= chunk < Z_CHUNKS:
                 sharing(near, chunk, back).wait_recv()
 
@@ -397,7 +401,7 @@
                 summing(far, chunk, acc, back).wait_send()
                 sharing(near, chunk, back).wait_send()
 
-    return [begin] + [step(turn) for turn in range(Z_CHUNKS + 3)] + [end]
+    return [begin] + [step(turn) for turn in range(-NEAR_LEAD, Z_CHUNKS + NEAR_LAG)] + [end]
 
 
 def transfer_kernel(sizes, counts, plan, *refs):
@@ -458,25 +462,24 @@
         small.append(sems.local(block, dst.at[mine]))
     for copy in small:
         copy.start()
-    stages = [[plane[stage] for plane in planes] for stage in range(4)]
-    for run in stages[0]:
-        run()
+    for plane in planes:
+        plane[0]()
     turns = max([len(line) for line in lines], default=0)
     for turn in range(turns + 1):
-        for stage in (1, 2):
-            if (plan[stage - 1] == turn) or (turn == turns and plan[stage - 1] > turns):
-                for run in stages[stage]:
-                    run()
+        for plane, at in zip(planes, plan):
+            for stage in (1, 2):
+                if min(at[stage - 1], turns) == turn:
+                    plane[stage]()
         for line in lines:
             if turn < len(line):
                 line[turn]()
-    for run in stages[3]:
-        run()
+    for plane in planes:
+        plane[3]()
     for copy in small:
         copy.wait()
 
 
-def transfer(sizes, number, z_sums=(), gathers=(), scatters=(), pieces=(), swaps=(), plan=(99, 99)):
+def transfer(sizes, number, z_sums=(), gathers=(), scatters=(), pieces=(), swaps=(), plan=((99, 99),) * 8):
     n = sizes[0] * sizes[1]
     any_space = pl.BlockSpec(memory_space=pl.ANY)
     in_vmem = pl.BlockSpec(memory_space=pltpu.VMEM)
@@ -519,6 +522,140 @@
         ),
         name="transfer%d" % number,
     )(*args)
+
+
+TILE = 256
+
+
+def mm(lhs, rhs, over):
+    return lax.dot_general(
+        lhs, rhs, (((over[0],), (over[1],)), ((), ())), preferred_element_type=jnp.float32
+    )
+
+
+def in_width(block, width):
+    column = pl.program_id(0) * TILE + lax.broadcasted_iota(jnp.int32, block.shape, 1)
+    return jnp.where(column < width, block, jnp.zeros_like(block))
+
+
+def forward_tile(width, n2, w_gate, w_up, w_down, gate_out, up_out, inner_out, part_out, total):
+    tile = pl.program_id(0)
+    gate = mm(n2[...], w_gate[...], (1, 0))
+    up = mm(n2[...], w_up[...], (1, 0))
+    gate_out[...] = gate
+    up_out[...] = up
+    inner = in_width(gate * jax.nn.sigmoid(gate) * up, width).astype(jnp.bfloat16)
+    inner_out[...] = inner
+    product = mm(inner, in_width(w_down[...], width), (1, 1))
+
+    @pl.when(tile == 0)
+    def _():
+        total[...] = product
+
+    @pl.when(tile > 0)
+    def _():
+        total[...] += product
+
+    @pl.when(tile == pl.num_programs(0) - 1)
+    def _():
+        part_out[...] = total[...].astype(part_out.dtype)
+
+
+def forward_ffn(n2, w_gate, w_up, w_down):
+    rows, model_width = n2.shape
+    width = w_gate.shape[1]
+    whole = pl.BlockSpec((rows, model_width), lambda j: (0, 0))
+    weight = pl.BlockSpec((model_width, TILE), lambda j: (0, j))
+    units = pl.BlockSpec((rows, TILE), lambda j: (0, j))
+    return pl.pallas_call(
+        functools.partial(forward_tile, width),
+        grid=(pl.cdiv(width, TILE),),
+        in_specs=[whole, weight, weight, weight],
+        out_specs=[units, units, units, whole],
+        out_shape=[
+            jax.ShapeDtypeStruct((rows, width), jnp.float32),
+            jax.ShapeDtypeStruct((rows, width), jnp.float32),
+            jax.ShapeDtypeStruct((rows, width), jnp.bfloat16),
+            jax.ShapeDtypeStruct((rows, model_width), jnp.bfloat16),
+        ],
+        scratch_shapes=[pltpu.VMEM((rows, model_width), jnp.float32)],
+        compiler_params=pltpu.CompilerParams(vmem_limit_bytes=56 << 20),
+        name="forward_ffn",
+    )(n2, w_gate, w_up, w_down)
+
+
+def backward_tile(
+    width,
+    grad,
+    n2,
+    gate_in,
+    up_in,
+    inner,
+    w_gate,
+    w_up,
+    w_down,
+    down_out,
+    gate_out,
+    up_out,
+    part_out,
+    grad_t,
+    n2_t,
+    total,
+):
+    tile = pl.program_id(0)
+
+    @pl.when(tile == 0)
+    def _():
+        grad_t[...] = grad[...].T
+        n2_t[...] = n2[...].T
+
+    gate = gate_in[...]
+    slope = jax.nn.sigmoid(gate)
+    grad_inner = mm(grad[...], w_down[...], (1, 0))
+    down_out[...] = mm(grad_t[...], inner[...], (1, 0)).astype(down_out.dtype)
+    grad_gate = grad_inner * up_in[...] * slope * (1.0 + gate * (1.0 - slope))
+    grad_gate = in_width(grad_gate, width).astype(jnp.bfloat16)
+    grad_up = in_width(grad_inner * gate * slope, width).astype(jnp.bfloat16)
+    product = mm(grad_gate, in_width(w_gate[...], width), (1, 1))
+    product += mm(grad_up, in_width(w_up[...], width), (1, 1))
+
+    @pl.when(tile == 0)
+    def _():
+        total[...] = product
+
+    @pl.when(tile > 0)
+    def _():
+        total[...] += product
+
+    gate_out[...] = mm(n2_t[...], grad_gate, (1, 0)).astype(gate_out.dtype)
+    up_out[...] = mm(n2_t[...], grad_up, (1, 0)).astype(up_out.dtype)
+
+    @pl.when(tile == pl.num_programs(0) - 1)
+    def _():
+        part_out[...] = total[...].astype(part_out.dtype)
+
+
+def backward_ffn(grad, n2, gate, up, inner, w_gate, w_up, w_down):
+    rows, model_width = n2.shape
+    width = w_gate.shape[1]
+    whole = pl.BlockSpec((rows, model_width), lambda j: (0, 0))
+    weight = pl.BlockSpec((model_width, TILE), lambda j: (0, j))
+    units = pl.BlockSpec((rows, TILE), lambda j: (0, j))
+    like = jax.ShapeDtypeStruct((model_width, width), jnp.bfloat16)
+    return pl.pallas_call(
+        functools.partial(backward_tile, width),
+        grid=(pl.cdiv(width, TILE),),
+        in_specs=[whole, whole, units, units, units, weight, weight, weight],
+        out_specs=[weight, weight, weight, whole],
+        out_shape=[like, like, like, jax.ShapeDtypeStruct((rows, model_width), jnp.bfloat16)],
+        scratch_shapes=[
+            pltpu.VMEM((model_width, rows), jnp.bfloat16),
+            pltpu.VMEM((model_width, rows), jnp.bfloat16),
+            pltpu.VMEM((rows, model_width), jnp.float32),
+        ],
+        compiler_params=pltpu.CompilerParams(vmem_limit_bytes=56 << 20),
+        name="backward_ffn",
+    )(grad, n2, gate, up, inner, w_gate, w_up, w_down)
 
 
 def rotate(values, cosine, sine):
@@ -710,7 +847,9 @@
         mixed_low = mixture.reshape(row_count, q_width).astype(low)
         part = dot(mixed_low, w_out, (1, 1)).astype(low)
         total, gate_weights, up_weights = move(
-            z_sums=[part], gathers=[gate_shards[layer], up_shards[layer]]
+            z_sums=[part],
+            gathers=[gate_shards[layer], up_shards[layer]],
+            plan=((15, 99), (16, 99)),
         )
         w_gate = gate_weights.reshape(model_width, hidden_units)
         w_up = up_weights.reshape(model_width, hidden_units)
@@ -718,9 +857,7 @@
         middle = hidden + total.astype(wide)
         scale_two = lax.rsqrt(jnp.mean(middle * middle, axis=-1, keepdims=True) + NORM_EPS)
         normed_two = (middle * scale_two * gains[layer, 1]).astype(low)
-        gate = dot(normed_two, w_gate, (1, 0))
-        up = dot(normed_two, w_up, (1, 0))
-        inner_low = (jax.nn.silu(gate) * up).astype(low)
+        gate, up, inner_low, part = forward_ffn(normed_two, w_gate, w_up, w_down)
         stored.append(
             (
                 hidden,
@@ -744,10 +881,11 @@
                 w_down,
             )
         )
-        part = dot(inner_low, w_down, (1, 1)).astype(low)
         if layer + 1 < LAYERS:
             total, attention_weights, down_weights = move(
-                z_sums=[part], gathers=[attention_shards[layer + 1], down_shards[layer + 1]]
+                z_sums=[part],
+                gathers=[attention_shards[layer + 1], down_shards[layer + 1]],
+                plan=((7, 17), (12, 18)),
             )
             hidden = middle + total.astype(wide)
         else:
@@ -786,18 +924,19 @@
             w_down,
         ) = stored[layer]
         grad_low = grad_hidden.astype(low)
-        grad_down_w = split(dot(grad_low, inner_low, (0, 0)))
-        grad_inner = dot(grad_low, w_down, (1, 0))
-        sigmoid_gate = jax.nn.sigmoid(gate)
-        grad_gate = (
-            grad_inner * up * sigmoid_gate * (1.0 + gate * (1.0 - sigmoid_gate))
-        ).astype(low)
-        grad_upper = (grad_inner * gate * sigmoid_gate).astype(low)
-        grad_gate_w = split(dot(normed_two, grad_gate, (0, 0)))
-        grad_up_w = split(dot(normed_two, grad_upper, (0, 0)))
-        part = (dot(grad_gate, w_gate, (1, 1)) + dot(grad_upper, w_up, (1, 1))).astype(low)
-        total, done[layer]["down"], done[layer]["gate"], *rest = move(
-            z_sums=[part], scatters=[grad_down_w, grad_gate_w] + [a for _, _, a in waiting]
+        grad_down_w, grad_gate_w, grad_up_w, part = backward_ffn(
+            grad_low, normed_two, gate, up, inner_low, w_gate, w_up, w_down
+        )
+        grad_down_w, grad_gate_w, grad_up_w = (
+            split(grad) for grad in (grad_down_w, grad_gate_w, grad_up_w)
+        )
+        waiting += [("gate", layer, grad_gate_w)]
+        if layer > 0:
+            waiting += [("down", layer, grad_down_w)]
+        total, *rest = move(
+            z_sums=[part],
+            scatters=[a for _, _, a in waiting],
+            plan=((4, 13), (5, 15)) if layer > 0 else ((3, 8), (4, 9), (5, 15)),
         )
         for (name, owner, _), result in zip(waiting, rest):
             done[owner][name] = result
@@ -859,12 +998,17 @@
         head_rows = grad_bias[:q_width].reshape(heads_here, HD)
         small_grads[layer] = [grad_gain_two, head_rows, kv_bias_grad.reshape(-1)]
         if layer > 0:
-            total, done[layer]["up"] = move(z_sums=[part], scatters=[grad_up_w])
+            total, done[layer]["up"] = move(
+                z_sums=[part], scatters=[grad_up_w], plan=((3, 10),)
+            )
             waiting = [("out", layer, grad_out_w), ("in", layer, grad_in_w)]
         else:
-            total, block_sum, done[layer]["up"], done[layer]["in"], done[layer]["out"] = move(
-                z_sums=[part, last_part], scatters=[grad_up_w, grad_in_w, grad_out_w]
+            total, block_sum, *rest = move(
+                z_sums=[part, last_part],
+                scatters=[grad_up_w, grad_down_w, grad_in_w, grad_out_w],
+                plan=((4, 10), (5, 12), (5, 13), (6, 14)),
             )
+            done[layer]["up"], done[layer]["down"], done[layer]["in"], done[layer]["out"] = rest
         back_one, grad_gain_one = norm_back(
             layer_input, scale_one, gains[layer, 0], total.astype(wide)
         )
@@ -898,6 +1042,15 @@
     )
 
     stack = lambda name, f=lambda a: a: jnp.stack([f(done[layer][name]) for layer in range(LAYERS)])
+    gate_up_grad = jnp.stack(
+        [
+            jnp.stack([done[layer]["gate"], done[layer]["up"]], axis=1)
+            for layer in range(LAYERS)
+        ]
+    )
+    gate_up_grad = lax.optimization_barrier(
+        with_layout_constraint(gate_up_grad, Layout((0, 1, 2, 3)))
+    )
     grads = (
         gains_grad,
         stack("in", lambda a: a[:, :q_width]),
@@ -905,7 +1058,7 @@
         kv_weight_grad,
         kv_bias_grad,
         stack("out", lambda a: a.T),
-        jnp.stack([stack("gate"), stack("up")], axis=2),
+        gate_up_grad,
         stack("down", lambda a: a.T),
     )
     params = (

time: 1390 us -> 985 us (0.71)
  Pallas kernels: 876 us -> 696 us
  matrix products: 206 us -> 62 us
  local copies, waits for them, and re-layouts: 166 us -> 61.9 us
  other arithmetic: 104 us -> 128 us
    pallas_call x13, Pallas kernels: 876 us -> 583 us  [transfer(): pl.pallas_call(functools.partial(transfer_kernel, sizes, counts, plan), o...]
    dot_general x30 -> x12, matrix products: 184 us -> 39.6 us  [dot(): lax.dot_general(lhs, rhs, ((over[0:1], over[1:2]), ((), ())), preferred_e...]
    pallas_call x0 -> x4, Pallas kernels: none -> 113 us  [the longest x2 70.6 us: backward_ffn(): pl.pallas_call(functools.partial(backward_tile, width), grid=(pl.cdiv(wid...]
    convert_element_type x6 -> x0, local copies, waits for them, and re-layouts: 61.5 us -> none  [split(): return gradient.astype(low).reshape(n, shard_rows, gradient.shape[1])]
    unnamed x252 -> x202, local copies, waits for them, and re-layouts: 62.5 us -> 15.6 us
    another operation x8 -> x9, other arithmetic: 19.1 us -> 33.5 us  [the longest x3 19.4 us: local(): jnp.stack([jnp.stack([done[layer]['gate'], done[layer]['up']], axis=1) fo...]
  transfers between devices with their start and end apart: 1 -> 1, of which waited for: 0 -> 0; matrix products, arithmetic and copies ran while one was open for 8% -> 9% of each run, Pallas kernels for 1% -> 1%
where the time goes in v2:
time: 985 us; the launch traced here: 975 us
  Pallas kernels  696 us (71%)
  other arithmetic  128 us (13%)
  matrix products  62 us (6%)
  local copies, waits for them, and re-layouts  61.9 us (6%)
  between operations  16.3 us (2%)
  blocking collectives  10.5 us (1%)
    pallas_call x13, Pallas kernels, transfer(): pl.pallas_call(functools.partial(transfer_kernel, sizes, counts, plan), o...  583 us
    pallas_call x2, Pallas kernels, backward_ffn(): pl.pallas_call(functools.partial(backward_tile, width), grid=(pl.cdiv(wid...  70.6 us
    pallas_call x2, Pallas kernels, forward_ffn(): pl.pallas_call(functools.partial(forward_tile, width), grid=(pl.cdiv(widt...  42.1 us
    sub x8, other arithmetic, adam_update(): weight - step_rate * (mean_hat / (jnp.sqrt(square_hat) + adam_eps) + deca...  41.4 us
    dot_general x12, matrix products, dot(): lax.dot_general(lhs, rhs, ((over[0:1], over[1:2]), ((), ())), preferred_e...  39.6 us
  transfers between devices with their start and end apart: 1, of which 0 were waited for; matrix products, arithmetic and copies ran while one was open for 9% of the time, Pallas kernels for 1%

profile of v2, /device:TPU:0, one launch (start us, length us, event | category | flops | bytes accessed | tf_op | source)
XLA Modules:
  0.0 974.9 jit_solution(11936471587902691709)
XLA Ops:
  14.2 21.8 %transfer1.1 = (bf16[8,16,256]{2,1,0:T(8,128)(2,1)}, bf16[8,192,1024]{2,1,0:T(8,128)(2,1)}) custom-call(bf16[16,256]{1,0:T(8,128)(2,1)} %pad.75.refs_0_, bf16[192,1024]{1,0:T(8,128)(2,1)} %get-tuple-element.338.refs_1_), custom_call_target="tpu_custom_call" | custom-call | tf_op jit(solution)/shard_map/transfer1/pallas_call | solution.py:514
  54.2 41.3 %transfer2.1 = (bf16[8,192,2240]{2,1,0:T(8,128)(2,1)}, bf16[2,512,256]{2,1,0:T(8,128)(2,1)}) custom-call(bf16[192,2240]{1,0:T(8,128)(2,1)} %get-tuple-element.283.refs_0_, bf16[512,256]{1,0:T(8,128)(2,1)} %pad_maximum_fusion.16.refs_1_), custom_call_target="tpu_custom_call" | custom-call | tf_op jit(solution)/shard_map/transfer2/pallas_call | solution.py:514
  106.3 5.9 fusion.138
  113.5 67.0 %transfer3.1 = (bf16[512,1536]{1,0:T(8,128)(2,1)}, bf16[8,192,2240]{2,1,0:T(8,128)(2,1)}, bf16[8,192,2240]{2,1,0:T(8,128)(2,1)}) custom-call(bf16[512,1536]{1,0:T(8,128)(2,1)} %convolution_convert_fusion.5.refs_0_, bf16[192,2240]{1,0:T(8,128)(2,1)} %get-tuple-element.345.refs_1_, bf16[192,2240]{1,0:T(8,128)(2,1)} %get-tuple-element.344.refs_2_), custom_call_target="tpu_custom_call" | custom-call | tf_op jit(solution)/shard_map/transfer3/pallas_call | solution.py:514
  184.4 21.1 %forward_ffn.2 = (f32[512,2240]{1,0:T(8,128)}, f32[512,2240]{1,0:T(8,128)}, bf16[512,2240]{1,0:T(8,128)(2,1)}, bf16[512,1536]{1,0:T(8,128)(2,1)}) custom-call(bf16[512,1536]{1,0:T(8,128)(2,1)} %multiply_convert_fusion.2.n2, bf16[1536,2240]{1,0:T(8,128)(2,1)} %bitcast.304, bf16[1536,2240]{1,0:T(8,128)(2,1)} %bitcast.306, bf16[1536,2240]{1,0:T(8,128)(2,1)} %bitcast.302), custom_call_target="tpu_custom_call" | custom-call | tf_op jit(solution)/shard_map/forward_ffn/pallas_call | solution.py:570
  205.5 52.3 %transfer4.1 = (bf16[512,1536]{1,0:T(8,128)(2,1)}, bf16[8,192,1024]{2,1,0:T(8,128)(2,1)}, bf16[8,192,2240]{2,1,0:T(8,128)(2,1)}) custom-call(bf16[512,1536]{1,0:T(8,128)(2,1)} %get-tuple-element.85.refs_0_, bf16[192,1024]{1,0:T(8,128)(2,1)} %get-tuple-element.339.refs_1_, bf16[192,2240]{1,0:T(8,128)(2,1)} %get-tuple-element.282.refs_2_), custom_call_target="tpu_custom_call" | custom-call | tf_op jit(solution)/shard_map/transfer4/pallas_call | solution.py:514
  261.7 3.9 fusion.65
  270.9 10.5 %transfer5.1 = bf16[2,512,256]{2,1,0:T(8,128)(2,1)} custom-call(bf16[512,256]{1,0:T(8,128)(2,1)} %pad_maximum_fusion.17.refs_0_), custom_call_target="tpu_custom_call" | custom-call | tf_op jit(solution)/shard_map/transfer5/pallas_call | solution.py:514
  291.7 65.1 %transfer6.1 = (bf16[512,1536]{1,0:T(8,128)(2,1)}, bf16[8,192,2240]{2,1,0:T(8,128)(2,1)}, bf16[8,192,2240]{2,1,0:T(8,128)(2,1)}) custom-call(bf16[512,1536]{1,0:T(8,128)(2,1)} %convolution_convert_fusion.4.refs_0_, bf16[192,2240]{1,0:T(8,128)(2,1)} %get-tuple-element.343.refs_1_, bf16[192,2240]{1,0:T(8,128)(2,1)} %get-tuple-element.342.refs_2_), custom_call_target="tpu_custom_call" | custom-call | tf_op jit(solution)/shard_map/transfer6/pallas_call | solution.py:514
  362.8 21.1 %forward_ffn.3 = (f32[512,2240]{1,0:T(8,128)}, f32[512,2240]{1,0:T(8,128)}, bf16[512,2240]{1,0:T(8,128)(2,1)}, bf16[512,1536]{1,0:T(8,128)(2,1)}) custom-call(bf16[512,1536]{1,0:T(8,128)(2,1)} %multiply_convert_fusion.n2, bf16[1536,2240]{1,0:T(8,128)(2,1)} %bitcast.310, bf16[1536,2240]{1,0:T(8,128)(2,1)} %bitcast.312, bf16[1536,2240]{1,0:T(8,128)(2,1)} %bitcast.308), custom_call_target="tpu_custom_call" | custom-call | tf_op jit(solution)/shard_map/forward_ffn/pallas_call | solution.py:570
  383.9 35.3 %backward_ffn.2 = (bf16[1536,2240]{1,0:T(8,128)(2,1)}, bf16[1536,2240]{1,0:T(8,128)(2,1)}, bf16[1536,2240]{1,0:T(8,128)(2,1)}, bf16[512,1536]{1,0:T(8,128)(2,1)}) custom-call(bf16[512,1536]{1,0:T(8,128)(2,1)} %bitcast.320, bf16[512,1536]{1,0:T(8,128)(2,1)} %multiply_convert_fusion.n2, f32[512,2240]{1,0:T(8,128)} %get-tuple-element.92.gate_in, ...), custom_call_target="tpu_custom_call" | custom-call | tf_op jit(solution)/shard_map/backward_ffn/pallas_call | solution.py:645
  419.2 77.5 %transfer7.1 = (bf16[512,1536]{1,0:T(8,128)(2,1)}, f32[192,2240]{1,0:T(8,128)}, f32[192,2240]{1,0:T(8,128)}) custom-call(bf16[512,1536]{1,0:T(8,128)(2,1)} %get-tuple-element.95.refs_0_, bf16[8,192,2240]{2,1,0:T(8,128)(2,1)} %bitcast.319, bf16[8,192,2240]{2,1,0:T(8,128)(2,1)} %bitcast.318), custom_call_target="tpu_custom_call" | custom-call | tf_op jit(solution)/shard_map/transfer7/pallas_call | solution.py:514
  496.8 4.1 fusion.36
  506.3 3.8 fusion.6
  510.2 6.4 fusion.41
  521.5 10.5 %transfer8.1 = bf16[2,512,256]{2,1,0:T(8,128)(2,1)} custom-call(bf16[2,512,256]{2,1,0:T(8,128)(2,1)} %pad_maximum_fusion.8.refs_0_), custom_call_target="tpu_custom_call" | custom-call | tf_op jit(solution)/shard_map/transfer8/pallas_call | solution.py:514
  537.9 4.6 convolution_convert_fusion.3.refs_0_
  545.3 49.8 %transfer9.1 = (bf16[512,1536]{1,0:T(8,128)(2,1)}, f32[192,2240]{1,0:T(8,128)}) custom-call(bf16[512,1536]{1,0:T(8,128)(2,1)} %convolution_convert_fusion.3.refs_0_, bf16[8,192,2240]{2,1,0:T(8,128)(2,1)} %bitcast.316), custom_call_target="tpu_custom_call" | custom-call | tf_op jit(solution)/shard_map/transfer9/pallas_call | solution.py:514
  600.3 35.3 %backward_ffn.3 = (bf16[1536,2240]{1,0:T(8,128)(2,1)}, bf16[1536,2240]{1,0:T(8,128)(2,1)}, bf16[1536,2240]{1,0:T(8,128)(2,1)}, bf16[512,1536]{1,0:T(8,128)(2,1)}) custom-call(bf16[512,1536]{1,0:T(8,128)(2,1)} %get-tuple-element.264.grad, bf16[512,1536]{1,0:T(8,128)(2,1)} %multiply_convert_fusion.2.n2, f32[512,2240]{1,0:T(8,128)} %get-tuple-element.101.gate_in, ...), custom_call_target="tpu_custom_call" | custom-call | tf_op jit(solution)/shard_map/backward_ffn/pallas_call | solution.py:645
  635.6 61.7 %transfer10.1 = (bf16[512,1536]{1,0:T(8,128)(2,1)}, f32[192,384]{1,0:T(8,128)}, f32[192,640]{1,0:T(8,128)}, f32[192,2240]{1,0:T(8,128)}) custom-call(bf16[512,1536]{1,0:T(8,128)(2,1)} %get-tuple-element.104.refs_0_, bf16[8,192,384]{2,1,0:T(8,128)(2,1)} %bitcast.321, bf16[8,192,640]{2,1,0:T(8,128)(2,1)} %bitcast.335, bf16[8,192,2240]{2,1,0:T(8,128)(2,1)} %bitcast.317), custom_call_target="tpu_custom_call" | custom-call | tf_op jit(solution)/shard_map/transfer10/pallas_call | solution.py:514
  701.2 3.8 convolution_convert_fusion.8
  708.8 6.4 fusion.42
  718.9 9.2 transfer11.1
  732.5 4.3 convolution_convert_fusion.2.refs_0_
  741.9 109.3 %transfer12.1 = (bf16[512,1536]{1,0:T(8,128)(2,1)}, bf16[512,1536]{1,0:T(8,128)(2,1)}, f32[192,2240]{1,0:T(8,128)}, f32[192,2240]{1,0:T(8,128)}, f32[192,640]{1,0:T(8,128)}, /*index=5*/f32[192,384]{1,0:T(8,128)}) custom-call(bf16[512,1536]{1,0:T(8,128)(2,1)} %convolution_convert_fusion.2.refs_0_, bf16[512,1536]{1,0:T(8,128)(2,1)} %get-tuple-element.107.refs_1_, ...), custom_call_target="tpu_custom_call" | custom-call | tf_op jit(solution)/shard_map/transfer12/pallas_call | solution.py:514
  872.8 7.5 transfer13.1
  881.0 10.5 %psum.15 = f32[2,64]{1,0:T(2,128)S(1)} all-reduce(f32[2,64]{1,0:T(2,128)S(1)} %bitcast.370), channel_id=1, replica_groups=mesh['dp'=4,'ctx'=2,'tensor'=4] {'tensor'}, use_global_device_ids=true, to_apply=%region_24.25 | all-reduce | flops 128 | bytes 1024 | tf_op jit(solution)/shard_map/psum | solution.py:1040
  898.2 5.0 maximum_bitcast_fusion.1
  903.2 5.0 maximum_bitcast_fusion
  908.5 9.3 pad_maximum_fusion
  919.3 27.0 %convert_subtract_fusion = (f32[2,192,2,2240]{3,2,1,0:T(2,128)}, f32[2,192,2,2240]{3,2,1,0:T(2,128)}, f32[2,192,2,2240]{3,2,1,0:T(2,128)}) fusion(bf16[2,192,2,2240]{3,2,1,0:T(2,128)(2,1)} %param.36, f32[2,192,2,2240]{3,2,1,0:T(2,128)} %pad_maximum_fusion, f32[2,192,2,2240]{3,2,1,0:T(2,128)} %param.52, f32[2,192,2,2240]{3,2,1,0:T(2,128)} %param.44), kind=kLoop, calls=%fused_computation.1 | loop fusion | flops 27525120 | bytes 44728320 | tf_op jit(solution)/shard_map/sub | solution.py:689
  951.8 6.5 convert_subtract_fusion.1
  (373 shorter events, 155.9 us)
Async XLA Ops:
  7.2 31.5 %copy-start.1 = (bf16[1,512,1536]{2,1,0:T(8,128)(2,1)S(1)}, bf16[1,512,1536]{2,1,0:T(8,128)(2,1)}, u32[]{:S(2)}) copy-start(bf16[1,512,1536]{2,1,0:T(8,128)(2,1)} %param.27) | copy-start | bytes 4718596
  7.2 956.0 %all-reduce.19.cloned.1.call-start = ((), (), s32[]{:S(2)}) async-start(), calls=%async_computation | async-start | bytes 1572864 | tf_op jit(solution)/shard_map/psum | solution.py:1040
  51.1 44.4 %copy-start.31 = (pred[512,1024]{0,1:T(8,128)(4,1)}, pred[512,1024]{0,1:T(8,128)(4,1)S(1)}, u32[]{:S(2)}) copy-start(pred[512,1024]{0,1:T(8,128)(4,1)S(1)} %fusion.54) | copy-start | bytes 1572868
  53.2 44.8 %copy-start.16 = (bf16[512,4,64]{2,0,1:T(8,128)(2,1)}, bf16[512,4,64]{2,0,1:T(8,128)(2,1)S(1)}, u32[]{:S(2)}) copy-start(bf16[512,4,64]{2,0,1:T(8,128)(2,1)S(1)} %get-tuple-element.280) | copy-start | bytes 786436
  53.2 44.8 %copy-start.18 = (bf16[512,4,64]{2,0,1:T(8,128)(2,1)}, bf16[512,4,64]{2,0,1:T(8,128)(2,1)S(1)}, u32[]{:S(2)}) copy-start(bf16[512,4,64]{2,0,1:T(8,128)(2,1)S(1)} %get-tuple-element.281) | copy-start | bytes 786436
  519.6 13.7 %copy-start.38 = (bf16[2,512,256]{2,1,0:T(8,128)(2,1)S(1)}, bf16[2,512,256]{2,1,0:T(8,128)(2,1)}, u32[]{:S(2)}) copy-start(bf16[2,512,256]{2,1,0:T(8,128)(2,1)} %transfer5.1) | copy-start | bytes 1572868
  520.6 12.8 %copy-start.14 = (bf16[3,512,1024]{1,2,0:T(8,128)(2,1)S(1)}, bf16[3,512,1024]{1,2,0:T(8,128)(2,1)}, u32[]{:S(2)}) copy-start(bf16[3,512,1024]{1,2,0:T(8,128)(2,1)} %copy-done.13) | copy-start | bytes 9437188
  635.6 61.7 %copy-start.12 = (bf16[512,1536]{1,0:T(8,128)(2,1)S(1)}, bf16[512,1536]{1,0:T(8,128)(2,1)}, u32[]{:S(2)}) copy-start(bf16[512,1536]{1,0:T(8,128)(2,1)} %get-tuple-element.81) | copy-start | bytes 4718596
  717.1 12.3 %copy-start.61 = (bf16[2,512,256]{2,1,0:T(8,128)(2,1)S(1)}, bf16[2,512,256]{2,1,0:T(8,128)(2,1)}, u32[]{:S(2)}) copy-start(bf16[2,512,256]{2,1,0:T(8,128)(2,1)} %get-tuple-element.80) | copy-start | bytes 1572868
  891.6 27.0 %copy-start.89 = (f32[2,64]{1,0:T(2,128)}, f32[2,64]{1,0:T(2,128)S(1)}, u32[]{:S(2)}) copy-start(f32[2,64]{1,0:T(2,128)S(1)} %psum.15) | copy-start | bytes 1540
  908.2 9.7 copy-start.84
  908.2 9.7 copy-start.87
  908.2 9.7 copy-start.88
  908.2 10.3 %copy-start.86 = (bf16[2,3,16]{2,0,1:T(2,128)(2,1)S(1)}, bf16[2,3,16]{2,0,1:T(2,128)(2,1)}, u32[]{:S(2)}) copy-start(bf16[2,3,16]{2,0,1:T(2,128)(2,1)} %param.32) | copy-start | bytes 580
  908.2 10.3 %copy-start.90 = (f32[2,3,16]{2,0,1:T(2,128)S(1)}, f32[2,3,16]{2,0,1:T(2,128)}, u32[]{:S(2)}) copy-start(f32[2,3,16]{2,0,1:T(2,128)} %param.48) | copy-start | bytes 1156
  908.5 10.0 %copy-start.91 = (f32[2,3,16]{2,0,1:T(2,128)S(1)}, f32[2,3,16]{2,0,1:T(2,128)}, u32[]{:S(2)}) copy-start(f32[2,3,16]{2,0,1:T(2,128)} %param.40) | copy-start | bytes 1156
  908.5 10.1 %copy-start.92 = (bf16[2,64]{1,0:T(2,128)(2,1)S(1)}, bf16[2,64]{1,0:T(2,128)(2,1)}, u32[]{:S(2)}) copy-start(bf16[2,64]{1,0:T(2,128)(2,1)} %param.34) | copy-start | bytes 772
  908.5 10.1 %copy-start.93 = (f32[2,64]{1,0:T(2,128)S(1)}, f32[2,64]{1,0:T(2,128)}, u32[]{:S(2)}) copy-start(f32[2,64]{1,0:T(2,128)} %param.50) | copy-start | bytes 1540
  908.5 10.1 %copy-start.94 = (f32[2,64]{1,0:T(2,128)S(1)}, f32[2,64]{1,0:T(2,128)}, u32[]{:S(2)}) copy-start(f32[2,64]{1,0:T(2,128)} %param.42) | copy-start | bytes 1540
  919.2 27.1 %copy-start.56 = (bf16[2,192,384]{2,1,0:T(8,128)(2,1)S(1)}, bf16[2,192,384]{2,1,0:T(8,128)(2,1)}, u32[]{:S(2)}) copy-start(bf16[2,192,384]{2,1,0:T(8,128)(2,1)} %param.31) | copy-start | bytes 884740
  919.2 27.1 %copy-start.58 = (f32[1,192,384]{2,1,0:T(8,128)S(1)}, f32[1,192,384]{2,1,0:T(8,128)}, u32[]{:S(2)}) copy-start(f32[1,192,384]{2,1,0:T(8,128)} %slice_bitcast_fusion.3) | copy-start | bytes 884740
  919.2 27.1 %copy-start.62 = (f32[2,192,384]{2,1,0:T(8,128)S(1)}, f32[2,192,384]{2,1,0:T(8,128)}, u32[]{:S(2)}) copy-start(f32[2,192,384]{2,1,0:T(8,128)} %param.47) | copy-start | bytes 1769476
  919.2 27.1 %copy-start.63 = (f32[2,192,384]{2,1,0:T(8,128)S(1)}, f32[2,192,384]{2,1,0:T(8,128)}, u32[]{:S(2)}) copy-start(f32[2,192,384]{2,1,0:T(8,128)} %param.39) | copy-start | bytes 1769476
  919.2 28.7 %copy-start.57 = (bf16[2,384,192]{1,2,0:T(8,128)(2,1)S(1)}, bf16[2,384,192]{1,2,0:T(8,128)(2,1)}, u32[]{:S(2)}) copy-start(bf16[2,384,192]{1,2,0:T(8,128)(2,1)} %param.35) | copy-start | bytes 884740
  919.2 28.7 %copy-start.64 = (f32[2,384,192]{1,2,0:T(8,128)S(1)}, f32[2,384,192]{1,2,0:T(8,128)}, u32[]{:S(2)}) copy-start(f32[2,384,192]{1,2,0:T(8,128)} %param.51) | copy-start | bytes 1769476
  919.2 28.7 %copy-start.65 = (f32[2,384,192]{1,2,0:T(8,128)S(1)}, f32[2,384,192]{1,2,0:T(8,128)}, u32[]{:S(2)}) copy-start(f32[2,384,192]{1,2,0:T(8,128)} %param.43) | copy-start | bytes 1769476
  919.2 28.7 %copy-start.71 = (f32[192,384]{1,0:T(8,128)S(1)}, f32[192,384]{1,0:T(8,128)}, u32[]{:S(2)}) copy-start(f32[192,384]{1,0:T(8,128)} %get-tuple-element.115) | copy-start | bytes 884740
  919.2 28.7 %copy-start.72 = (f32[192,384]{1,0:T(8,128)S(1)}, f32[192,384]{1,0:T(8,128)}, u32[]{:S(2)}) copy-start(f32[192,384]{1,0:T(8,128)} %get-tuple-element.114) | copy-start | bytes 884740
  919.2 30.2 %copy-start.47 = (f32[192,2240]{1,0:T(8,128)S(1)}, f32[192,2240]{1,0:T(8,128)}, u32[]{:S(2)}) copy-start(f32[192,2240]{1,0:T(8,128)} %get-tuple-element.121) | copy-start | bytes 5160964
  919.3 30.2 %copy-start.48 = (f32[192,2240]{1,0:T(8,128)S(1)}, f32[192,2240]{1,0:T(8,128)}, u32[]{:S(2)}) copy-start(f32[192,2240]{1,0:T(8,128)} %get-tuple-element.120) | copy-start | bytes 5160964
  951.8 8.8 copy-start.78
  951.8 8.8 copy-start.85
  (66 other events, 253.5 us)
Sparse Core Ops, SparseCore 0:
  854.3 42.2 all-reduce.18

commit v3 on v2

--- a/solution.py
+++ b/solution.py
@@ -404,25 +404,29 @@
     return [begin] + [step(turn) for turn in range(-NEAR_LEAD, Z_CHUNKS + NEAR_LAG)] + [end]
 
 
-def transfer_kernel(sizes, counts, plan, *refs):
-    z_count, g_count, s_count, p_count, w_count = counts
-    inputs = sum(counts)
-    ins, outs, rest = refs[:inputs], refs[inputs : 2 * inputs], list(refs[2 * inputs :])
-    place = Place(sizes)
-    sems = Sems(rest.pop(), rest.pop())
-
+class Work:
+    def __init__(self, body, inputs, outputs, scratch, sems, part, makes=()):
+        self.body, self.inputs, self.outputs = body, inputs, outputs
+        self.scratch, self.sems, self.part, self.makes = scratch, sems, part, makes
+
+
+def take(refs, count):
+    taken, refs[:count] = refs[:count], []
+    return taken
+
+
+def greet(place, plane, ctx, line):
     barrier = pltpu.get_barrier_semaphore()
     partners = []
-    arrived = 0
-    if g_count or s_count:
+    if plane:
         partners.append(place.to_core())
         partners += [place.to_x(place.x_at(step)) for step in range(1, place.xs)]
-    if g_count or s_count or p_count or w_count:
+    if ctx:
         partners += [place.to_ctx(place.ctx_at(step)) for step in range(1, place.ctxs)]
     for partner in partners:
         pl.semaphore_signal(barrier, inc=1, device_id=partner, device_id_type=MESH)
     arrived = len(partners)
-    if z_count:
+    if line:
         above = place.tensor < place.tensors - 1
         below = place.tensor > 0
 
@@ -441,15 +445,34 @@
         arrived = arrived + above.astype(jnp.int32) + below.astype(jnp.int32)
     pl.semaphore_wait(barrier, arrived)
 
-    ins, outs = list(ins), list(outs)
-    lines, planes, ends = [], [], []
-    for _ in range(z_count):
-        lines.append(line_steps(place, sems, ins.pop(0), outs.pop(0), rest.pop(0), rest.pop(0)))
+
+def transfer_kernel(sizes, counts, plan, work, *refs):
+    z_count, g_count, s_count, p_count, w_count = counts
+    refs = list(refs)
+    given = 0 if work else z_count
+    ins = take(refs, sum(counts) - z_count + given - (len(work.makes) if work else 0))
+    work_ins = take(refs, len(work.inputs)) if work else []
+    outs = take(refs, sum(counts))
+    work_outs = take(refs, len(work.outputs)) if work else []
+    sem_refs = refs[-2:]
+    rest = refs[:-2]
+    place = Place(sizes)
+    sems = Sems(*sem_refs)
+    plane = bool(g_count or s_count)
+    greet(place, plane, plane or p_count or w_count or work, z_count)
+
+    lines, planes = [], []
+    parts = take(rest, 1) if work else take(ins, z_count)
+    for part in parts:
+        lines.append(line_steps(place, sems, part, outs.pop(0), rest.pop(0), rest.pop(0)))
     for _ in range(g_count):
         planes.append(gather_steps(place, sems, ins.pop(0), outs.pop(0)))
-    for _ in range(s_count):
-        buffers = [rest.pop(0) for _ in range(5)]
-        planes.append(scatter_steps(place, sems, ins.pop(0), outs.pop(0), *buffers))
+    made = take(rest, len(work.makes)) if work else []
+    for index in range(s_count):
+        early = index < s_count - len(made)
+        source = ins.pop(0) if early else made[index - s_count]
+        planes.append(scatter_steps(place, sems, source, outs.pop(0), *take(rest, 5)))
+    late = len(planes) - len(made)
     small = []
     for index in range(p_count + w_count):
         src, dst = ins.pop(0), outs.pop(0)
@@ -462,29 +485,57 @@
         small.append(sems.local(block, dst.at[mine]))
     for copy in small:
         copy.start()
-    for plane in planes:
-        plane[0]()
+    body = iter(())
+    if work:
+        body = work.body(place, sems, work_ins, work_outs, rest, parts[0], *made)
+    next(body, None)
+    for steps in planes[:late]:
+        steps[0]()
+    next(body, None)
+    for steps, at in zip(planes, plan):
+        if at[0] < 0:
+            steps[1]()
+    next(body, None)
     turns = max([len(line) for line in lines], default=0)
     for turn in range(turns + 1):
-        for plane, at in zip(planes, plan):
+        if turn == 1 and made:
+            next(body, None)
+            for steps in planes[late:]:
+                steps[0]()
+        for steps, at in zip(planes, plan):
             for stage in (1, 2):
                 if min(at[stage - 1], turns) == turn:
-                    plane[stage]()
+                    steps[stage]()
         for line in lines:
             if turn < len(line):
                 line[turn]()
-    for plane in planes:
-        plane[3]()
+    for steps in planes:
+        steps[3]()
     for copy in small:
         copy.wait()
 
 
-def transfer(sizes, number, z_sums=(), gathers=(), scatters=(), pieces=(), swaps=(), plan=((99, 99),) * 8):
+def transfer(
+    sizes,
+    number,
+    z_sums=(),
+    gathers=(),
+    scatters=(),
+    pieces=(),
+    swaps=(),
+    plan=((99, 99),) * 8,
+    work=None,
+):
     n = sizes[0] * sizes[1]
     any_space = pl.BlockSpec(memory_space=pl.ANY)
     in_vmem = pl.BlockSpec(memory_space=pltpu.VMEM)
-    args = (*z_sums, *gathers, *scatters, *pieces, *swaps)
-    in_specs = [in_vmem] * len(z_sums) + [any_space] * (len(args) - len(z_sums))
+    given = () if work else z_sums
+    early = len(scatters)
+    if work:
+        z_sums = (work.part,)
+        scatters = (*scatters, *work.makes)
+    args = (*given, *gathers, *scatters[:early], *pieces, *swaps)
+    in_specs = [in_vmem] * len(given) + [any_space] * (len(args) - len(given))
     out_specs = (
         [in_vmem] * len(z_sums)
         + [any_space] * len(gathers)
@@ -499,8 +550,16 @@
         + [jax.ShapeDtypeStruct(a.shape, a.dtype) for a in swaps]
     )
     scratch = []
+    if work:
+        args += tuple(work.inputs)
+        in_specs += [in_vmem] * len(work.inputs)
+        out_specs += [in_vmem] * len(work.outputs)
+        out_shape += work.outputs
+        scratch.append(pltpu.VMEM(work.part.shape, work.part.dtype))
     for a in z_sums:
         scratch += [pltpu.VMEM(a.shape, a.dtype)] * 2
+    if work:
+        scratch += [pltpu.VMEM(a.shape, a.dtype) for a in work.makes]
     for a in scatters:
         scratch += scatter_buffers(sizes, a.shape, a.dtype)
     count = (
@@ -509,28 +568,305 @@
         + scatter_sems(sizes) * len(scatters)
         + sizes[1] * (len(pieces) + len(swaps))
     )
+    if work:
+        scratch += work.scratch
+        count += work.sems
     scratch += [pltpu.SemaphoreType.DMA((count,)), pltpu.SemaphoreType.DMA((count,))]
     counts = (len(z_sums), len(gathers), len(scatters), len(pieces), len(swaps))
     return pl.pallas_call(
-        functools.partial(transfer_kernel, sizes, counts, plan),
+        functools.partial(transfer_kernel, sizes, counts, plan, work),
         out_shape=out_shape,
         in_specs=in_specs,
         out_specs=out_specs,
         scratch_shapes=scratch,
         compiler_params=pltpu.CompilerParams(
-            collective_id=number, has_side_effects=True, vmem_limit_bytes=56 << 20
+            collective_id=number, has_side_effects=True, vmem_limit_bytes=62 << 20
+        ),
+        cost_estimate=pl.CostEstimate(
+            flops=30_000_000_000, bytes_accessed=150_000_000, transcendentals=0
         ),
         name="transfer%d" % number,
     )(*args)
 
 
-TILE = 256
-
-
 def mm(lhs, rhs, over):
     return lax.dot_general(
         lhs, rhs, (((over[0],), (over[1],)), ((), ())), preferred_element_type=jnp.float32
     )
+
+
+def turn_heads(values, cosine, sine):
+    return values * cosine + pltpu.roll(values, HD // 2, 1) * sine
+
+
+def allowed_pairs(place, query_segments, key_segments, local_len):
+    shape = (local_len, key_segments.shape[1])
+    query = place.ctx * local_len + lax.broadcasted_iota(jnp.int32, shape, 0)
+    key = lax.broadcasted_iota(jnp.int32, shape, 1)
+    return jnp.logical_and(query_segments == key_segments, key <= query)
+
+
+def sequence_pairs(pairs, sequence, local_len, column):
+    block = pairs[:, pl.ds(sequence * local_len, local_len), pl.ds(column * HD, HD)]
+    return block.reshape(-1, HD)
+
+
+def attend(seq_count, place, sems, ins, outs, scratch, part):
+    normed, w_attention, bias, cosine, sine, query_segments, key_segments = ins
+    queries, pairs, log_total, mixed = outs
+    rows = normed.shape[0]
+    local_len = rows // seq_count
+    q_width = queries.shape[1]
+    heads = q_width // HD
+    cos, sin = cosine[...], sine[...]
+    columns = pl.ds(q_width, 2 * HD)
+    lin = mm(normed[...], w_attention[:, columns], (1, 0)) + bias[:, columns]
+    me = place.ctx
+    pairs[me, :, :HD] = turn_heads(lin[:, :HD], cos, sin).astype(jnp.bfloat16)
+    pairs[me, :, HD:] = lin[:, HD:].astype(jnp.bfloat16)
+    sent = [
+        sems.remote(pairs.at[me], pairs.at[me], place.to_ctx(place.ctx_at(step)))
+        for step in range(1, place.ctxs)
+    ]
+    for copy in sent:
+        copy.start()
+    yield
+    yield
+    lin = mm(normed[...], w_attention[:, :q_width], (1, 0)) + bias[:, :q_width]
+    for index in range(heads):
+        columns = slice(index * HD, (index + 1) * HD)
+        queries[:, columns] = turn_heads(lin[:, columns], cos, sin).astype(jnp.bfloat16)
+    for copy in sent:
+        copy.wait()
+    for sequence in range(seq_count):
+        span = pl.ds(sequence * local_len, local_len)
+        allowed = allowed_pairs(
+            place, query_segments[span, :], key_segments[pl.ds(sequence, 1), :], local_len
+        )
+        keys = sequence_pairs(pairs, sequence, local_len, 0)
+        values = sequence_pairs(pairs, sequence, local_len, 1)
+        for index in range(heads):
+            columns = pl.ds(index * HD, HD)
+            scores = mm(queries[span, columns], keys, (1, 1)) * HD ** (-0.5)
+            scores = jnp.where(allowed, scores, MASK_FILL)
+            row_max = jnp.max(scores, axis=1, keepdims=True)
+            exp_scores = jnp.exp(scores - row_max)
+            row_total = jnp.sum(exp_scores, axis=1, keepdims=True)
+            weights = (exp_scores / row_total).astype(jnp.bfloat16)
+            log_total[span, pl.ds(index, 1)] = row_max + jnp.log(row_total)
+            mixed[span, columns] = mm(weights, values, (1, 0)).astype(jnp.bfloat16)
+    w_out = w_attention[:, q_width + 2 * HD :]
+    part[...] = mm(mixed[...], w_out, (1, 1)).astype(part.dtype)
+
+
+def attend_back(seq_count, place, sems, ins, outs, scratch, part, in_grad, out_grad):
+    grad, normed, w_attention, cosine, sine, query_segments, key_segments = ins[:7]
+    queries, pairs, log_total, mixed = ins[7:]
+    (lin_grad,) = outs
+    mixed_grad, pair_grad, got = scratch
+    rows = grad.shape[0]
+    local_len = rows // seq_count
+    q_width = queries.shape[1]
+    heads = q_width // HD
+    scale = HD ** (-0.5)
+    yield
+    cos, sin = cosine[...], -sine[...]
+    w_in = w_attention[:, : q_width + 2 * HD]
+    w_out = w_attention[:, q_width + 2 * HD :]
+    mixed_grad[...] = mm(grad[...], w_out, (1, 0)).astype(jnp.bfloat16)
+    totals = log_total[...].T
+    for sequence in range(seq_count):
+        first = sequence * local_len
+        span = pl.ds(first, local_len)
+        keys = sequence_pairs(pairs, sequence, local_len, 0)
+        values = sequence_pairs(pairs, sequence, local_len, 1)
+        shape = (keys.shape[0], local_len)
+        key = lax.broadcasted_iota(jnp.int32, shape, 0)
+        query = place.ctx * local_len + lax.broadcasted_iota(jnp.int32, shape, 1)
+        same = key_segments[:, pl.ds(sequence, 1)] == query_segments[:, span]
+        allowed = jnp.logical_and(same, key <= query)
+        key_grad = value_grad = None
+        for index in range(heads):
+            columns = pl.ds(index * HD, HD)
+            query_rows = queries[span, columns]
+            grad_rows = mixed_grad[span, columns]
+            scores = mm(keys, query_rows, (1, 1)) * scale
+            scores = jnp.where(allowed, scores, MASK_FILL)
+            weights = jnp.exp(scores - totals[index : index + 1, first : first + local_len])
+            weight_grads = mm(values, grad_rows, (1, 1))
+            row_delta = jnp.sum(weights * weight_grads, axis=0, keepdims=True)
+            score_grads = (weights * (weight_grads - row_delta)).astype(jnp.bfloat16)
+            for_keys = mm(score_grads, query_rows, (1, 0))
+            for_values = mm(weights.astype(jnp.bfloat16), grad_rows, (1, 0))
+            key_grad = for_keys if key_grad is None else key_grad + for_keys
+            value_grad = for_values if value_grad is None else value_grad + for_values
+            query_grad = mm(score_grads, keys, (0, 0)) * scale
+            lin_grad[span, columns] = turn_heads(
+                query_grad, cosine[span, :], -sine[span, :]
+            ).astype(jnp.bfloat16)
+        pieces = (place.ctxs, local_len, HD)
+        pair_grad[:, span, :HD] = (key_grad * scale).astype(jnp.bfloat16).reshape(pieces)
+        pair_grad[:, span, HD:] = value_grad.astype(jnp.bfloat16).reshape(pieces)
+    sent = []
+    for step in range(1, place.ctxs):
+        to = place.ctx_at(step)
+        sent.append(sems.remote(pair_grad.at[to], got.at[step - 1], place.to_ctx(to)))
+        sent[-1].start()
+    yield
+    total = pair_grad[place.ctx].astype(jnp.float32)
+    for step, copy in enumerate(sent):
+        copy.wait()
+        total = total + got[step].astype(jnp.float32)
+    lin_grad[:, pl.ds(q_width, HD)] = turn_heads(total[:, :HD], cos, sin).astype(jnp.bfloat16)
+    lin_grad[:, pl.ds(q_width + HD, HD)] = total[:, HD:].astype(jnp.bfloat16)
+    part[...] = mm(lin_grad[...], w_in, (1, 1)).astype(part.dtype)
+    yield
+    product = mm(normed[...], lin_grad[...], (0, 0)).astype(in_grad.dtype)
+    in_grad[...] = product.reshape(in_grad.shape)
+    product = mm(grad[...], mixed[...], (0, 0)).astype(out_grad.dtype)
+    out_grad[...] = product.reshape(out_grad.shape)
+
+
+def finish_kernel(sizes, *refs):
+    refs = list(refs)
+    gain_grads = take(refs, 2 * LAYERS)
+    lin_grads = take(refs, LAYERS)
+    in_grads = take(refs, LAYERS)
+    sums, kv_parts, kv_rows, rows, send, recv = refs
+    place = Place(sizes)
+    sems = Sems(send, recv)
+    shard_rows, width = in_grads[0].shape
+    q_width = width - 2 * HD
+    group = H // KV
+    heads = q_width // HD
+    dps, ctxs, tensors = sizes
+    at = lambda index, step, size: lax.rem(index + step, size)
+    line = [place.to_tensor(at(place.tensor, step, tensors)) for step in range(1, tensors)]
+    plane = [
+        {"dp": at(place.dp, step, dps), "ctx": at(place.ctx, turn, ctxs)}
+        for step in range(dps)
+        for turn in range(ctxs)
+        if step or turn
+    ]
+    barrier = pltpu.get_barrier_semaphore()
+    for device in line + plane:
+        pl.semaphore_signal(barrier, inc=1, device_id=device, device_id_type=MESH)
+
+    me = place.tensor
+    here = place.dp * ctxs + place.ctx
+    kv_rows[me] = jnp.zeros(kv_rows.shape[1:], jnp.float32)
+    rows[here] = jnp.zeros(rows.shape[1:], jnp.float32)
+    for layer in range(LAYERS):
+        span = pl.ds(layer * shard_rows, shard_rows)
+        kv_parts[me, span, :] = in_grads[layer][:, q_width:].astype(kv_parts.dtype)
+        bias = jnp.sum(lin_grads[layer][...].astype(jnp.float32), axis=0, keepdims=True)
+        kv_rows[me, pl.ds(layer, 1), :] = bias[:, q_width:]
+        rows[here, pl.ds(2 * LAYERS + layer, 1), pl.ds(0, q_width)] = bias[:, :q_width]
+    for index, gain in enumerate(gain_grads):
+        rows[here, pl.ds(index, 1), :] = gain[...]
+    pl.semaphore_wait(barrier, len(line) + len(plane))
+
+    big = [sems.remote(kv_parts.at[me], kv_parts.at[me], device) for device in line]
+    first = [sems.remote(kv_rows.at[me], kv_rows.at[me], device) for device in line]
+    for copy in first + big:
+        copy.start()
+    for copy in first:
+        copy.wait()
+    for head in range(KV):
+        owners = [t for t in range(tensors) if t * heads // group == head]
+        total = sum(kv_rows[t, pl.ds(0, LAYERS), :] for t in owners)
+        span = pl.ds(3 * LAYERS, LAYERS)
+        rows[here, span, pl.ds(head * HD, HD)] = total[:, :HD]
+        rows[here, span, pl.ds((KV + head) * HD, HD)] = total[:, HD:]
+    second = [sems.remote(rows.at[here], rows.at[here], device) for device in plane]
+    for copy in second:
+        copy.start()
+    for copy in second:
+        copy.wait()
+    total = rows[0]
+    for index in range(1, dps * ctxs):
+        total = total + rows[index]
+    sums[...] = total
+    for copy in big:
+        copy.wait()
+
+
+def finish(sizes, number, gain_grads, lin_grads, in_grads):
+    dps, ctxs, tensors = sizes
+    in_vmem = pl.BlockSpec(memory_space=pltpu.VMEM)
+    args = (*[gain[None] for gain in gain_grads], *lin_grads, *in_grads)
+    height, width = -(-4 * LAYERS // 8) * 8, gain_grads[0].shape[0]
+    count = 2 * (tensors - 1) + dps * ctxs - 1
+    return pl.pallas_call(
+        functools.partial(finish_kernel, sizes),
+        out_shape=[
+            jax.ShapeDtypeStruct((height, width), jnp.float32),
+            jax.ShapeDtypeStruct((tensors, LAYERS * in_grads[0].shape[0], 2 * HD), jnp.bfloat16),
+        ],
+        in_specs=[in_vmem] * len(args),
+        out_specs=[in_vmem] * 2,
+        scratch_shapes=[
+            pltpu.VMEM((tensors, 8, 2 * HD), jnp.float32),
+            pltpu.VMEM((dps * ctxs, height, width), jnp.float32),
+            pltpu.SemaphoreType.DMA((count,)),
+            pltpu.SemaphoreType.DMA((count,)),
+        ],
+        compiler_params=pltpu.CompilerParams(
+            collective_id=number, has_side_effects=True, vmem_limit_bytes=32 << 20
+        ),
+        name="finish",
+    )(*args)
+
+
+def adam_update(weight, gradient, first_old, second_old, decayed, step_rate):
+    first_new = beta_first * first_old + (1.0 - beta_first) * gradient
+    second_new = beta_second * second_old + (1.0 - beta_second) * gradient * gradient
+    mean_hat = first_new / (1.0 - beta_first**adam_step)
+    square_hat = second_new / (1.0 - beta_second**adam_step)
+    new_weight = weight - step_rate * (
+        mean_hat / (jnp.sqrt(square_hat) + adam_eps) + decayed * decay_rate * weight
+    )
+    return (first_new, second_new, new_weight)
+
+
+def pair_adam_block(step_rate, weight, first, second, *rest):
+    grads, outs = rest[: 2 * LAYERS], rest[2 * LAYERS :]
+    for layer in range(LAYERS):
+
+        @pl.when(pl.program_id(0) == layer)
+        def _():
+            gate, up = grads[2 * layer], grads[2 * layer + 1]
+            grad = jnp.stack([gate[...], up[...]], axis=1)[None]
+            moved = adam_update(
+                weight[...].astype(jnp.float32), grad, first[...], second[...], 1.0, step_rate
+            )
+            for out, value in zip(outs, (grad, *moved)):
+                out[...] = value
+
+
+def pair_adam(weight, first, second, grads, step_rate):
+    layers, rows, _, columns = weight.shape
+    size = rows // (4 if rows % 64 == 0 else 3)
+    last = rows // size - 1
+    block = pl.BlockSpec((1, size, 2, columns), lambda layer, i: (layer, i, 0, 0))
+
+    def grad_block(own):
+        at = lambda layer, i: (jnp.where(layer == own, i, jnp.where(layer < own, 0, last)), 0)
+        return pl.BlockSpec((size, columns), at)
+
+    return pl.pallas_call(
+        functools.partial(pair_adam_block, step_rate),
+        grid=(layers, rows // size),
+        in_specs=[block] * 3 + [grad_block(own) for own in range(layers) for _ in range(2)],
+        out_specs=[block] * 4,
+        out_shape=[jax.ShapeDtypeStruct(weight.shape, jnp.float32)] * 4,
+        compiler_params=pltpu.CompilerParams(vmem_limit_bytes=56 << 20),
+        name="pair_adam",
+    )(weight, first, second, *grads)
+
+
+TILE = 256
+DOWN_TILES = 4
 
 
 def in_width(block, width):
@@ -595,6 +931,7 @@
     w_up,
     w_down,
     down_out,
+    down_rest,
     gate_out,
     up_out,
     part_out,
@@ -612,7 +949,16 @@
     gate = gate_in[...]
     slope = jax.nn.sigmoid(gate)
     grad_inner = mm(grad[...], w_down[...], (1, 0))
-    down_out[...] = mm(grad_t[...], inner[...], (1, 0)).astype(down_out.dtype)
+    down_grad = mm(grad_t[...], inner[...], (1, 0)).astype(down_out.dtype)
+
+    @pl.when(tile < DOWN_TILES)
+    def _():
+        down_out[...] = down_grad
+
+    @pl.when(tile >= DOWN_TILES)
+    def _():
+        down_rest[...] = down_grad
+
     grad_gate = grad_inner * up_in[...] * slope * (1.0 + gate * (1.0 - slope))
     grad_gate = in_width(grad_gate, width).astype(jnp.bfloat16)
     grad_up = in_width(grad_inner * gate * slope, width).astype(jnp.bfloat16)
@@ -641,13 +987,22 @@
     whole = pl.BlockSpec((rows, model_width), lambda j: (0, 0))
     weight = pl.BlockSpec((model_width, TILE), lambda j: (0, j))
     units = pl.BlockSpec((rows, TILE), lambda j: (0, j))
-    like = jax.ShapeDtypeStruct((model_width, width), jnp.bfloat16)
+    like = lambda size: jax.ShapeDtypeStruct((model_width, size), jnp.bfloat16)
+    cut = DOWN_TILES * TILE
+    before = pl.BlockSpec((model_width, TILE), lambda j: (0, jnp.minimum(j, DOWN_TILES - 1)))
+    behind = pl.BlockSpec((model_width, TILE), lambda j: (0, jnp.maximum(j - DOWN_TILES, 0)))
     return pl.pallas_call(
         functools.partial(backward_tile, width),
         grid=(pl.cdiv(width, TILE),),
         in_specs=[whole, whole, units, units, units, weight, weight, weight],
-        out_specs=[weight, weight, weight, whole],
-        out_shape=[like, like, like, jax.ShapeDtypeStruct((rows, model_width), jnp.bfloat16)],
+        out_specs=[before, behind, weight, weight, whole],
+        out_shape=[
+            like(cut),
+            like(width - cut),
+            like(width),
+            like(width),
+            jax.ShapeDtypeStruct((rows, model_width), jnp.bfloat16),
+        ],
         scratch_shapes=[
             pltpu.VMEM((model_width, rows), jnp.bfloat16),
             pltpu.VMEM((model_width, rows), jnp.bfloat16),
@@ -679,29 +1034,6 @@
         norm_scale * weighted - values * (norm_scale * norm_scale * norm_scale) * inner_mean
     )
     return (grad_values, jnp.sum(grad_rows * values * norm_scale, axis=0))
-
-
-def adam_update(weight, gradient, first_old, second_old, decayed, step_rate):
-    first_new = beta_first * first_old + (1.0 - beta_first) * gradient
-    second_new = beta_second * second_old + (1.0 - beta_second) * gradient * gradient
-    mean_hat = first_new / (1.0 - beta_first**adam_step)
-    square_hat = second_new / (1.0 - beta_second**adam_step)
-    new_weight = weight - step_rate * (
-        mean_hat / (jnp.sqrt(square_hat) + adam_eps) + decayed * decay_rate * weight
-    )
-    return (first_new, second_new, new_weight)
-
-
-def dot(lhs, rhs, over):
-    return lax.dot_general(lhs, rhs, ((over[0:1], over[1:2]), ((), ())), preferred_element_type=jnp.float32)
-
-
-def masked_scores(queries, all_keys, allowed, score_scale):
-    scores = (
-        jnp.einsum("sqhd,skd->shqk", queries, all_keys, preferred_element_type=jnp.float32)
-        * score_scale
-    )
-    return jnp.where(allowed, scores, MASK_FILL)
 
 
 def local(
@@ -750,9 +1082,16 @@
         )
         for layer in range(LAYERS)
     ]
-    gate_shards = [gate_up_weight[layer, :, 0] for layer in range(LAYERS)]
-    up_shards = [gate_up_weight[layer, :, 1] for layer in range(LAYERS)]
     down_shards = [down_weight[layer].T for layer in range(LAYERS)]
+
+    def after(array, *earlier):
+        return lax.optimization_barrier((array, *earlier))[0]
+
+    def gather(shard):
+        return lax.all_gather(shard, ("dp", "ctx"), axis=0, tiled=True)
+
+    def scatter(gradient):
+        return lax.psum_scatter(gradient, ("dp", "ctx"), scatter_dimension=0, tiled=True)
 
     bias_part = kv_bias.shape[1]
     head_part = query_bias.shape[2]
@@ -772,6 +1111,9 @@
     )
 
     small, attention_weights = move(gathers=[small_shard, attention_shards[0]])
+    gate_up = after(gate_up_weight, small)
+    gate_shards = [after(gate_up[layer, :, 0]) for layer in range(LAYERS)]
+    up_shards = [after(gate_up[layer, :, 1]) for layer in range(LAYERS)]
     at = LAYERS * 2
     gains = (
         small[:, :at, :shard_rows]
@@ -805,55 +1147,46 @@
     angles = position[..., None] * frequency
     cosine = jnp.cos(angles).reshape(row_count, 1, HD // 2)
     sine = jnp.sin(angles).reshape(row_count, 1, HD // 2)
-    key_index = jnp.arange(seq_length, dtype=jnp.int32)
-    allowed = (own_segments[:, :, None] == segment_ids[:, None, :]) & (
-        key_index[None, None, :] <= token_index[None, :, None]
-    )
-    allowed = allowed[:, None]
-
+    cos_wide = jnp.concatenate([cosine[:, 0], cosine[:, 0]], axis=1)
+    sin_wide = jnp.concatenate([-sine[:, 0], sine[:, 0]], axis=1)
     hidden = hidden_in.astype(wide).reshape(row_count, model_width)
     stored = []
-    gate_weights = up_weights = down_weights = None
     for layer in range(LAYERS):
         w_attention = attention_weights.reshape(model_width, q_width + 2 * HD + q_width)
-        w_in = w_attention[:, : q_width + 2 * HD]
-        w_out = w_attention[:, q_width + 2 * HD :]
         scale_one = lax.rsqrt(jnp.mean(hidden * hidden, axis=-1, keepdims=True) + NORM_EPS)
         normed = (hidden * scale_one * gains[layer, 0]).astype(low)
-        lin = dot(normed, w_in, (1, 0)) + jnp.concatenate([q_biases[layer], kv_biases[layer]])
-        lin_heads = lin[:, : q_width + HD].reshape(row_count, heads_here + 1, HD)
-        turned = rotate(lin_heads, cosine, sine).astype(low)
-        queries = turned[:, :heads_here].reshape(seq_count, local_len, heads_here, HD)
-        pair = jnp.concatenate([turned[:, heads_here], lin[:, q_width + HD :].astype(low)], axis=1)
+        work = Work(
+            functools.partial(attend, seq_count),
+            [
+                normed,
+                w_attention,
+                jnp.concatenate([q_biases[layer], kv_biases[layer]])[None],
+                cos_wide,
+                sin_wide,
+                own_segments.reshape(row_count, 1),
+                segment_ids,
+            ],
+            [
+                jax.ShapeDtypeStruct((row_count, q_width), low),
+                jax.ShapeDtypeStruct((ctxs, row_count, 2 * HD), low),
+                jax.ShapeDtypeStruct((row_count, HD), wide),
+                jax.ShapeDtypeStruct((row_count, q_width), low),
+            ],
+            [],
+            ctxs,
+            jax.ShapeDtypeStruct((row_count, model_width), low),
+        )
+        mine = [gate_shards[layer], up_shards[layer]]
         if layer == 0:
-            down_weights, pairs = move(gathers=[down_shards[0]], pieces=[pair])
-        else:
-            (pairs,) = move(pieces=[pair])
-        pairs = (
-            pairs.reshape(ctxs, seq_count, local_len, 2 * HD)
-            .transpose(1, 0, 2, 3)
-            .reshape(seq_count, seq_length, 2 * HD)
+            mine.append(down_shards[layer])
+        total, *moved, queries, pairs, log_total, mixed_low = move(
+            work=work, gathers=mine, plan=((8, 14), (12, 18), (14, 99))
         )
-        all_keys, all_values = pairs[..., :HD], pairs[..., HD:]
-        scores = masked_scores(queries, all_keys, allowed, score_scale)
-        row_max = jnp.max(scores, axis=-1, keepdims=True)
-        exp_scores = jnp.exp(scores - row_max)
-        row_total = jnp.sum(exp_scores, axis=-1, keepdims=True)
-        weights = exp_scores / row_total
-        log_total = row_max + jnp.log(row_total)
-        mixture = jnp.einsum(
-            "shqk,skd->sqhd", weights.astype(low), all_values, preferred_element_type=wide
-        )
-        mixed_low = mixture.reshape(row_count, q_width).astype(low)
-        part = dot(mixed_low, w_out, (1, 1)).astype(low)
-        total, gate_weights, up_weights = move(
-            z_sums=[part],
-            gathers=[gate_shards[layer], up_shards[layer]],
-            plan=((15, 99), (16, 99)),
-        )
-        w_gate = gate_weights.reshape(model_width, hidden_units)
-        w_up = up_weights.reshape(model_width, hidden_units)
-        w_down = down_weights.reshape(model_width, hidden_units)
+        if layer == 0:
+            down_weights = moved.pop()
+        w_gate, w_up, w_down = [
+            a.reshape(model_width, hidden_units) for a in (*moved, down_weights)
+        ]
         middle = hidden + total.astype(wide)
         scale_two = lax.rsqrt(jnp.mean(middle * middle, axis=-1, keepdims=True) + NORM_EPS)
         normed_two = (middle * scale_two * gains[layer, 1]).astype(low)
@@ -864,8 +1197,7 @@
                 scale_one,
                 normed,
                 queries,
-                all_keys,
-                all_values,
+                pairs,
                 log_total,
                 mixed_low,
                 middle,
@@ -874,8 +1206,7 @@
                 gate,
                 up,
                 inner_low,
-                w_in,
-                w_out,
+                w_attention,
                 w_gate,
                 w_up,
                 w_down,
@@ -885,7 +1216,7 @@
             total, attention_weights, down_weights = move(
                 z_sums=[part],
                 gathers=[attention_shards[layer + 1], down_shards[layer + 1]],
-                plan=((7, 17), (12, 18)),
+                plan=((8, 15), (13, 18)),
             )
             hidden = middle + total.astype(wide)
         else:
@@ -894,21 +1225,16 @@
     def split(gradient):
         return gradient.astype(low).reshape(n, shard_rows, gradient.shape[1])
 
-    def by_owner(row, width):
-        return jnp.pad(row.reshape(n, 1, width), ((0, 0), (0, 0), (0, small_width - width)))
-
     grad_hidden = out_grad.astype(wide).reshape(row_count, model_width)
     done = [{} for _ in range(LAYERS)]
     small_grads = [None] * LAYERS
-    waiting = []
     for layer in reversed(range(LAYERS)):
         (
             layer_input,
             scale_one,
             normed,
             queries,
-            all_keys,
-            all_values,
+            pairs,
             log_total,
             mixed_low,
             middle,
@@ -917,150 +1243,102 @@
             gate,
             up,
             inner_low,
-            w_in,
-            w_out,
+            w_attention,
             w_gate,
             w_up,
             w_down,
         ) = stored[layer]
         grad_low = grad_hidden.astype(low)
-        grad_down_w, grad_gate_w, grad_up_w, part = backward_ffn(
+        *ffn_grads, part = backward_ffn(
             grad_low, normed_two, gate, up, inner_low, w_gate, w_up, w_down
         )
-        grad_down_w, grad_gate_w, grad_up_w = (
-            split(grad) for grad in (grad_down_w, grad_gate_w, grad_up_w)
+        down_first, down_rest, grad_gate_w, grad_up_w = (split(grad) for grad in ffn_grads)
+        total, done[layer]["gate"], done[layer]["down_first"] = move(
+            z_sums=[part], scatters=[grad_gate_w, down_first], plan=((2, 9), (3, 11))
         )
-        waiting += [("gate", layer, grad_gate_w)]
-        if layer > 0:
-            waiting += [("down", layer, grad_down_w)]
-        total, *rest = move(
-            z_sums=[part],
-            scatters=[a for _, _, a in waiting],
-            plan=((4, 13), (5, 15)) if layer > 0 else ((3, 8), (4, 9), (5, 15)),
-        )
-        for (name, owner, _), result in zip(waiting, rest):
-            done[owner][name] = result
         back_two, grad_gain_two = norm_back(middle, scale_two, gains[layer, 1], total.astype(wide))
         grad_middle = grad_hidden + back_two
         grad_mid_low = grad_middle.astype(low)
-        grad_out_w = split(dot(grad_mid_low, mixed_low, (0, 0)))
-        grad_mixed = (
-            dot(grad_mid_low, w_out, (1, 0))
-            .astype(low)
-            .reshape(seq_count, local_len, heads_here, HD)
+        work = Work(
+            functools.partial(attend_back, seq_count),
+            [
+                grad_mid_low,
+                normed,
+                w_attention,
+                cos_wide,
+                sin_wide,
+                own_segments.reshape(1, row_count),
+                segment_ids.T,
+                queries,
+                pairs,
+                log_total,
+                mixed_low,
+            ],
+            [jax.ShapeDtypeStruct((row_count, q_width + 2 * HD), low)],
+            [
+                pltpu.VMEM((row_count, q_width), low),
+                pltpu.VMEM((ctxs, row_count, 2 * HD), low),
+                pltpu.VMEM((max(1, ctxs - 1), row_count, 2 * HD), low),
+            ],
+            ctxs,
+            jax.ShapeDtypeStruct((row_count, model_width), low),
+            [
+                jax.ShapeDtypeStruct((n, shard_rows, q_width + 2 * HD), low),
+                jax.ShapeDtypeStruct((n, shard_rows, q_width), low),
+            ],
         )
-        scores = masked_scores(queries, all_keys, allowed, score_scale)
-        probabilities = jnp.exp(scores - log_total)
-        grad_probs = jnp.einsum(
-            "sqhd,skd->shqk", grad_mixed, all_values, preferred_element_type=wide
+        total, *results, grad_lin = move(
+            work=work,
+            scatters=[grad_up_w, down_rest],
+            plan=((-1, 4), (-1, 6), (5, 9), (5, 10)),
         )
-        row_delta = jnp.sum(probabilities * grad_probs, axis=-1, keepdims=True)
-        grad_scores = (probabilities * (grad_probs - row_delta)).astype(low)
-        grad_queries = (
-            jnp.einsum("shqk,skd->sqhd", grad_scores, all_keys, preferred_element_type=wide)
-            * score_scale
-        )
-        grad_keys = (
-            jnp.einsum("shqk,sqhd->skd", grad_scores, queries, preferred_element_type=wide)
-            * score_scale
-        )
-        grad_values = jnp.einsum(
-            "shqk,sqhd->skd", probabilities.astype(low), grad_mixed, preferred_element_type=wide
-        )
-        grad_pair = jnp.concatenate([grad_keys, grad_values], axis=2).astype(low)
-        grad_pair = (
-            grad_pair.reshape(seq_count, ctxs, local_len, 2 * HD)
-            .transpose(1, 0, 2, 3)
-            .reshape(ctxs, row_count, 2 * HD)
-        )
-        (grad_pair,) = move(swaps=[grad_pair])
-        grad_pair = jnp.sum(grad_pair.astype(wide), axis=0)
-        grad_heads = jnp.concatenate(
-            [grad_queries.reshape(row_count, heads_here, HD), grad_pair[:, None, :HD]], axis=1
-        )
-        grad_lin = jnp.concatenate(
-            [
-                rotate_back(grad_heads, cosine, sine).reshape(row_count, q_width + HD),
-                grad_pair[:, HD:],
-            ],
-            axis=1,
-        ).astype(low)
-        grad_in_w = split(dot(normed, grad_lin, (0, 0)))
-        grad_bias = jnp.sum(grad_lin.astype(wide), axis=0)
-        part = dot(grad_lin, w_in, (1, 1)).astype(low)
-        zeros = jnp.zeros((2 * KV, HD), wide)
-        kv_bias_grad = lax.dynamic_update_slice_in_dim(
-            zeros, grad_bias[q_width : q_width + HD][None], kv_head, 0
-        )
-        kv_bias_grad = lax.dynamic_update_slice_in_dim(
-            kv_bias_grad, grad_bias[q_width + HD :][None], KV + kv_head, 0
-        )
-        head_rows = grad_bias[:q_width].reshape(heads_here, HD)
-        small_grads[layer] = [grad_gain_two, head_rows, kv_bias_grad.reshape(-1)]
-        if layer > 0:
-            total, done[layer]["up"] = move(
-                z_sums=[part], scatters=[grad_up_w], plan=((3, 10),)
-            )
-            waiting = [("out", layer, grad_out_w), ("in", layer, grad_in_w)]
-        else:
-            total, block_sum, *rest = move(
-                z_sums=[part, last_part],
-                scatters=[grad_up_w, grad_down_w, grad_in_w, grad_out_w],
-                plan=((4, 10), (5, 12), (5, 13), (6, 14)),
-            )
-            done[layer]["up"], done[layer]["down"], done[layer]["in"], done[layer]["out"] = rest
+        for name, result in zip(("up", "down_rest", "in", "out"), results):
+            done[layer][name] = result
+        done[layer]["lin"] = grad_lin
         back_one, grad_gain_one = norm_back(
             layer_input, scale_one, gains[layer, 0], total.astype(wide)
         )
-        small_grads[layer].insert(0, grad_gain_one)
+        small_grads[layer] = [grad_gain_one, grad_gain_two]
         grad_hidden = grad_middle + back_one
 
-    block_out = (stored[-1][8] + block_sum.astype(wide)).astype(low)
+    last_total = lax.psum(after(last_part, grad_hidden), "tensor")
+    block_out = (stored[-1][7] + last_total.astype(wide)).astype(low)
     block_out = block_out.reshape(seq_count, local_len, model_width)
     input_grad = grad_hidden.reshape(seq_count, local_len, model_width)
 
-    small_part = []
-    for layer in range(LAYERS):
-        gain_one, gain_two, head_rows, kv_row = small_grads[layer]
-        small_part += [by_owner(gain_one, shard_rows), by_owner(gain_two, shard_rows)]
-        small_part += [by_owner(head_rows[head], head_part) for head in range(heads_here)]
-        small_part.append(by_owner(kv_row, bias_part))
-    small_part = jnp.pad(
-        jnp.concatenate(small_part, axis=1), ((0, 0), (0, -small_rows % ROW_TILE), (0, 0))
-    ).astype(low)
-    (small_sum,) = move(scatters=[small_part])
-    small_sum = small_sum[:small_rows].reshape(LAYERS, 2 + heads_here + 1, small_width)
-    gains_grad = small_sum[:, :2, :shard_rows]
-    query_bias_grad = small_sum[:, 2 : 2 + heads_here, :head_part]
-
-    kv_part = jnp.stack([done[layer]["in"][:, q_width:] for layer in range(LAYERS)])
-    kv_full = jnp.zeros((LAYERS, shard_rows, 2 * KV * HD), wide)
-    kv_full = lax.dynamic_update_slice_in_dim(kv_full, kv_part[..., :HD], kv_head * HD, 2)
-    kv_full = lax.dynamic_update_slice_in_dim(kv_full, kv_part[..., HD:], (KV + kv_head) * HD, 2)
-    kv_weight_grad, kv_bias_grad = lax.psum(
-        (kv_full, small_sum[:, 2 + heads_here, :bias_part]), "tensor"
-    )
+    sums, kv_parts = finish(
+        sizes,
+        next(numbers),
+        [gain for layer in range(LAYERS) for gain in small_grads[layer]],
+        [done[layer]["lin"] for layer in range(LAYERS)],
+        [done[layer]["in"] for layer in range(LAYERS)],
+    )
+    shard = lax.axis_index("dp") * ctxs + lax.axis_index("ctx")
+    cut = lambda a, size: lax.dynamic_slice_in_dim(a, shard * size, size, a.ndim - 1)
+    gains_grad = cut(sums[: 2 * LAYERS], shard_rows).reshape(LAYERS, 2, shard_rows)
+    q_rows = sums[2 * LAYERS : 3 * LAYERS, :q_width].reshape(LAYERS, heads_here, HD)
+    query_bias_grad = cut(q_rows, head_part)
+    kv_bias_grad = cut(sums[3 * LAYERS : 4 * LAYERS, : 2 * KV * HD], bias_part)
+    kv_heads = []
+    for head in range(KV):
+        owners = [t for t in range(tensors) if t * heads_here // (H // KV) == head]
+        kv_heads.append(sum(kv_parts[t].astype(wide) for t in owners))
+    kv_weight_grad = jnp.concatenate(
+        [a[:, :HD] for a in kv_heads] + [a[:, HD:] for a in kv_heads], axis=1
+    ).reshape(LAYERS, shard_rows, 2 * KV * HD)
 
     stack = lambda name, f=lambda a: a: jnp.stack([f(done[layer][name]) for layer in range(LAYERS)])
-    gate_up_grad = jnp.stack(
-        [
-            jnp.stack([done[layer]["gate"], done[layer]["up"]], axis=1)
-            for layer in range(LAYERS)
-        ]
-    )
-    gate_up_grad = lax.optimization_barrier(
-        with_layout_constraint(gate_up_grad, Layout((0, 1, 2, 3)))
-    )
-    grads = (
+    down_grad = jnp.concatenate([stack("down_first"), stack("down_rest")], axis=2)
+    grads = [
         gains_grad,
         stack("in", lambda a: a[:, :q_width]),
         query_bias_grad,
         kv_weight_grad,
         kv_bias_grad,
         stack("out", lambda a: a.T),
-        gate_up_grad,
-        stack("down", lambda a: a.T),
-    )
+        None,
+        down_grad.transpose(0, 2, 1),
+    ]
     params = (
         norm_gains,
         query_weight,
@@ -1074,12 +1352,16 @@
     firsts, seconds = moments[:8], moments[8:]
     decays = (0.0, 1.0, 0.0, 1.0, 0.0, 1.0, 1.0, 1.0)
     rates = (0.5, 0.02, 0.5, 0.02, 0.5, 0.1, 0.02, 0.02)
-    moved = [
-        adam_update(
-            params[i].astype(wide), grads[i], firsts[i], seconds[i], decays[i], rates[i]
-        )
-        for i in range(8)
-    ]
+    moved = []
+    for i in range(8):
+        if grads[i] is None:
+            pair = [done[layer][name] for layer in range(LAYERS) for name in ("gate", "up")]
+            grads[i], *new = pair_adam(params[i], firsts[i], seconds[i], pair, rates[i])
+        else:
+            new = adam_update(
+                params[i].astype(wide), grads[i], firsts[i], seconds[i], decays[i], rates[i]
+            )
+        moved.append(new)
     return (
         block_out,
         input_grad,

time: 985 us -> 827 us (0.84)
  matrix products: 62 us -> 0 us
  other arithmetic: 128 us -> 72.7 us
  local copies, waits for them, and re-layouts: 61.9 us -> 22.9 us
  blocking collectives: 10.5 us -> 0 us
    dot_general x24 -> x0, matrix products: 62 us -> none  [the longest x12 39.6 us: dot(): lax.dot_general(lhs, rhs, ((over[0:1], over[1:2]), ((), ())), preferred_e...]
    another operation x9 -> x0, other arithmetic: 33.5 us -> none  [the longest x3 19.4 us: local(): jnp.stack([jnp.stack([done[layer]['gate'], done[layer]['up']], axis=1) fo...]
    sub x8 -> x7, other arithmetic: 41.4 us -> 15 us  [adam_update(): weight - step_rate * (mean_hat / (jnp.sqrt(square_hat) + adam_eps) + deca...]
    slice x19 -> x6, local copies, waits for them, and re-layouts: 12.2 us -> 0.13 us  [the longest x1 0.06 us: local(): normed = (hidden * scale_one * gains[layer, 0]).astype(low)]
    convert_element_type x0 -> x4, other arithmetic: none -> 11.3 us  [the longest x2 8.3 us: local(): grad_mid_low = grad_middle.astype(low)]
    psum x1 -> x0, blocking collectives: 10.5 us -> none  [local(): lax.psum((kv_full, small_sum[:, 2 + heads_here, :bias_part]), 'tensor')]
    pallas_call x13 -> x10, Pallas kernels: 583 us -> 579 us  [the longest x8 526 us: transfer(): pl.pallas_call(functools.partial(transfer_kernel, sizes, counts, plan, wo...]
  transfers between devices with their start and end apart: 1 -> 1, of which waited for: 0 -> 1; matrix products, arithmetic and copies ran while one was open for 9% -> 2% of each run, Pallas kernels for 1% -> 7%
where the time goes in v3:
time: 827 us; the launch traced here: 815 us
  Pallas kernels  698 us (84%)
  other arithmetic  72.7 us (9%)
  local copies, waits for them, and re-layouts  22.9 us (3%)
  between operations  15.2 us (2%)
    pallas_call x8, Pallas kernels, transfer(): pl.pallas_call(functools.partial(transfer_kernel, sizes, counts, plan, wo...  526 us
    pallas_call x2, Pallas kernels, backward_ffn(): pl.pallas_call(functools.partial(backward_tile, width), grid=(pl.cdiv(wid...  76.1 us
    pallas_call x2, Pallas kernels, forward_ffn(): pl.pallas_call(functools.partial(forward_tile, width), grid=(pl.cdiv(widt...  42.2 us
    pallas_call x1, Pallas kernels, finish(): pl.pallas_call(functools.partial(finish_kernel, sizes), out_shape=[jax.Sh...  28.7 us
    pallas_call x1, Pallas kernels, pair_adam(): pl.pallas_call(functools.partial(pair_adam_block, step_rate), grid=(layer...  24.7 us
  transfers between devices with their start and end apart: 1, of which 1 were waited for; matrix products, arithmetic and copies ran while one was open for 2% of the time, Pallas kernels for 7%

profile of v3, /device:TPU:0, one launch (start us, length us, event | category | flops | bytes accessed | tf_op | source)
XLA Modules:
  0.0 815.5 jit_solution(1173498393637750613)
XLA Ops:
  14.1 21.8 %transfer1.1 = (bf16[8,16,256]{2,1,0:T(8,128)(2,1)}, bf16[8,192,1024]{2,1,0:T(8,128)(2,1)}) custom-call(bf16[16,256]{1,0:T(8,128)(2,1)} %pad.19.refs_0_, bf16[192,1024]{1,0:T(8,128)(2,1)} %get-tuple-element.311.refs_1_), custom_call_target="tpu_custom_call" | custom-call | flops 30000001024 | bytes 150000000 | tf_op jit(solution)/shard_map/transfer1/pallas_call | solution.py:576
  38.4 2.3 copy.88
  40.8 1.8 slice_bitcast_fusion
  51.3 102.9 %transfer2.1 = (bf16[512,1536]{1,0:T(8,128)(2,1)}, bf16[8,192,2240]{2,1,0:T(8,128)(2,1)}, bf16[8,192,2240]{2,1,0:T(8,128)(2,1)}, bf16[8,192,2240]{2,1,0:T(8,128)...) custom-call(bf16[192,2240]{1,0:T(8,128)(2,1)} %get-tuple-element.275, ...), custom_call_target="tpu_custom_call" | custom-call | flops 30000001024 | bytes 150000000 | tf_op jit(solution)/shard_map/transfer2/pallas_call | solution.py:576
  154.3 2.1 multiply_reduce_fusion.2
  157.0 1.7 multiply_convert_fusion.2.n2
  158.7 21.1 %forward_ffn.2 = (f32[512,2240]{1,0:T(8,128)}, f32[512,2240]{1,0:T(8,128)}, bf16[512,2240]{1,0:T(8,128)(2,1)}, bf16[512,1536]{1,0:T(8,128)(2,1)}) custom-call(bf16[512,1536]{1,0:T(8,128)(2,1)} %multiply_convert_fusion.2.n2, bf16[1536,2240]{1,0:T(8,128)(2,1)} %bitcast.121, bf16[1536,2240]{1,0:T(8,128)(2,1)} %bitcast.123, bf16[1536,2240]{1,0:T(8,128)(2,1)} %bitcast.125), custom_call_target="tpu_custom_call" | custom-call | tf_op jit(solution)/shard_map/forward_ffn/pallas_call | solution.py:906
  179.8 53.1 %transfer3.1 = (bf16[512,1536]{1,0:T(8,128)(2,1)}, bf16[8,192,1024]{2,1,0:T(8,128)(2,1)}, bf16[8,192,2240]{2,1,0:T(8,128)(2,1)}) custom-call(bf16[512,1536]{1,0:T(8,128)(2,1)} %get-tuple-element.105.refs_0_, bf16[192,1024]{1,0:T(8,128)(2,1)} %get-tuple-element.312.refs_1_, bf16[192,2240]{1,0:T(8,128)(2,1)} %get-tuple-element.276.refs_2_), custom_call_target="tpu_custom_call" | custom-call | flops 30000001024 | bytes 150000000 | tf_op jit(solution)/shard_map/transfer3/pallas_call | solution.py:576
  232.9 3.1 multiply_reduce_fusion.1
  239.2 74.2 %transfer4.1 = (bf16[512,1536]{1,0:T(8,128)(2,1)}, bf16[8,192,2240]{2,1,0:T(8,128)(2,1)}, bf16[8,192,2240]{2,1,0:T(8,128)(2,1)}, bf16[512,384]{1,0:T(8,128)(2,1)...) custom-call(bf16[192,2240]{1,0:T(8,128)(2,1)} %get-tuple-element.273.refs_0_, ...), custom_call_target="tpu_custom_call" | custom-call | flops 30000001024 | bytes 150000000 | tf_op jit(solution)/shard_map/transfer4/pallas_call | solution.py:576
  313.4 3.0 multiply_reduce_fusion
  318.8 21.1 %forward_ffn.3 = (f32[512,2240]{1,0:T(8,128)}, f32[512,2240]{1,0:T(8,128)}, bf16[512,2240]{1,0:T(8,128)(2,1)}, bf16[512,1536]{1,0:T(8,128)(2,1)}) custom-call(bf16[512,1536]{1,0:T(8,128)(2,1)} %multiply_convert_fusion.n2, bf16[1536,2240]{1,0:T(8,128)(2,1)} %bitcast.129, bf16[1536,2240]{1,0:T(8,128)(2,1)} %bitcast.131, bf16[1536,2240]{1,0:T(8,128)(2,1)} %bitcast.127), custom_call_target="tpu_custom_call" | custom-call | tf_op jit(solution)/shard_map/forward_ffn/pallas_call | solution.py:906
  339.9 38.0 %backward_ffn.2 = (bf16[1536,1024]{1,0:T(8,128)(2,1)}, bf16[1536,1216]{1,0:T(8,128)(2,1)}, bf16[1536,2240]{1,0:T(8,128)(2,1)}, bf16[1536,2240]{1,0:T(8,128)(2,1)}, bf16[512,1536]{1,0:T(8,128)(2,1)}) custom-call(bf16[512,1536]{1,0:T(8,128)(2,1)} %bitcast.133, bf16[512,1536]{1,0:T(8,128)(2,1)} %multiply_convert_fusion.n2, ...), custom_call_target="tpu_custom_call" | custom-call | tf_op jit(solution)/shard_map/backward_ffn/pallas_call | solution.py:994
  378.0 58.1 %transfer5.1 = (bf16[512,1536]{1,0:T(8,128)(2,1)}, f32[192,2240]{1,0:T(8,128)}, f32[192,1024]{1,0:T(8,128)}) custom-call(bf16[512,1536]{1,0:T(8,128)(2,1)} %get-tuple-element.116.refs_0_, bf16[8,192,2240]{2,1,0:T(8,128)(2,1)} %bitcast.153, bf16[8,192,1024]{2,1,0:T(8,128)(2,1)} %bitcast.157), custom_call_target="tpu_custom_call" | custom-call | flops 30000001024 | bytes 150000000 | tf_op jit(solution)/shard_map/transfer5/pallas_call | solution.py:576
  436.1 4.1 fusion.22
  441.2 4.6 fusion.61.refs_2_
  445.8 79.2 %transfer6.1 = (bf16[512,1536]{1,0:T(8,128)(2,1)}, f32[192,2240]{1,0:T(8,128)}, f32[192,1216]{1,0:T(8,128)}, f32[192,640]{1,0:T(8,128)}, f32[192,384]{1,0:T(8,128)}, /*index=5*/bf16[512,640]{1,0:T(8,128)(2,1)}) custom-call(bf16[8,192,2240]{2,1,0:T(8,128)(2,1)} %bitcast.151, bf16[8,192,1216]{2,1,0:T(8,128)(2,1)} %bitcast.155, ...), custom_call_target="tpu_custom_call" | custom-call | flops 30000001024 | bytes 150000000 | tf_op jit(solution)/shard_map/transfer6/pallas_call | solution.py:576
  525.1 3.5 fusion.24
  528.8 5.0 fusion.71
  533.8 38.0 %backward_ffn.3 = (bf16[1536,1024]{1,0:T(8,128)(2,1)}, bf16[1536,1216]{1,0:T(8,128)(2,1)}, bf16[1536,2240]{1,0:T(8,128)(2,1)}, bf16[1536,2240]{1,0:T(8,128)(2,1)}, bf16[512,1536]{1,0:T(8,128)(2,1)}) custom-call(bf16[512,1536]{1,0:T(8,128)(2,1)} %get-tuple-element.268.grad, bf16[512,1536]{1,0:T(8,128)(2,1)} %multiply_convert_fusion.2.n2, ...), custom_call_target="tpu_custom_call" | custom-call | tf_op jit(solution)/shard_map/backward_ffn/pallas_call | solution.py:994
  571.9 57.6 %transfer7.1 = (bf16[512,1536]{1,0:T(8,128)(2,1)}, f32[192,2240]{1,0:T(8,128)}, f32[192,1024]{1,0:T(8,128)}) custom-call(bf16[512,1536]{1,0:T(8,128)(2,1)} %get-tuple-element.130.refs_0_, bf16[8,192,2240]{2,1,0:T(8,128)(2,1)} %bitcast.152, bf16[8,192,1024]{2,1,0:T(8,128)(2,1)} %bitcast.156), custom_call_target="tpu_custom_call" | custom-call | flops 30000001024 | bytes 150000000 | tf_op jit(solution)/shard_map/transfer7/pallas_call | solution.py:576
  629.6 3.2 fusion.26
  632.8 3.7 fusion.62.refs_2_
  636.6 79.0 %transfer8.1 = (bf16[512,1536]{1,0:T(8,128)(2,1)}, f32[192,2240]{1,0:T(8,128)}, f32[192,1216]{1,0:T(8,128)}, f32[192,640]{1,0:T(8,128)}, f32[192,384]{1,0:T(8,128)}, /*index=5*/bf16[512,640]{1,0:T(8,128)(2,1)}) custom-call(bf16[8,192,2240]{2,1,0:T(8,128)(2,1)} %bitcast.150, bf16[8,192,1216]{2,1,0:T(8,128)(2,1)} %bitcast.154, ...), custom_call_target="tpu_custom_call" | custom-call | flops 30000001024 | bytes 150000000 | tf_op jit(solution)/shard_map/transfer8/pallas_call | solution.py:576
  715.6 2.8 fusion.33
  718.4 5.2 fusion.11
  725.2 28.7 %finish.1 = (f32[8,1536]{1,0:T(8,128)S(1)}, bf16[4,384,256]{2,1,0:T(8,128)(2,1)S(1)}) custom-call(f32[1,1536]{1,0:T(1,128)S(1)} %broadcast_in_dim.14.refs_0_, f32[1,1536]{1,0:T(1,128)S(1)} %broadcast_in_dim.15.refs_1_, f32[1,1536]{1,0:T(1,128)S(1)} %broadcast_in_dim.16.refs_2_, f32[1,1536]{1,0:T(1,128)S(1)} %broadcast_in_dim.17.refs_3_, ...), custom_call_target="tpu_custom_call" | custom-call | tf_op jit(solution)/shard_map/finish/pallas_call | solution.py:800
  755.3 1.8 convert_subtract_fusion.1
  764.2 24.7 %pair_adam.1 = (f32[2,192,2,2240]{3,2,1,0:T(2,128)}, f32[2,192,2,2240]{3,2,1,0:T(2,128)}, f32[2,192,2,2240]{3,2,1,0:T(2,128)}, f32[2,192,2,2240]{3,2,1,0:T(2,128)}) custom-call(bf16[2,192,2,2240]{3,2,1,0:T(2,128)(2,1)} %weight.1, f32[2,192,2,2240]{3,2,1,0:T(2,128)} %first.1, f32[2,192,2,2240]{3,2,1,0:T(2,128)} %second.1, ...), custom_call_target="tpu_custom_call" | custom-call | tf_op jit(solution)/shard_map/pair_adam/pallas_call | solution.py:857
  789.0 8.7 %convert_subtract_fusion = (f32[2,2240,192]{1,2,0:T(8,128)}, f32[2,2240,192]{1,2,0:T(8,128)}, f32[2,2240,192]{1,2,0:T(8,128)}, f32[2,2240,192]{1,2,0:T(8,128)}) fusion(bf16[2,2240,192]{1,2,0:T(8,128)(2,1)S(1)} %copy-done.20, f32[2,2240,192]{1,2,0:T(8,128)} %param.53, f32[2,2240,192]{1,2,0:T(8,128)} %param.45, f32[1,192,1216]{2,1,0:T(8,128)S(1)} %bitcast.137, ...), kind=kLoop, calls=%fused_computation.7 | loop fusion | flops 16343040 | bytes 25804800 | tf_op jit(solution)/shard_map/sub | solution.py:826
  797.8 7.1 all-reduce.6.cloned.1.call-done
  804.8 3.6 fusion.34
  (204 shorter events, 35.3 us)
Async XLA Ops:
  7.2 797.6 %all-reduce.6.cloned.1.call-start = ((), (), s32[]{:S(2)}) async-start(), calls=%async_computation | async-start | bytes 3145728 | tf_op jit(solution)/shard_map/psum | solution.py:1304
  14.1 24.1 %copy-start.44 = (s32[1,1024]{1,0:T(1,128)S(1)}, s32[1,1024]{1,0:T(1,128)}, u32[]{:S(2)}) copy-start(s32[1,1024]{1,0:T(1,128)} %refs_8_.1) | copy-start | bytes 12292
  38.2 8.3 %copy-start.51 = (s32[1,512]{1,0:T(1,128)}, s32[1,512]{1,0:T(1,128)S(1)}, u32[]{:S(2)}) copy-start(s32[1,512]{1,0:T(1,128)S(1)} %constant_dynamic-slice_fusion.3.refs_7_) | copy-start | bytes 6148
  38.4 9.4 %copy-start.40 = (f32[1536]{0:T(1024)}, f32[1536]{0:T(1024)S(1)}, u32[]{:S(2)}) copy-start(f32[1536]{0:T(1024)S(1)} %get-tuple-element.241) | copy-start | bytes 18436
  38.4 118.6 %copy-start.38 = (f32[1536]{0:T(1024)}, f32[1536]{0:T(1024)S(1)}, u32[]{:S(2)}) copy-start(f32[1536]{0:T(1024)S(1)} %get-tuple-element.240) | copy-start | bytes 18436
  45.7 108.6 %copy-start.46 = (f32[512]{0:T(512)}, f32[512]{0:T(512)S(1)}, u32[]{:S(2)}) copy-start(f32[512]{0:T(512)S(1)} %get-tuple-element.300) | copy-start | bytes 6148
  157.0 22.8 %copy-start.42 = (f32[512]{0:T(512)}, f32[512]{0:T(512)S(1)}, u32[]{:S(2)}) copy-start(f32[512]{0:T(512)S(1)} %get-tuple-element.302) | copy-start | bytes 6148
  313.4 3.3 copy-start.5
  313.4 3.8 copy-start.14
  436.1 4.1 copy-start.45
  436.1 5.1 copy-start.6
  445.8 82.7 %copy-start.17 = (bf16[1,512,1536]{2,1,0:T(8,128)(2,1)S(1)}, bf16[1,512,1536]{2,1,0:T(8,128)(2,1)}, u32[]{:S(2)}) copy-start(bf16[1,512,1536]{2,1,0:T(8,128)(2,1)} %param.29) | copy-start | bytes 4718596
  525.1 3.5 copy-start.7
  525.1 3.8 copy-start.15
  571.8 57.7 %copy-start.10 = (bf16[1,512,1536]{2,1,0:T(8,128)(2,1)S(1)}, bf16[1,512,1536]{2,1,0:T(8,128)(2,1)}, u32[]{:S(2)}) copy-start(bf16[1,512,1536]{2,1,0:T(8,128)(2,1)} %param.27) | copy-start | bytes 4718596
  571.8 57.7 %copy-start.39 = (f32[1536]{0:T(1024)S(1)}, f32[1536]{0:T(1024)}, u32[]{:S(2)}) copy-start(f32[1536]{0:T(1024)} %copy-done.38) | copy-start | bytes 18436
  571.9 57.7 %copy-start.43 = (f32[512]{0:T(512)S(1)}, f32[512]{0:T(512)}, u32[]{:S(2)}) copy-start(f32[512]{0:T(512)} %copy-done.42) | copy-start | bytes 6148
  629.5 3.3 copy-start.16
  636.6 79.0 %copy-start.41 = (f32[1536]{0:T(1024)S(1)}, f32[1536]{0:T(1024)}, u32[]{:S(2)}) copy-start(f32[1536]{0:T(1024)} %copy-done.40) | copy-start | bytes 18436
  636.6 79.0 %copy-start.47 = (f32[512]{0:T(512)S(1)}, f32[512]{0:T(512)}, u32[]{:S(2)}) copy-start(f32[512]{0:T(512)} %copy-done.46) | copy-start | bytes 6148
  718.4 5.3 copy-start
  718.4 6.0 copy-start.1
  724.4 29.8 %copy-start.52 = (bf16[2,2,192]{2,1,0:T(2,128)(2,1)S(1)}, bf16[2,2,192]{2,1,0:T(2,128)(2,1)}, u32[]{:S(2)}) copy-start(bf16[2,2,192]{2,1,0:T(2,128)(2,1)} %param.30) | copy-start | bytes 4612
  724.4 29.8 %copy-start.54 = (f32[2,2,192]{2,1,0:T(2,128)S(1)}, f32[2,2,192]{2,1,0:T(2,128)}, u32[]{:S(2)}) copy-start(f32[2,2,192]{2,1,0:T(2,128)} %param.46) | copy-start | bytes 9220
  724.4 29.8 %copy-start.55 = (f32[2,2,192]{2,1,0:T(2,128)S(1)}, f32[2,2,192]{2,1,0:T(2,128)}, u32[]{:S(2)}) copy-start(f32[2,2,192]{2,1,0:T(2,128)} %param.38) | copy-start | bytes 9220
  725.2 29.8 %copy-start.22 = (bf16[2,192,512]{2,1,0:T(8,128)(2,1)S(1)}, bf16[2,192,512]{2,1,0:T(8,128)(2,1)}, u32[]{:S(2)}) copy-start(bf16[2,192,512]{2,1,0:T(8,128)(2,1)} %param.33) | copy-start | bytes 1179652
  755.0 3.9 copy-start.21
  764.2 24.8 %copy-start.20 = (bf16[2,2240,192]{1,2,0:T(8,128)(2,1)S(1)}, bf16[2,2240,192]{1,2,0:T(8,128)(2,1)}, u32[]{:S(2)}) copy-start(bf16[2,2240,192]{1,2,0:T(8,128)(2,1)} %param.37) | copy-start | bytes 5160964
  764.2 24.8 %copy-start.27 = (f32[192,1216]{1,0:T(8,128)S(1)}, f32[192,1216]{1,0:T(8,128)}, u32[]{:S(2)}) copy-start(f32[192,1216]{1,0:T(8,128)} %get-tuple-element.158) | copy-start | bytes 2801668
  764.2 24.8 %copy-start.28 = (f32[192,1216]{1,0:T(8,128)S(1)}, f32[192,1216]{1,0:T(8,128)}, u32[]{:S(2)}) copy-start(f32[192,1216]{1,0:T(8,128)} %get-tuple-element.157) | copy-start | bytes 2801668
  764.2 24.8 %copy-start.29 = (f32[192,1024]{1,0:T(8,128)S(1)}, f32[192,1024]{1,0:T(8,128)}, u32[]{:S(2)}) copy-start(f32[192,1024]{1,0:T(8,128)} %get-tuple-element.156) | copy-start | bytes 2359300
  789.0 15.8 %copy-start.8 = (f32[512,1536]{1,0:T(8,128)S(1)}, f32[512,1536]{1,0:T(8,128)}, u32[]{:S(2)}) copy-start(f32[512,1536]{1,0:T(8,128)} %copy-done.4) | copy-start | bytes 9437188
  (30 other events, 66.2 us)
Sparse Core Ops, SparseCore 0:
  723.8 80.9 all-reduce.5

commit v4 on v3

--- a/solution.py
+++ b/solution.py
@@ -58,6 +58,20 @@
 
     def to_tensor(self, tensor):
         return {"tensor": tensor}
+
+    def plane_partners(self):
+        return [
+            {"dp": lax.rem(self.dp + step, self.dps), "ctx": self.ctx_at(turn)}
+            for step in range(self.dps)
+            for turn in range(self.ctxs)
+            if step or turn
+        ]
+
+    def line_partners(self):
+        return [
+            self.to_tensor(lax.rem(self.tensor + step, self.tensors))
+            for step in range(1, self.tensors)
+        ]
 
 
 class Sems:
@@ -405,9 +419,12 @@
 
 
 class Work:
-    def __init__(self, body, inputs, outputs, scratch, sems, part, makes=()):
+    def __init__(
+        self, body, inputs, outputs, scratch, sems, part, makes=(), shards=(), whole_plane=False
+    ):
         self.body, self.inputs, self.outputs = body, inputs, outputs
         self.scratch, self.sems, self.part, self.makes = scratch, sems, part, makes
+        self.shards, self.whole_plane = shards, whole_plane
 
 
 def take(refs, count):
@@ -415,18 +432,23 @@
     return taken
 
 
-def greet(place, plane, ctx, line):
+def greet(place, plane, ctx, line, whole_plane=False, whole_line=False):
     barrier = pltpu.get_barrier_semaphore()
     partners = []
-    if plane:
-        partners.append(place.to_core())
-        partners += [place.to_x(place.x_at(step)) for step in range(1, place.xs)]
-    if ctx:
-        partners += [place.to_ctx(place.ctx_at(step)) for step in range(1, place.ctxs)]
+    if whole_plane:
+        partners += place.plane_partners()
+    else:
+        if plane:
+            partners.append(place.to_core())
+            partners += [place.to_x(place.x_at(step)) for step in range(1, place.xs)]
+        if ctx:
+            partners += [place.to_ctx(place.ctx_at(step)) for step in range(1, place.ctxs)]
+    if whole_line:
+        partners += place.line_partners()
     for partner in partners:
         pl.semaphore_signal(barrier, inc=1, device_id=partner, device_id_type=MESH)
     arrived = len(partners)
-    if line:
+    if line and not whole_line:
         above = place.tensor < place.tensors - 1
         below = place.tensor > 0
 
@@ -447,10 +469,11 @@
 
 
 def transfer_kernel(sizes, counts, plan, work, *refs):
-    z_count, g_count, s_count, p_count, w_count = counts
+    z_count, g_count, s_count, p_count = counts
     refs = list(refs)
     given = 0 if work else z_count
-    ins = take(refs, sum(counts) - z_count + given - (len(work.makes) if work else 0))
+    own = len(work.makes) + len(work.shards) if work else 0
+    ins = take(refs, sum(counts) - z_count + given - own)
     work_ins = take(refs, len(work.inputs)) if work else []
     outs = take(refs, sum(counts))
     work_outs = take(refs, len(work.outputs)) if work else []
@@ -459,52 +482,53 @@
     place = Place(sizes)
     sems = Sems(*sem_refs)
     plane = bool(g_count or s_count)
-    greet(place, plane, plane or p_count or w_count or work, z_count)
+    whole_plane = bool(work) and work.whole_plane
+    greet(place, plane, plane or work, z_count, whole_plane, p_count)
 
     lines, planes = [], []
     parts = take(rest, 1) if work else take(ins, z_count)
     for part in parts:
         lines.append(line_steps(place, sems, part, outs.pop(0), rest.pop(0), rest.pop(0)))
-    for _ in range(g_count):
-        planes.append(gather_steps(place, sems, ins.pop(0), outs.pop(0)))
+    shards = take(rest, len(work.shards)) if work else []
     made = take(rest, len(work.makes)) if work else []
+    for index in range(g_count):
+        shard = shards[index] if index < len(shards) else ins.pop(0)
+        planes.append(gather_steps(place, sems, shard, outs.pop(0)))
     for index in range(s_count):
         early = index < s_count - len(made)
         source = ins.pop(0) if early else made[index - s_count]
         planes.append(scatter_steps(place, sems, source, outs.pop(0), *take(rest, 5)))
     late = len(planes) - len(made)
     small = []
-    for index in range(p_count + w_count):
+    for _ in range(p_count):
         src, dst = ins.pop(0), outs.pop(0)
-        mine = place.ctx
-        for step in range(1, place.ctxs):
-            to = place.ctx_at(step)
-            block = src if index < p_count else src.at[to]
-            small.append(sems.remote(block, dst.at[mine], place.to_ctx(to)))
-        block = src if index < p_count else src.at[mine]
-        small.append(sems.local(block, dst.at[mine]))
+        small.append(sems.local(src, dst.at[place.tensor]))
+        for partner in place.line_partners():
+            small.append(sems.remote(src, dst.at[place.tensor], partner))
     for copy in small:
         copy.start()
-    body = iter(())
+    body, asked = iter(()), set()
     if work:
-        body = work.body(place, sems, work_ins, work_outs, rest, parts[0], *made)
-    next(body, None)
-    for steps in planes[:late]:
-        steps[0]()
-    next(body, None)
-    for steps, at in zip(planes, plan):
-        if at[0] < 0:
-            steps[1]()
-    next(body, None)
-    turns = max([len(line) for line in lines], default=0)
+        body = work.body(place, sems, work_ins, work_outs, rest, parts[0], *shards, *made)
+    for request in body:
+        if request is None:
+            break
+        for which, stage in request:
+            asked.add((which, stage))
+            planes[which][stage]()
+    for which in range(late):
+        if (which, 0) not in asked:
+            planes[which][0]()
+    turns, working = max([len(line) for line in lines], default=0), bool(work)
     for turn in range(turns + 1):
-        if turn == 1 and made:
-            next(body, None)
-            for steps in planes[late:]:
-                steps[0]()
-        for steps, at in zip(planes, plan):
+        if turn > 0 and working:
+            working = next(body, "done") is None
+            if not working:
+                for steps in planes[late:]:
+                    steps[0]()
+        for which, (steps, at) in enumerate(zip(planes, plan)):
             for stage in (1, 2):
-                if min(at[stage - 1], turns) == turn:
+                if min(at[stage - 1], turns) == turn and (which, stage) not in asked:
                     steps[stage]()
         for line in lines:
             if turn < len(line):
@@ -521,8 +545,7 @@
     z_sums=(),
     gathers=(),
     scatters=(),
-    pieces=(),
-    swaps=(),
+    line_pieces=(),
     plan=((99, 99),) * 8,
     work=None,
 ):
@@ -530,24 +553,24 @@
     any_space = pl.BlockSpec(memory_space=pl.ANY)
     in_vmem = pl.BlockSpec(memory_space=pltpu.VMEM)
     given = () if work else z_sums
-    early = len(scatters)
+    early, given_shards = len(scatters), gathers
     if work:
         z_sums = (work.part,)
+        gathers = (*work.shards, *gathers)
         scatters = (*scatters, *work.makes)
-    args = (*given, *gathers, *scatters[:early], *pieces, *swaps)
+    args = (*given, *given_shards, *scatters[:early], *line_pieces)
     in_specs = [in_vmem] * len(given) + [any_space] * (len(args) - len(given))
     out_specs = (
         [in_vmem] * len(z_sums)
         + [any_space] * len(gathers)
         + [in_vmem] * len(scatters)
-        + [any_space] * (len(pieces) + len(swaps))
+        + [any_space] * len(line_pieces)
     )
     out_shape = (
         [jax.ShapeDtypeStruct(a.shape, a.dtype) for a in z_sums]
         + [jax.ShapeDtypeStruct((n, *a.shape), a.dtype) for a in gathers]
         + [jax.ShapeDtypeStruct(a.shape[1:], jnp.float32) for a in scatters]
-        + [jax.ShapeDtypeStruct((sizes[1], *a.shape), a.dtype) for a in pieces]
-        + [jax.ShapeDtypeStruct(a.shape, a.dtype) for a in swaps]
+        + [jax.ShapeDtypeStruct((sizes[2], *a.shape), a.dtype) for a in line_pieces]
     )
     scratch = []
     if work:
@@ -559,20 +582,20 @@
     for a in z_sums:
         scratch += [pltpu.VMEM(a.shape, a.dtype)] * 2
     if work:
-        scratch += [pltpu.VMEM(a.shape, a.dtype) for a in work.makes]
+        scratch += [pltpu.VMEM(a.shape, a.dtype) for a in (*work.shards, *work.makes)]
     for a in scatters:
         scratch += scatter_buffers(sizes, a.shape, a.dtype)
     count = (
         4 * Z_CHUNKS * len(z_sums)
         + gather_sems(sizes) * len(gathers)
         + scatter_sems(sizes) * len(scatters)
-        + sizes[1] * (len(pieces) + len(swaps))
+        + sizes[2] * len(line_pieces)
     )
     if work:
         scratch += work.scratch
         count += work.sems
     scratch += [pltpu.SemaphoreType.DMA((count,)), pltpu.SemaphoreType.DMA((count,))]
-    counts = (len(z_sums), len(gathers), len(scatters), len(pieces), len(swaps))
+    counts = (len(z_sums), len(gathers), len(scatters), len(line_pieces))
     return pl.pallas_call(
         functools.partial(transfer_kernel, sizes, counts, plan, work),
         out_shape=out_shape,
@@ -589,6 +612,9 @@
     )(*args)
 
 
+LATE_PIECES = 1
+
+
 def mm(lhs, rhs, over):
     return lax.dot_general(
         lhs, rhs, (((over[0],), (over[1],)), ((), ())), preferred_element_type=jnp.float32
@@ -611,28 +637,100 @@
     return block.reshape(-1, HD)
 
 
-def attend(seq_count, place, sems, ins, outs, scratch, part):
-    normed, w_attention, bias, cosine, sine, query_segments, key_segments = ins
-    queries, pairs, log_total, mixed = outs
+def normalize(rows, block, read, gain, write):
+    @pl.loop(0, rows // block)
+    def _(index):
+        span = pl.ds(pl.multiple_of(index * block, block), block)
+        values = read(span)
+        scale = lax.rsqrt(jnp.mean(values * values, axis=1, keepdims=True) + NORM_EPS)
+        write(span, (values * scale * gain).astype(jnp.bfloat16))
+
+
+def attention_shard(layer, kv_head, query_weight, kv_weight, out_weight, shard):
+    q_width = query_weight.shape[2]
+    shard[:, pl.ds(0, q_width)] = query_weight[layer]
+    for index, head in enumerate((kv_head, KV + kv_head)):
+        columns = pl.ds(pl.multiple_of(head * HD, HD), HD)
+        shard[:, pl.ds(q_width + index * HD, HD)] = kv_weight[layer, :, columns]
+    shard[:, pl.ds(q_width + 2 * HD, q_width)] = out_weight[layer]
+
+
+def split_pair(layer, weight, gate, up):
+    @pl.loop(0, weight.shape[1] // ROW_TILE)
+    def _(index):
+        span = pl.ds(pl.multiple_of(index * ROW_TILE, ROW_TILE), ROW_TILE)
+        both = weight[layer, span, :, :].astype(jnp.float32)
+        gate[span, :] = both[:, 0, :].astype(gate.dtype)
+        up[span, :] = both[:, 1, :].astype(up.dtype)
+
+
+def attend(layer, seq_count, place, sems, ins, outs, scratch, part, *shards):
+    if layer == 0:
+        x_in, own_table, cosine, sine, query_segments, key_segments = ins[:6]
+        query_weight, kv_weight, out_weight, gate_up_weight = ins[6:]
+        queries, pairs, log_total, mixed, normed, w_attention, table = outs[:7]
+        next_shards = outs[7:]
+        tables, shard = scratch
+        first_head = place.tensor * query_weight.shape[2] // HD // (H // KV)
+        attention_shard(0, first_head, query_weight, kv_weight, out_weight, shard)
+        here = place.shard(place.x, place.core, place.ctx)
+        sent = [
+            sems.remote(own_table, tables.at[here], partner) for partner in place.plane_partners()
+        ]
+        sent.append(sems.local(own_table, tables.at[here]))
+        steps = gather_steps(place, sems, shard, w_attention)
+        steps[0]()
+        for copy in sent:
+            copy.start()
+        split_pair(0, gate_up_weight, *shards)
+        steps[1]()
+        yield [(0, 0)]
+        for copy in sent:
+            copy.wait()
+        total = tables[0]
+        for index in range(1, tables.shape[0]):
+            total = total + tables[index]
+        table[...] = total
+        read = lambda span: x_in[span, :].astype(jnp.float32)
+    else:
+        middle, sums, table, w_attention, cosine, sine, query_segments, key_segments = ins
+        queries, pairs, log_total, mixed, normed, x_out = outs
+
+        def read(span):
+            values = middle[span, :] + sums[span, :].astype(jnp.float32)
+            x_out[span, :] = values
+            return values
+
     rows = normed.shape[0]
     local_len = rows // seq_count
     q_width = queries.shape[1]
     heads = q_width // HD
+    weight = lambda start, size: w_attention[:, :, pl.ds(start, size)].reshape(-1, size)
+
+    def write(span, values):
+        normed[span, :] = values
+
+    normalize(rows, 64, read, table[pl.ds(2 * layer, 1), :], write)
+    if layer == 0:
+        steps[2]()
+        steps[3]()
     cos, sin = cosine[...], sine[...]
-    columns = pl.ds(q_width, 2 * HD)
-    lin = mm(normed[...], w_attention[:, columns], (1, 0)) + bias[:, columns]
+    kv_head = place.tensor * heads // (H // KV)
+    bias_row = pl.ds(3 * LAYERS + layer, 1)
+    bias_at = lambda head: table[bias_row, pl.ds(pl.multiple_of(head * HD, HD), HD)]
+    lin = mm(normed[...], weight(q_width, 2 * HD), (1, 0))
     me = place.ctx
-    pairs[me, :, :HD] = turn_heads(lin[:, :HD], cos, sin).astype(jnp.bfloat16)
-    pairs[me, :, HD:] = lin[:, HD:].astype(jnp.bfloat16)
+    pairs[me, :, :HD] = turn_heads(lin[:, :HD] + bias_at(kv_head), cos, sin).astype(jnp.bfloat16)
+    pairs[me, :, HD:] = (lin[:, HD:] + bias_at(KV + kv_head)).astype(jnp.bfloat16)
     sent = [
         sems.remote(pairs.at[me], pairs.at[me], place.to_ctx(place.ctx_at(step)))
         for step in range(1, place.ctxs)
     ]
     for copy in sent:
         copy.start()
-    yield
-    yield
-    lin = mm(normed[...], w_attention[:, :q_width], (1, 0)) + bias[:, :q_width]
+    yield [(1, 0), (2, 0)] if layer == 0 else [(0, 0), (1, 0)]
+    bias = table[pl.ds(2 * LAYERS + layer, 1), pl.ds(0, q_width)]
+    lin = mm(normed[...], weight(0, q_width), (1, 0)) + bias
     for index in range(heads):
         columns = slice(index * HD, (index + 1) * HD)
         queries[:, columns] = turn_heads(lin[:, columns], cos, sin).astype(jnp.bfloat16)
@@ -655,8 +753,14 @@
             weights = (exp_scores / row_total).astype(jnp.bfloat16)
             log_total[span, pl.ds(index, 1)] = row_max + jnp.log(row_total)
             mixed[span, columns] = mm(weights, values, (1, 0)).astype(jnp.bfloat16)
-    w_out = w_attention[:, q_width + 2 * HD :]
-    part[...] = mm(mixed[...], w_out, (1, 1)).astype(part.dtype)
+    part[...] = mm(mixed[...], weight(q_width + 2 * HD, q_width), (1, 1)).astype(part.dtype)
+    yield None
+    if layer == 0:
+        for other in range(1, LAYERS):
+            yield None
+            shard, gate, up = next_shards[3 * other - 3 : 3 * other]
+            attention_shard(other, first_head, query_weight, kv_weight, out_weight, shard)
+            split_pair(other, gate_up_weight, gate, up)
 
 
 def attend_back(seq_count, place, sems, ins, outs, scratch, part, in_grad, out_grad):
@@ -669,10 +773,10 @@
     q_width = queries.shape[1]
     heads = q_width // HD
     scale = HD ** (-0.5)
-    yield
+    yield [(0, 0), (1, 0)]
     cos, sin = cosine[...], -sine[...]
-    w_in = w_attention[:, : q_width + 2 * HD]
-    w_out = w_attention[:, q_width + 2 * HD :]
+    weight = lambda start, size: w_attention[:, :, pl.ds(start, size)].reshape(-1, size)
+    w_out = weight(q_width + 2 * HD, q_width)
     mixed_grad[...] = mm(grad[...], w_out, (1, 0)).astype(jnp.bfloat16)
     totals = log_total[...].T
     for sequence in range(seq_count):
@@ -712,42 +816,40 @@
         to = place.ctx_at(step)
         sent.append(sems.remote(pair_grad.at[to], got.at[step - 1], place.to_ctx(to)))
         sent[-1].start()
-    yield
+    yield [(0, 1), (1, 1)]
     total = pair_grad[place.ctx].astype(jnp.float32)
     for step, copy in enumerate(sent):
         copy.wait()
         total = total + got[step].astype(jnp.float32)
     lin_grad[:, pl.ds(q_width, HD)] = turn_heads(total[:, :HD], cos, sin).astype(jnp.bfloat16)
     lin_grad[:, pl.ds(q_width + HD, HD)] = total[:, HD:].astype(jnp.bfloat16)
-    part[...] = mm(lin_grad[...], w_in, (1, 1)).astype(part.dtype)
-    yield
-    product = mm(normed[...], lin_grad[...], (0, 0)).astype(in_grad.dtype)
-    in_grad[...] = product.reshape(in_grad.shape)
-    product = mm(grad[...], mixed[...], (0, 0)).astype(out_grad.dtype)
-    out_grad[...] = product.reshape(out_grad.shape)
+    part[...] = mm(lin_grad[...], weight(0, q_width + 2 * HD), (1, 1)).astype(part.dtype)
+    yield None
+    shard_rows = in_grad.shape[1]
+    width = normed.shape[1] // LATE_PIECES
+    for piece in range(LATE_PIECES):
+        columns = pl.ds(piece * width, width)
+        shards = pl.ds(piece * width // shard_rows, width // shard_rows)
+        for rows_in, grads_in, made in ((normed, lin_grad, in_grad), (grad, mixed, out_grad)):
+            product = mm(rows_in[:, columns], grads_in[...], (0, 0)).astype(made.dtype)
+            made[shards] = product.reshape(-1, *made.shape[1:])
+            yield None
 
 
 def finish_kernel(sizes, *refs):
     refs = list(refs)
     gain_grads = take(refs, 2 * LAYERS)
     lin_grads = take(refs, LAYERS)
-    in_grads = take(refs, LAYERS)
+    (in_grad,) = take(refs, 1)
     sums, kv_parts, kv_rows, rows, send, recv = refs
     place = Place(sizes)
     sems = Sems(send, recv)
-    shard_rows, width = in_grads[0].shape
+    width = in_grad.shape[1]
     q_width = width - 2 * HD
     group = H // KV
     heads = q_width // HD
     dps, ctxs, tensors = sizes
-    at = lambda index, step, size: lax.rem(index + step, size)
-    line = [place.to_tensor(at(place.tensor, step, tensors)) for step in range(1, tensors)]
-    plane = [
-        {"dp": at(place.dp, step, dps), "ctx": at(place.ctx, turn, ctxs)}
-        for step in range(dps)
-        for turn in range(ctxs)
-        if step or turn
-    ]
+    line, plane = place.line_partners(), place.plane_partners()
     barrier = pltpu.get_barrier_semaphore()
     for device in line + plane:
         pl.semaphore_signal(barrier, inc=1, device_id=device, device_id_type=MESH)
@@ -756,9 +858,8 @@
     here = place.dp * ctxs + place.ctx
     kv_rows[me] = jnp.zeros(kv_rows.shape[1:], jnp.float32)
     rows[here] = jnp.zeros(rows.shape[1:], jnp.float32)
+    kv_parts[me] = in_grad[:, q_width:].astype(kv_parts.dtype)
     for layer in range(LAYERS):
-        span = pl.ds(layer * shard_rows, shard_rows)
-        kv_parts[me, span, :] = in_grads[layer][:, q_width:].astype(kv_parts.dtype)
         bias = jnp.sum(lin_grads[layer][...].astype(jnp.float32), axis=0, keepdims=True)
         kv_rows[me, pl.ds(layer, 1), :] = bias[:, q_width:]
         rows[here, pl.ds(2 * LAYERS + layer, 1), pl.ds(0, q_width)] = bias[:, :q_width]
@@ -791,17 +892,17 @@
         copy.wait()
 
 
-def finish(sizes, number, gain_grads, lin_grads, in_grads):
+def finish(sizes, number, gain_grads, lin_grads, in_grad):
     dps, ctxs, tensors = sizes
     in_vmem = pl.BlockSpec(memory_space=pltpu.VMEM)
-    args = (*[gain[None] for gain in gain_grads], *lin_grads, *in_grads)
+    args = (*[gain[None] for gain in gain_grads], *lin_grads, in_grad)
     height, width = -(-4 * LAYERS // 8) * 8, gain_grads[0].shape[0]
     count = 2 * (tensors - 1) + dps * ctxs - 1
     return pl.pallas_call(
         functools.partial(finish_kernel, sizes),
         out_shape=[
             jax.ShapeDtypeStruct((height, width), jnp.float32),
-            jax.ShapeDtypeStruct((tensors, LAYERS * in_grads[0].shape[0], 2 * HD), jnp.bfloat16),
+            jax.ShapeDtypeStruct((tensors, in_grad.shape[0], 2 * HD), jnp.bfloat16),
         ],
         in_specs=[in_vmem] * len(args),
         out_specs=[in_vmem] * 2,
@@ -874,8 +975,23 @@
     return jnp.where(column < width, block, jnp.zeros_like(block))
 
 
-def forward_tile(width, n2, w_gate, w_up, w_down, gate_out, up_out, inner_out, part_out, total):
+def forward_tile(
+    width, layer, x_in, sums, table, w_gate, w_up, w_down, middle, n2, gate_out, up_out, inner_out, part_out, total
+):
     tile = pl.program_id(0)
+
+    @pl.when(tile == 0)
+    def _():
+        def read(span):
+            values = x_in[span, :].astype(jnp.float32) + sums[span, :].astype(jnp.float32)
+            middle[span, :] = values
+            return values
+
+        def write(span, values):
+            n2[span, :] = values
+
+        normalize(n2.shape[0], 64, read, table[pl.ds(2 * layer + 1, 1), :], write)
+
     gate = mm(n2[...], w_gate[...], (1, 0))
     up = mm(n2[...], w_up[...], (1, 0))
     gate_out[...] = gate
@@ -897,18 +1013,20 @@
         part_out[...] = total[...].astype(part_out.dtype)
 
 
-def forward_ffn(n2, w_gate, w_up, w_down):
-    rows, model_width = n2.shape
+def forward_ffn(layer, x_in, sums, table, w_gate, w_up, w_down):
+    rows, model_width = x_in.shape
     width = w_gate.shape[1]
     whole = pl.BlockSpec((rows, model_width), lambda j: (0, 0))
     weight = pl.BlockSpec((model_width, TILE), lambda j: (0, j))
     units = pl.BlockSpec((rows, TILE), lambda j: (0, j))
     return pl.pallas_call(
-        functools.partial(forward_tile, width),
+        functools.partial(forward_tile, width, layer),
         grid=(pl.cdiv(width, TILE),),
-        in_specs=[whole, weight, weight, weight],
-        out_specs=[units, units, units, whole],
+        in_specs=[whole, whole, pl.BlockSpec(table.shape, lambda j: (0, 0)), weight, weight, weight],
+        out_specs=[whole, whole, units, units, units, whole],
         out_shape=[
+            jax.ShapeDtypeStruct((rows, model_width), jnp.float32),
+            jax.ShapeDtypeStruct((rows, model_width), jnp.bfloat16),
             jax.ShapeDtypeStruct((rows, width), jnp.float32),
             jax.ShapeDtypeStruct((rows, width), jnp.float32),
             jax.ShapeDtypeStruct((rows, width), jnp.bfloat16),
@@ -917,7 +1035,7 @@
         scratch_shapes=[pltpu.VMEM((rows, model_width), jnp.float32)],
         compiler_params=pltpu.CompilerParams(vmem_limit_bytes=56 << 20),
         name="forward_ffn",
-    )(n2, w_gate, w_up, w_down)
+    )(x_in, sums, table, w_gate, w_up, w_down)
 
 
 def backward_tile(
@@ -1027,7 +1145,8 @@
     return rotate(grad_rows, cosine, -sine)
 
 
-def norm_back(values, norm_scale, gain, grad_rows):
+def norm_back(values, gain, grad_rows):
+    norm_scale = lax.rsqrt(jnp.mean(values * values, axis=-1, keepdims=True) + NORM_EPS)
     weighted = grad_rows * gain
     inner_mean = jnp.mean(weighted * values, axis=-1, keepdims=True)
     grad_values = (
@@ -1070,73 +1189,33 @@
     def move(**what):
         return transfer(sizes, next(numbers), **what)
 
-    attention_shards = [
-        jnp.concatenate(
-            [
-                query_weight[layer],
-                lax.dynamic_slice_in_dim(kv_weight[layer], kv_head * HD, HD, 1),
-                lax.dynamic_slice_in_dim(kv_weight[layer], (KV + kv_head) * HD, HD, 1),
-                out_weight[layer].T,
-            ],
-            axis=1,
-        )
-        for layer in range(LAYERS)
-    ]
     down_shards = [down_weight[layer].T for layer in range(LAYERS)]
 
     def after(array, *earlier):
         return lax.optimization_barrier((array, *earlier))[0]
 
-    def gather(shard):
-        return lax.all_gather(shard, ("dp", "ctx"), axis=0, tiled=True)
-
-    def scatter(gradient):
-        return lax.psum_scatter(gradient, ("dp", "ctx"), scatter_dimension=0, tiled=True)
-
-    bias_part = kv_bias.shape[1]
-    head_part = query_bias.shape[2]
-    small_width = -(-max(shard_rows, bias_part) // 128) * 128
-    pad = lambda a: jnp.pad(a, ((0, 0), (0, small_width - a.shape[1])))
-    small_rows = LAYERS * (2 + heads_here + 1)
-    small_shard = jnp.pad(
-        jnp.concatenate(
-            [
-                pad(norm_gains.reshape(LAYERS * 2, shard_rows)),
-                pad(query_bias.reshape(LAYERS * heads_here, head_part)),
-                pad(kv_bias),
-            ],
-            axis=0,
-        ),
-        ((0, -small_rows % ROW_TILE), (0, 0)),
+    head_part, bias_part = query_bias.shape[2], kv_bias.shape[1]
+    shard = lax.axis_index("dp") * ctxs + lax.axis_index("ctx")
+
+    def placed(part, width):
+        zeros = jnp.zeros((*part.shape[:-1], width), wide)
+        return lax.dynamic_update_slice_in_dim(
+            zeros, part.astype(wide), shard * part.shape[-1], part.ndim - 1
+        )
+
+    own_table = jnp.concatenate(
+        [
+            placed(norm_gains, model_width).reshape(2 * LAYERS, model_width),
+            jnp.pad(
+                placed(query_bias, HD).reshape(LAYERS, q_width),
+                ((0, 0), (0, model_width - q_width)),
+            ),
+            jnp.pad(
+                placed(kv_bias, 2 * KV * HD), ((0, 0), (0, model_width - 2 * KV * HD))
+            ),
+        ]
     )
-
-    small, attention_weights = move(gathers=[small_shard, attention_shards[0]])
-    gate_up = after(gate_up_weight, small)
-    gate_shards = [after(gate_up[layer, :, 0]) for layer in range(LAYERS)]
-    up_shards = [after(gate_up[layer, :, 1]) for layer in range(LAYERS)]
-    at = LAYERS * 2
-    gains = (
-        small[:, :at, :shard_rows]
-        .transpose(1, 0, 2)
-        .reshape(LAYERS, 2, model_width)
-        .astype(wide)
-    )
-    q_biases = (
-        small[:, at : at + LAYERS * heads_here, :head_part]
-        .transpose(1, 0, 2)
-        .reshape(LAYERS, q_width)
-        .astype(wide)
-    )
-    at += LAYERS * heads_here
-    kv_biases = small[:, at : at + LAYERS, :bias_part].transpose(1, 0, 2).reshape(LAYERS, 2 * KV, HD)
-    kv_biases = jnp.concatenate(
-        [
-            lax.dynamic_slice_in_dim(kv_biases, kv_head, 1, 1)[:, 0],
-            lax.dynamic_slice_in_dim(kv_biases, KV + kv_head, 1, 1)[:, 0],
-        ],
-        axis=1,
-    ).astype(wide)
-
+    own_table = jnp.pad(own_table, ((0, -own_table.shape[0] % 8), (0, 0)))
     own_segments = lax.dynamic_slice_in_dim(segment_ids, local_start, local_len, 1)
     earlier = jnp.sum(
         (segment_ids[:, None, :] < own_segments[:, :, None]).astype(jnp.int32), axis=-1
@@ -1149,59 +1228,73 @@
     sine = jnp.sin(angles).reshape(row_count, 1, HD // 2)
     cos_wide = jnp.concatenate([cosine[:, 0], cosine[:, 0]], axis=1)
     sin_wide = jnp.concatenate([-sine[:, 0], sine[:, 0]], axis=1)
-    hidden = hidden_in.astype(wide).reshape(row_count, model_width)
+    hidden = hidden_in.reshape(row_count, model_width)
     stored = []
     for layer in range(LAYERS):
-        w_attention = attention_weights.reshape(model_width, q_width + 2 * HD + q_width)
-        scale_one = lax.rsqrt(jnp.mean(hidden * hidden, axis=-1, keepdims=True) + NORM_EPS)
-        normed = (hidden * scale_one * gains[layer, 0]).astype(low)
-        work = Work(
-            functools.partial(attend, seq_count),
-            [
-                normed,
-                w_attention,
-                jnp.concatenate([q_biases[layer], kv_biases[layer]])[None],
-                cos_wide,
-                sin_wide,
-                own_segments.reshape(row_count, 1),
-                segment_ids,
-            ],
-            [
-                jax.ShapeDtypeStruct((row_count, q_width), low),
-                jax.ShapeDtypeStruct((ctxs, row_count, 2 * HD), low),
-                jax.ShapeDtypeStruct((row_count, HD), wide),
-                jax.ShapeDtypeStruct((row_count, q_width), low),
-            ],
-            [],
-            ctxs,
+        sides = [cos_wide, sin_wide, own_segments.reshape(row_count, 1), segment_ids]
+        outputs = [
+            jax.ShapeDtypeStruct((row_count, q_width), low),
+            jax.ShapeDtypeStruct((ctxs, row_count, 2 * HD), low),
+            jax.ShapeDtypeStruct((row_count, HD), wide),
+            jax.ShapeDtypeStruct((row_count, q_width), low),
             jax.ShapeDtypeStruct((row_count, model_width), low),
+        ]
+        if layer == 0:
+            unit_shard = jax.ShapeDtypeStruct((shard_rows, hidden_units), low)
+            attention_shard = jax.ShapeDtypeStruct((shard_rows, 2 * q_width + 2 * HD), low)
+            outputs.append(jax.ShapeDtypeStruct((n, *attention_shard.shape), low))
+            outputs.append(jax.ShapeDtypeStruct(own_table.shape, wide))
+            outputs += [attention_shard, unit_shard, unit_shard] * (LAYERS - 1)
+            weights = [query_weight, kv_weight, out_weight.transpose(0, 2, 1), gate_up_weight]
+            work = Work(
+                functools.partial(attend, layer, seq_count),
+                [hidden, own_table, *sides, *weights],
+                outputs,
+                [
+                    pltpu.VMEM((n, *own_table.shape), wide),
+                    pltpu.VMEM(attention_shard.shape, low),
+                ],
+                n + gather_sems(sizes) + ctxs,
+                jax.ShapeDtypeStruct((row_count, model_width), low),
+                shards=[unit_shard, unit_shard],
+                whole_plane=True,
+            )
+            total, *moved = move(
+                work=work, gathers=[down_shards[0]], plan=((8, 14), (12, 18), (14, 99))
+            )
+            w_gate, w_up, down_weights = moved[:3]
+            queries, pairs, log_total, mixed_low, normed, w_attention, table = moved[3:10]
+            later_shards = moved[10:]
+        else:
+            outputs.append(jax.ShapeDtypeStruct((row_count, model_width), wide))
+            work = Work(
+                functools.partial(attend, layer, seq_count),
+                [middle, total, table, w_attention, *sides],
+                outputs,
+                [],
+                ctxs,
+                jax.ShapeDtypeStruct((row_count, model_width), low),
+            )
+            total, w_gate, w_up, queries, pairs, log_total, mixed_low, normed, hidden = move(
+                work=work,
+                gathers=later_shards[3 * layer - 2 : 3 * layer],
+                plan=((8, 14), (12, 18)),
+            )
+        w_gate, w_up, w_down = [
+            a.reshape(model_width, hidden_units) for a in (w_gate, w_up, down_weights)
+        ]
+        middle, normed_two, gate, up, inner_low, part = forward_ffn(
+            layer, hidden, total, table, w_gate, w_up, w_down
         )
-        mine = [gate_shards[layer], up_shards[layer]]
-        if layer == 0:
-            mine.append(down_shards[layer])
-        total, *moved, queries, pairs, log_total, mixed_low = move(
-            work=work, gathers=mine, plan=((8, 14), (12, 18), (14, 99))
-        )
-        if layer == 0:
-            down_weights = moved.pop()
-        w_gate, w_up, w_down = [
-            a.reshape(model_width, hidden_units) for a in (*moved, down_weights)
-        ]
-        middle = hidden + total.astype(wide)
-        scale_two = lax.rsqrt(jnp.mean(middle * middle, axis=-1, keepdims=True) + NORM_EPS)
-        normed_two = (middle * scale_two * gains[layer, 1]).astype(low)
-        gate, up, inner_low, part = forward_ffn(normed_two, w_gate, w_up, w_down)
         stored.append(
             (
                 hidden,
-                scale_one,
                 normed,
                 queries,
                 pairs,
                 log_total,
                 mixed_low,
                 middle,
-                scale_two,
                 normed_two,
                 gate,
                 up,
@@ -1213,12 +1306,11 @@
             )
         )
         if layer + 1 < LAYERS:
-            total, attention_weights, down_weights = move(
+            total, w_attention, down_weights = move(
                 z_sums=[part],
-                gathers=[attention_shards[layer + 1], down_shards[layer + 1]],
+                gathers=[later_shards[3 * layer], down_shards[layer + 1]],
                 plan=((8, 15), (13, 18)),
             )
-            hidden = middle + total.astype(wide)
         else:
             last_part = part
 
@@ -1231,14 +1323,12 @@
     for layer in reversed(range(LAYERS)):
         (
             layer_input,
-            scale_one,
             normed,
             queries,
             pairs,
             log_total,
             mixed_low,
             middle,
-            scale_two,
             normed_two,
             gate,
             up,
@@ -1256,7 +1346,7 @@
         total, done[layer]["gate"], done[layer]["down_first"] = move(
             z_sums=[part], scatters=[grad_gate_w, down_first], plan=((2, 9), (3, 11))
         )
-        back_two, grad_gain_two = norm_back(middle, scale_two, gains[layer, 1], total.astype(wide))
+        back_two, grad_gain_two = norm_back(middle, table[2 * layer + 1], total.astype(wide))
         grad_middle = grad_hidden + back_two
         grad_mid_low = grad_middle.astype(low)
         work = Work(
@@ -1287,45 +1377,57 @@
                 jax.ShapeDtypeStruct((n, shard_rows, q_width), low),
             ],
         )
+        extra = [kv_part] if layer + 1 < LAYERS else []
         total, *results, grad_lin = move(
             work=work,
+            line_pieces=extra,
             scatters=[grad_up_w, down_rest],
-            plan=((-1, 4), (-1, 6), (5, 9), (5, 10)),
+            plan=((-1, 4), (-1, 6), (6, 10), (6, 10)),
         )
         for name, result in zip(("up", "down_rest", "in", "out"), results):
             done[layer][name] = result
         done[layer]["lin"] = grad_lin
+        kv_part = done[layer]["in"][:, q_width:].astype(low)
+        if extra:
+            done[layer + 1]["kv"] = results[-1]
         back_one, grad_gain_one = norm_back(
-            layer_input, scale_one, gains[layer, 0], total.astype(wide)
+            layer_input.astype(wide), table[2 * layer], total.astype(wide)
         )
         small_grads[layer] = [grad_gain_one, grad_gain_two]
         grad_hidden = grad_middle + back_one
-
-    last_total = lax.psum(after(last_part, grad_hidden), "tensor")
-    block_out = (stored[-1][7] + last_total.astype(wide)).astype(low)
-    block_out = block_out.reshape(seq_count, local_len, model_width)
-    input_grad = grad_hidden.reshape(seq_count, local_len, model_width)
+        if layer + 1 == LAYERS:
+            half = row_count // 2
+            last_totals = [lax.psum(after(last_part[:half], total), "tensor")]
 
     sums, kv_parts = finish(
         sizes,
         next(numbers),
         [gain for layer in range(LAYERS) for gain in small_grads[layer]],
         [done[layer]["lin"] for layer in range(LAYERS)],
-        [done[layer]["in"] for layer in range(LAYERS)],
+        done[0]["in"],
     )
-    shard = lax.axis_index("dp") * ctxs + lax.axis_index("ctx")
+    done[0]["kv"] = kv_parts
     cut = lambda a, size: lax.dynamic_slice_in_dim(a, shard * size, size, a.ndim - 1)
+    last_totals.append(lax.psum(after(last_part[half:], sums), "tensor"))
+    last_total = jnp.concatenate([after(last_totals[0], sums), last_totals[1]])
+    block_out = (stored[-1][6] + last_total.astype(wide)).astype(low)
+    block_out = block_out.reshape(seq_count, local_len, model_width)
+    input_grad = grad_hidden.reshape(seq_count, local_len, model_width)
+
     gains_grad = cut(sums[: 2 * LAYERS], shard_rows).reshape(LAYERS, 2, shard_rows)
     q_rows = sums[2 * LAYERS : 3 * LAYERS, :q_width].reshape(LAYERS, heads_here, HD)
     query_bias_grad = cut(q_rows, head_part)
     kv_bias_grad = cut(sums[3 * LAYERS : 4 * LAYERS, : 2 * KV * HD], bias_part)
-    kv_heads = []
-    for head in range(KV):
-        owners = [t for t in range(tensors) if t * heads_here // (H // KV) == head]
-        kv_heads.append(sum(kv_parts[t].astype(wide) for t in owners))
-    kv_weight_grad = jnp.concatenate(
-        [a[:, :HD] for a in kv_heads] + [a[:, HD:] for a in kv_heads], axis=1
-    ).reshape(LAYERS, shard_rows, 2 * KV * HD)
+    kv_weight_grad = []
+    for layer in range(LAYERS):
+        heads = []
+        for head in range(KV):
+            owners = [t for t in range(tensors) if t * heads_here // (H // KV) == head]
+            heads.append(sum(done[layer]["kv"][t].astype(wide) for t in owners))
+        kv_weight_grad.append(
+            jnp.concatenate([a[:, :HD] for a in heads] + [a[:, HD:] for a in heads], axis=1)
+        )
+    kv_weight_grad = jnp.stack(kv_weight_grad)
 
     stack = lambda name, f=lambda a: a: jnp.stack([f(done[layer][name]) for layer in range(LAYERS)])
     down_grad = jnp.concatenate([stack("down_first"), stack("down_rest")], axis=2)

time: 827 us -> 840 us (1.016)
  Pallas kernels: 698 us -> 717 us
  waiting for transfers between devices: 7.07 us -> 19.3 us
  other arithmetic: 72.7 us -> 63.6 us
    pallas_call x8 -> x7, Pallas kernels: 526 us -> 552 us  [transfer(): pl.pallas_call(functools.partial(transfer_kernel, sizes, counts, plan, wo...]
    pallas_call x1, Pallas kernels: 28.7 us -> 14.6 us  [finish(): pl.pallas_call(functools.partial(finish_kernel, sizes), out_shape=[jax.Sh...]
    psum x1, waiting for transfers between devices: 7.05 us -> 19.3 us  [local(): last_totals.append(lax.psum(after(last_part[half:], sums), 'tensor'))]
  transfers between devices with their start and end apart: 1 -> 1, of which waited for: 1 -> 1; matrix products, arithmetic and copies ran while one was open for 2% -> 3% of each run, Pallas kernels for 7% -> 3%
where the time goes in v4:
time: 840 us; the launch traced here: 830 us
  Pallas kernels  717 us (85%)
  other arithmetic  63.6 us (8%)
  waiting for transfers between devices  19.3 us (2%)
  between operations  15 us (2%)
  local copies, waits for them, and re-layouts  14.9 us (2%)
    pallas_call x7, Pallas kernels, transfer(): pl.pallas_call(functools.partial(transfer_kernel, sizes, counts, plan, wo...  552 us
    pallas_call x2, Pallas kernels, backward_ffn(): pl.pallas_call(functools.partial(backward_tile, width), grid=(pl.cdiv(wid...  76.1 us
    pallas_call x2, Pallas kernels, forward_ffn(): pl.pallas_call(functools.partial(forward_tile, width, layer), grid=(pl.cd...  49.6 us
    pallas_call x1, Pallas kernels, pair_adam(): pl.pallas_call(functools.partial(pair_adam_block, step_rate), grid=(layer...  24.7 us
    psum x1, waiting for transfers between devices, local(): last_totals.append(lax.psum(after(last_part[half:], sums), 'tensor'))  19.3 us
  transfers between devices with their start and end apart: 1, of which 1 were waited for; matrix products, arithmetic and copies ran while one was open for 3% of the time, Pallas kernels for 3%

profile of v4, /device:TPU:0, one launch (start us, length us, event | category | flops | bytes accessed | tf_op | source)
XLA Modules:
  0.0 830.3 jit_solution(9178427809632520658)
XLA Ops:
  13.1 2.7 slice_bitcast_fusion
  19.5 124.7 %transfer1.1 = (bf16[512,1536]{1,0:T(8,128)(2,1)}, bf16[8,192,2240]{2,1,0:T(8,128)(2,1)}, bf16[8,192,2240]{2,1,0:T(8,128)(2,1)}, bf16[8,192,2240]{2,1,0:T(8,128)...) custom-call(bf16[192,2240]{1,0:T(8,128)(2,1)} %get-tuple-element.300, ...), custom_call_target="tpu_custom_call" | custom-call | flops 30000001024 | bytes 150000000 | tf_op jit(solution)/shard_map/transfer1/pallas_call | solution.py:599
  144.2 1.6 slice_reduce_fusion
  145.8 24.7 %forward_ffn.2 = (f32[512,1536]{1,0:T(8,128)}, bf16[512,1536]{1,0:T(8,128)(2,1)}, f32[512,2240]{1,0:T(8,128)}, f32[512,2240]{1,0:T(8,128)}, bf16[512,2240]{1,0:T(8,128)(2,1)}, /*index=5*/bf16[512,1536]{1,0:T(8,128)(2,1)}) custom-call(bf16[512,1536]{1,0:T(8,128)(2,1)} %bitcast.90, bf16[512,1536]{1,0:T(8,128)(2,1)} %get-tuple-element.112.sums, ...), custom_call_target="tpu_custom_call" | custom-call | tf_op jit(solution)/shard_map/forward_ffn/pallas_call | solution.py:1022
  170.5 2.2 multiply_reduce_fusion
  172.7 53.1 %transfer2.1 = (bf16[512,1536]{1,0:T(8,128)(2,1)}, bf16[8,192,1024]{2,1,0:T(8,128)(2,1)}, bf16[8,192,2240]{2,1,0:T(8,128)(2,1)}) custom-call(bf16[512,1536]{1,0:T(8,128)(2,1)} %get-tuple-element.118.refs_0_, bf16[192,1024]{1,0:T(8,128)(2,1)} %get-tuple-element.119.refs_1_, bf16[192,2240]{1,0:T(8,128)(2,1)} %get-tuple-element.299.refs_2_), custom_call_target="tpu_custom_call" | custom-call | flops 30000001024 | bytes 150000000 | tf_op jit(solution)/shard_map/transfer2/pallas_call | solution.py:599
  225.8 78.0 %transfer3.1 = (bf16[512,1536]{1,0:T(8,128)(2,1)}, bf16[8,192,2240]{2,1,0:T(8,128)(2,1)}, bf16[8,192,2240]{2,1,0:T(8,128)(2,1)}, bf16[512,384]{1,0:T(8,128)(2,1)...) custom-call(bf16[192,2240]{1,0:T(8,128)(2,1)} %get-tuple-element.110, ...), custom_call_target="tpu_custom_call" | custom-call | flops 30000001024 | bytes 150000000 | tf_op jit(solution)/shard_map/transfer3/pallas_call | solution.py:599
  303.8 2.2 multiply_reduce_fusion.1
  306.0 24.9 %forward_ffn.3 = (f32[512,1536]{1,0:T(8,128)}, bf16[512,1536]{1,0:T(8,128)(2,1)}, f32[512,2240]{1,0:T(8,128)}, f32[512,2240]{1,0:T(8,128)}, bf16[512,2240]{1,0:T(8,128)(2,1)}, /*index=5*/bf16[512,1536]{1,0:T(8,128)(2,1)}) custom-call(f32[512,1536]{1,0:T(8,128)} %get-tuple-element.122.x_in, bf16[512,1536]{1,0:T(8,128)(2,1)} %get-tuple-element.123.sums, ...), custom_call_target="tpu_custom_call" | custom-call | tf_op jit(solution)/shard_map/forward_ffn/pallas_call | solution.py:1022
  330.9 2.2 multiply_reduce_fusion.2
  333.1 38.0 %backward_ffn.2 = (bf16[1536,1024]{1,0:T(8,128)(2,1)}, bf16[1536,1216]{1,0:T(8,128)(2,1)}, bf16[1536,2240]{1,0:T(8,128)(2,1)}, bf16[1536,2240]{1,0:T(8,128)(2,1)}, bf16[512,1536]{1,0:T(8,128)(2,1)}) custom-call(bf16[512,1536]{1,0:T(8,128)(2,1)} %bitcast.91, bf16[512,1536]{1,0:T(8,128)(2,1)} %get-tuple-element.129.n2, ...), custom_call_target="tpu_custom_call" | custom-call | tf_op jit(solution)/shard_map/backward_ffn/pallas_call | solution.py:1112
  371.1 58.3 %transfer4.1 = (bf16[512,1536]{1,0:T(8,128)(2,1)}, f32[192,2240]{1,0:T(8,128)}, f32[192,1024]{1,0:T(8,128)}) custom-call(bf16[512,1536]{1,0:T(8,128)(2,1)} %get-tuple-element.135.refs_0_, bf16[8,192,2240]{2,1,0:T(8,128)(2,1)} %bitcast.107, bf16[8,192,1024]{2,1,0:T(8,128)(2,1)} %bitcast.111), custom_call_target="tpu_custom_call" | custom-call | flops 30000001024 | bytes 150000000 | tf_op jit(solution)/shard_map/transfer4/pallas_call | solution.py:599
  429.4 3.5 fusion.23
  433.9 4.0 fusion.49.refs_2_
  437.9 89.4 %transfer5.1 = (bf16[512,1536]{1,0:T(8,128)(2,1)}, f32[192,2240]{1,0:T(8,128)}, f32[192,1216]{1,0:T(8,128)}, f32[192,640]{1,0:T(8,128)}, f32[192,384]{1,0:T(8,128)}, /*index=5*/bf16[512,640]{1,0:T(8,128)(2,1)}) custom-call(bf16[8,192,2240]{2,1,0:T(8,128)(2,1)} %bitcast.105, bf16[8,192,1216]{2,1,0:T(8,128)(2,1)} %bitcast.109, ...), custom_call_target="tpu_custom_call" | custom-call | flops 30000001024 | bytes 150000000 | tf_op jit(solution)/shard_map/transfer5/pallas_call | solution.py:599
  527.3 3.5 fusion.25
  531.1 5.0 fusion.60
  536.1 38.0 %backward_ffn.3 = (bf16[1536,1024]{1,0:T(8,128)(2,1)}, bf16[1536,1216]{1,0:T(8,128)(2,1)}, bf16[1536,2240]{1,0:T(8,128)(2,1)}, bf16[1536,2240]{1,0:T(8,128)(2,1)}, bf16[512,1536]{1,0:T(8,128)(2,1)}) custom-call(bf16[512,1536]{1,0:T(8,128)(2,1)} %get-tuple-element.297.grad, bf16[512,1536]{1,0:T(8,128)(2,1)} %get-tuple-element.146.n2, ...), custom_call_target="tpu_custom_call" | custom-call | tf_op jit(solution)/shard_map/backward_ffn/pallas_call | solution.py:1112
  574.2 60.0 %transfer6.1 = (bf16[512,1536]{1,0:T(8,128)(2,1)}, f32[192,2240]{1,0:T(8,128)}, f32[192,1024]{1,0:T(8,128)}) custom-call(bf16[512,1536]{1,0:T(8,128)(2,1)} %get-tuple-element.153.refs_0_, bf16[8,192,2240]{2,1,0:T(8,128)(2,1)} %bitcast.106, bf16[8,192,1024]{2,1,0:T(8,128)(2,1)} %bitcast.110), custom_call_target="tpu_custom_call" | custom-call | flops 30000001024 | bytes 150000000 | tf_op jit(solution)/shard_map/transfer6/pallas_call | solution.py:599
  634.2 3.5 fusion.27
  637.7 1.6 slice.147.refs_2_
  639.3 5.0 fusion.58
  644.3 88.9 %transfer7.1 = (bf16[512,1536]{1,0:T(8,128)(2,1)}, f32[192,2240]{1,0:T(8,128)}, f32[192,1216]{1,0:T(8,128)}, f32[192,640]{1,0:T(8,128)}, f32[192,384]{1,0:T(8,12...) custom-call(bf16[8,192,2240]{2,1,0:T(8,128)(2,1)} %bitcast.104, bf16[8,192,1216]{2,1,0:T(8,128)(2,1)} %bitcast.108, ...), custom_call_target="tpu_custom_call" | custom-call | flops 30000001024 | bytes 150000000 | tf_op jit(solution)/shard_map/transfer7/pallas_call | solution.py:599
  733.2 2.7 fusion.32
  737.2 14.6 %finish.1 = (f32[8,1536]{1,0:T(8,128)S(1)}, bf16[4,192,256]{2,1,0:T(8,128)(2,1)S(1)}) custom-call(f32[1,1536]{1,0:T(1,128)S(1)} %broadcast_in_dim.17.refs_0_, f32[1,1536]{1,0:T(1,128)S(1)} %broadcast_in_dim.18.refs_1_, f32[1,1536]{1,0:T(1,128)S(1)} %broadcast_in_dim.19.refs_2_, f32[1,1536]{1,0:T(1,128)S(1)} %broadcast_in_dim.40.refs_3_, ...), custom_call_target="tpu_custom_call" | custom-call | tf_op jit(solution)/shard_map/finish/pallas_call | solution.py:901
  753.4 5.0 fusion.12
  760.9 1.9 convert_subtract_fusion.1
  762.9 1.5 convert_subtract_fusion.3
  767.4 24.7 %pair_adam.1 = (f32[2,192,2,2240]{3,2,1,0:T(2,128)}, f32[2,192,2,2240]{3,2,1,0:T(2,128)}, f32[2,192,2,2240]{3,2,1,0:T(2,128)}, f32[2,192,2,2240]{3,2,1,0:T(2,128)}) custom-call(bf16[2,192,2,2240]{3,2,1,0:T(2,128)(2,1)} %weight.1, f32[2,192,2,2240]{3,2,1,0:T(2,128)} %first.1, f32[2,192,2,2240]{3,2,1,0:T(2,128)} %second.1, ...), custom_call_target="tpu_custom_call" | custom-call | tf_op jit(solution)/shard_map/pair_adam/pallas_call | solution.py:958
  792.2 8.8 %convert_subtract_fusion = (f32[2,2240,192]{1,2,0:T(8,128)}, f32[2,2240,192]{1,2,0:T(8,128)}, f32[2,2240,192]{1,2,0:T(8,128)}, f32[2,2240,192]{1,2,0:T(8,128)}) fusion(bf16[2,2240,192]{1,2,0:T(8,128)(2,1)S(1)} %copy-done.11, f32[2,2240,192]{1,2,0:T(8,128)} %param.53, f32[2,2240,192]{1,2,0:T(8,128)} %param.45, f32[1,192,1216]{2,1,0:T(8,128)S(1)} %bitcast.92, ...), kind=kLoop, calls=%fused_computation.5 | loop fusion | flops 16343040 | bytes 25804800 | tf_op jit(solution)/shard_map/sub | solution.py:927
  801.0 19.3 %all-reduce.5.cloned.1.call-done = (bf16[256,1536]{1,0:T(8,128)(2,1)}, bf16[256,1536]{1,0:T(8,128)(2,1)}) async-done(((bf16[256,1536]{1,0:T(8,128)(2,1)}, bf16[256,1536]{1,0:T(8,128)(2,1)}), (bf16[256,1536]{1,0:T(8,128)(2,1)}, bf16[256,1536]{1,0:T(8,128)(2,1)})) %all-reduce.5.cloned.1.call-update) | async-done | bytes 1572880 | tf_op jit(solution)/shard_map/psum | solution.py:1411
  820.3 3.0 fusion.33
  (151 shorter events, 18.8 us)
Async XLA Ops:
  7.2 8.6 %copy-start.7 = (bf16[1,512,1536]{2,1,0:T(8,128)(2,1)S(1)}, bf16[1,512,1536]{2,1,0:T(8,128)(2,1)}, u32[]{:S(2)}) copy-start(bf16[1,512,1536]{2,1,0:T(8,128)(2,1)} %param.27) | copy-start | bytes 4718596
  7.2 813.0 %all-reduce.5.cloned.1.call-start = ((), (), s32[]{:S(2)}) async-start(), calls=%async_computation | async-start | bytes 3145728 | tf_op jit(solution)/shard_map/psum | solution.py:1411
  429.4 4.5 copy-start.3
  437.9 89.4 %copy-start.29 = (f32[1536]{0:T(1024)S(1)}, f32[1536]{0:T(1024)}, u32[]{:S(2)}) copy-start(f32[1536]{0:T(1024)} %get-tuple-element.264) | copy-start | bytes 18436
  437.9 92.9 %copy-start.10 = (bf16[512,1536]{1,0:T(8,128)(2,1)S(1)}, bf16[512,1536]{1,0:T(8,128)(2,1)}, u32[]{:S(2)}) copy-start(bf16[512,1536]{1,0:T(8,128)(2,1)} %get-tuple-element.138) | copy-start | bytes 4718596
  574.2 60.1 %copy-start.31 = (f32[1536]{0:T(1024)S(1)}, f32[1536]{0:T(1024)}, u32[]{:S(2)}) copy-start(f32[1536]{0:T(1024)} %get-tuple-element.263) | copy-start | bytes 18436
  634.2 5.1 copy-start.34
  634.2 5.1 copy-start.6
  634.2 5.1 copy-start.12
  644.3 88.9 %copy-start.8 = (bf16[1,512,1536]{2,1,0:T(8,128)(2,1)S(1)}, bf16[1,512,1536]{2,1,0:T(8,128)(2,1)}, u32[]{:S(2)}) copy-start(bf16[1,512,1536]{2,1,0:T(8,128)(2,1)} %param.27) | copy-start | bytes 4718596
  644.3 88.9 %copy-start.30 = (f32[1536]{0:T(1024)S(1)}, f32[1536]{0:T(1024)}, u32[]{:S(2)}) copy-start(f32[1536]{0:T(1024)} %get-tuple-element.262) | copy-start | bytes 18436
  733.2 4.0 copy-start
  733.2 4.0 copy-start.1
  733.2 4.0 copy-start.2
  737.2 15.8 %copy-start.24 = (bf16[4,192,256]{2,1,0:T(8,128)(2,1)S(1)}, bf16[4,192,256]{2,1,0:T(8,128)(2,1)}, u32[]{:S(2)}) copy-start(bf16[4,192,256]{2,1,0:T(8,128)(2,1)} %get-tuple-element.171) | copy-start | bytes 1179652
  753.2 5.2 copy-start.33
  753.2 5.2 copy-start.36
  753.3 5.2 copy-start.38
  753.3 5.1 copy-start.39
  753.3 5.8 copy-start.37
  753.3 5.8 copy-start.40
  753.3 5.8 copy-start.41
  753.3 5.9 copy-start.19
  753.3 5.9 copy-start.20
  753.3 5.9 copy-start.25
  753.4 5.9 copy-start.27
  753.4 5.9 copy-start.28
  767.4 24.7 %copy-start.11 = (bf16[2,2240,192]{1,2,0:T(8,128)(2,1)S(1)}, bf16[2,2240,192]{1,2,0:T(8,128)(2,1)}, u32[]{:S(2)}) copy-start(bf16[2,2240,192]{1,2,0:T(8,128)(2,1)} %param.37) | copy-start | bytes 5160964
  767.4 24.7 %copy-start.14 = (f32[192,1216]{1,0:T(8,128)S(1)}, f32[192,1216]{1,0:T(8,128)}, u32[]{:S(2)}) copy-start(f32[192,1216]{1,0:T(8,128)} %get-tuple-element.182) | copy-start | bytes 2801668
  767.4 24.7 %copy-start.15 = (f32[192,1216]{1,0:T(8,128)S(1)}, f32[192,1216]{1,0:T(8,128)}, u32[]{:S(2)}) copy-start(f32[192,1216]{1,0:T(8,128)} %get-tuple-element.181) | copy-start | bytes 2801668
  767.4 24.7 %copy-start.16 = (f32[192,1024]{1,0:T(8,128)S(1)}, f32[192,1024]{1,0:T(8,128)}, u32[]{:S(2)}) copy-start(f32[192,1024]{1,0:T(8,128)} %get-tuple-element.180) | copy-start | bytes 2359300
  792.2 28.1 %copy-start.5 = (f32[512,1536]{1,0:T(8,128)S(1)}, f32[512,1536]{1,0:T(8,128)}, u32[]{:S(2)}) copy-start(f32[512,1536]{1,0:T(8,128)} %get-tuple-element.127) | copy-start | bytes 9437188
  (14 other events, 33.8 us)
Sparse Core Ops, SparseCore 0:
  752.0 68.2 all-reduce.4

commit v5 on v4

--- a/solution.py
+++ b/solution.py
@@ -201,7 +201,7 @@
 
 def scatter_sems(sizes):
     xs, ctxs = sizes[0] // 2 - 1, sizes[1] - 1
-    return 2 * (xs + 1) + (xs + ctxs) + 2 * xs * ctxs
+    return (xs + 1) * (ctxs + 2) + (xs + ctxs) + 2 * xs * ctxs
 
 
 def scatter_steps(place, sems, whole, out, mine, other, far_x, far_ctx, near):
@@ -214,23 +214,24 @@
     wide = lambda ref, *at: ref[at].astype(jnp.float32)
 
     def first():
+        order = [(step, turn) for step in xs for turn in ctxs]
+        order += [(0, turn) for turn in ctxs] + [(step, 0) for step in xs] + [(0, 0)]
+        for step, turn in order:
+            ctx = place.ctx_at(turn)
+            at = place.shard(place.x_at(step), 1 - place.core, ctx)
+            swaps[step, turn] = sems.remote(whole.at[at], other.at[step, ctx], place.to_core())
+            swaps[step, turn].start()
         for step in list(xs) + [0]:
-            to = place.x_at(step)
-            at = place.shard(to, 1 - place.core, 0)
-            swaps[step] = sems.remote(
-                whole.at[pl.ds(at, place.ctxs)], other.at[step], place.to_core()
-            )
-            swaps[step].start()
-            at = place.shard(to, place.core, 0)
+            at = place.shard(place.x_at(step), place.core, 0)
             loads[step] = sems.local(whole.at[pl.ds(at, place.ctxs)], mine.at[step])
             loads[step].start()
 
     def second():
         for step in xs:
             loads[step].wait()
-            swaps[step].wait_recv()
             for turn in ctxs:
                 ctx = place.ctx_at(turn)
+                swaps[step, turn].wait_recv()
 
                 def add(span):
                     total = wide(mine, step, ctx, span) + wide(other, step, ctx, span)
@@ -249,12 +250,12 @@
                         place.to_x(place.x_at(step)),
                     )
                     far[step, turn, 1].start()
+
+    def third():
         loads[0].wait()
-        swaps[0].wait_recv()
-
-    def third():
         for turn in ctxs:
             ctx = place.ctx_at(turn)
+            swaps[0, turn].wait_recv()
             if rows > cut:
                 for step in xs:
                     far[step, turn, 1].wait_recv()
@@ -278,6 +279,7 @@
             close["ctx", turn] = sems.remote(mine.at[0, ctx], near.at[slot], place.to_ctx(ctx))
             close["ctx", turn].start()
         for step in xs:
+            swaps[step, 0].wait_recv()
             for turn in ctxs:
                 far[step, turn, 0].wait_recv()
 
@@ -301,6 +303,7 @@
             close["x", step].start()
 
     def last():
+        swaps[0, 0].wait_recv()
         for copy in close.values():
             copy.wait_recv()
 
@@ -468,7 +471,7 @@
     pl.semaphore_wait(barrier, arrived)
 
 
-def transfer_kernel(sizes, counts, plan, work, *refs):
+def transfer_kernel(sizes, counts, layers, plan, work, *refs):
     z_count, g_count, s_count, p_count = counts
     refs = list(refs)
     given = 0 if work else z_count
@@ -488,11 +491,13 @@
     lines, planes = [], []
     parts = take(rest, 1) if work else take(ins, z_count)
     for part in parts:
-        lines.append(line_steps(place, sems, part, outs.pop(0), rest.pop(0), rest.pop(0)))
+        recv = rest.pop(0)
+        acc = part if work else rest.pop(0)
+        lines.append(line_steps(place, sems, part, outs.pop(0), recv, acc))
     shards = take(rest, len(work.shards)) if work else []
     made = take(rest, len(work.makes)) if work else []
     for index in range(g_count):
-        shard = shards[index] if index < len(shards) else ins.pop(0)
+        shard = shards[index] if index < len(shards) else ins.pop(0).at[layers[index]]
         planes.append(gather_steps(place, sems, shard, outs.pop(0)))
     for index in range(s_count):
         early = index < s_count - len(made)
@@ -553,10 +558,13 @@
     any_space = pl.BlockSpec(memory_space=pl.ANY)
     in_vmem = pl.BlockSpec(memory_space=pltpu.VMEM)
     given = () if work else z_sums
-    early, given_shards = len(scatters), gathers
+    early, given_shards = len(scatters), [array for array, _ in gathers]
+    layers = [layer for _, layer in gathers]
+    gathers = [jax.ShapeDtypeStruct(array.shape[1:], array.dtype) for array in given_shards]
     if work:
         z_sums = (work.part,)
         gathers = (*work.shards, *gathers)
+        layers = [None] * len(work.shards) + layers
         scatters = (*scatters, *work.makes)
     args = (*given, *given_shards, *scatters[:early], *line_pieces)
     in_specs = [in_vmem] * len(given) + [any_space] * (len(args) - len(given))
@@ -580,7 +588,7 @@
         out_shape += work.outputs
         scratch.append(pltpu.VMEM(work.part.shape, work.part.dtype))
     for a in z_sums:
-        scratch += [pltpu.VMEM(a.shape, a.dtype)] * 2
+        scratch += [pltpu.VMEM(a.shape, a.dtype)] * (1 if work else 2)
     if work:
         scratch += [pltpu.VMEM(a.shape, a.dtype) for a in (*work.shards, *work.makes)]
     for a in scatters:
@@ -597,7 +605,7 @@
     scratch += [pltpu.SemaphoreType.DMA((count,)), pltpu.SemaphoreType.DMA((count,))]
     counts = (len(z_sums), len(gathers), len(scatters), len(line_pieces))
     return pl.pallas_call(
-        functools.partial(transfer_kernel, sizes, counts, plan, work),
+        functools.partial(transfer_kernel, sizes, counts, layers, plan, work),
         out_shape=out_shape,
         in_specs=in_specs,
         out_specs=out_specs,
@@ -612,9 +620,6 @@
     )(*args)
 
 
-LATE_PIECES = 1
-
-
 def mm(lhs, rhs, over):
     return lax.dot_general(
         lhs, rhs, (((over[0],), (over[1],)), ((), ())), preferred_element_type=jnp.float32
@@ -646,6 +651,21 @@
         write(span, (values * scale * gain).astype(jnp.bfloat16))
 
 
+def normalize_back(rows, block, values_in, sums, gain, gain_grad, write):
+    gain_grad[...] = jnp.zeros_like(gain_grad)
+
+    @pl.loop(0, rows // block)
+    def _(index):
+        span = pl.ds(pl.multiple_of(index * block, block), block)
+        values = values_in[span, :].astype(jnp.float32)
+        grads = sums[span, :].astype(jnp.float32)
+        scale = lax.rsqrt(jnp.mean(values * values, axis=1, keepdims=True) + NORM_EPS)
+        weighted = grads * gain
+        inner_mean = jnp.mean(weighted * values, axis=1, keepdims=True)
+        gain_grad[...] += jnp.sum(grads * values * scale, axis=0, keepdims=True)
+        write(span, scale * weighted - values * (scale * scale * scale) * inner_mean)
+
+
 def attention_shard(layer, kv_head, query_weight, kv_weight, out_weight, shard):
     q_width = query_weight.shape[2]
     shard[:, pl.ds(0, q_width)] = query_weight[layer]
@@ -670,7 +690,7 @@
         query_weight, kv_weight, out_weight, gate_up_weight = ins[6:]
         queries, pairs, log_total, mixed, normed, w_attention, table = outs[:7]
         next_shards = outs[7:]
-        tables, shard = scratch
+        tables, shard, totals = scratch
         first_head = place.tensor * query_weight.shape[2] // HD // (H // KV)
         attention_shard(0, first_head, query_weight, kv_weight, out_weight, shard)
         here = place.shard(place.x, place.core, place.ctx)
@@ -694,6 +714,7 @@
         read = lambda span: x_in[span, :].astype(jnp.float32)
     else:
         middle, sums, table, w_attention, cosine, sine, query_segments, key_segments = ins
+        (totals,) = scratch
         queries, pairs, log_total, mixed, normed, x_out = outs
 
         def read(span):
@@ -736,6 +757,7 @@
         queries[:, columns] = turn_heads(lin[:, columns], cos, sin).astype(jnp.bfloat16)
     for copy in sent:
         copy.wait()
+    totals[...] = jnp.zeros_like(totals)
     for sequence in range(seq_count):
         span = pl.ds(sequence * local_len, local_len)
         allowed = allowed_pairs(
@@ -751,10 +773,11 @@
             exp_scores = jnp.exp(scores - row_max)
             row_total = jnp.sum(exp_scores, axis=1, keepdims=True)
             weights = (exp_scores / row_total).astype(jnp.bfloat16)
-            log_total[span, pl.ds(index, 1)] = row_max + jnp.log(row_total)
+            totals[span, pl.ds(index, 1)] = row_max + jnp.log(row_total)
             mixed[span, columns] = mm(weights, values, (1, 0)).astype(jnp.bfloat16)
     part[...] = mm(mixed[...], weight(q_width + 2 * HD, q_width), (1, 1)).astype(part.dtype)
     yield None
+    log_total[...] = totals[...].T[: log_total.shape[0], :]
     if layer == 0:
         for other in range(1, LAYERS):
             yield None
@@ -763,22 +786,31 @@
             split_pair(other, gate_up_weight, gate, up)
 
 
-def attend_back(seq_count, place, sems, ins, outs, scratch, part, in_grad, out_grad):
-    grad, normed, w_attention, cosine, sine, query_segments, key_segments = ins[:7]
-    queries, pairs, log_total, mixed = ins[7:]
-    (lin_grad,) = outs
+def attend_back(layer, seq_count, place, sems, ins, outs, scratch, part, out_grad, in_grad):
+    sums, middle, base, table, normed, w_attention, cosine, sine = ins[:8]
+    query_segments, key_segments, queries, pairs, log_total, mixed = ins[8:]
+    lin_grad, middle_grad, gain_grad = outs
     mixed_grad, pair_grad, got = scratch
+    grad = part
     rows = grad.shape[0]
     local_len = rows // seq_count
     q_width = queries.shape[1]
     heads = q_width // HD
     scale = HD ** (-0.5)
     yield [(0, 0), (1, 0)]
+
+    def write(span, back):
+        total = base[span, :].astype(jnp.float32) + back
+        middle_grad[span, :] = total
+        grad[span, :] = total.astype(grad.dtype)
+
+    gain = table[pl.ds(2 * layer + 1, 1), :]
+    normalize_back(rows, 64, middle, sums, gain, gain_grad, write)
     cos, sin = cosine[...], -sine[...]
     weight = lambda start, size: w_attention[:, :, pl.ds(start, size)].reshape(-1, size)
     w_out = weight(q_width + 2 * HD, q_width)
     mixed_grad[...] = mm(grad[...], w_out, (1, 0)).astype(jnp.bfloat16)
-    totals = log_total[...].T
+    totals = log_total[...]
     for sequence in range(seq_count):
         first = sequence * local_len
         span = pl.ds(first, local_len)
@@ -817,6 +849,8 @@
         sent.append(sems.remote(pair_grad.at[to], got.at[step - 1], place.to_ctx(to)))
         sent[-1].start()
     yield [(0, 1), (1, 1)]
+    product = mm(grad[...], mixed[...], (0, 0)).astype(out_grad.dtype)
+    out_grad[...] = product.reshape(out_grad.shape)
     total = pair_grad[place.ctx].astype(jnp.float32)
     for step, copy in enumerate(sent):
         copy.wait()
@@ -825,15 +859,8 @@
     lin_grad[:, pl.ds(q_width + HD, HD)] = total[:, HD:].astype(jnp.bfloat16)
     part[...] = mm(lin_grad[...], weight(0, q_width + 2 * HD), (1, 1)).astype(part.dtype)
     yield None
-    shard_rows = in_grad.shape[1]
-    width = normed.shape[1] // LATE_PIECES
-    for piece in range(LATE_PIECES):
-        columns = pl.ds(piece * width, width)
-        shards = pl.ds(piece * width // shard_rows, width // shard_rows)
-        for rows_in, grads_in, made in ((normed, lin_grad, in_grad), (grad, mixed, out_grad)):
-            product = mm(rows_in[:, columns], grads_in[...], (0, 0)).astype(made.dtype)
-            made[shards] = product.reshape(-1, *made.shape[1:])
-            yield None
+    product = mm(normed[...], lin_grad[...], (0, 0)).astype(in_grad.dtype)
+    in_grad[...] = product.reshape(in_grad.shape)
 
 
 def finish_kernel(sizes, *refs):
@@ -967,7 +994,7 @@
 
 
 TILE = 256
-DOWN_TILES = 4
+DOWN_TILES = 6
 
 
 def in_width(block, width):
@@ -1038,7 +1065,29 @@
     )(x_in, sums, table, w_gate, w_up, w_down)
 
 
-def backward_tile(
+def backward_tile(width, layer, *refs):
+    refs = list(refs)
+    if layer is None:
+        grad = refs.pop(0)
+    else:
+        base, values, sums, table = take(refs, 4)
+        *refs, grad_out, gain_grad, grad_t, n2_t, total, grad = refs
+        refs += [grad_t, n2_t, total]
+
+        @pl.when(pl.program_id(0) == 0)
+        def _():
+            def write(span, back):
+                made = base[span, :] + back
+                grad_out[span, :] = made
+                grad[span, :] = made.astype(grad.dtype)
+
+            gain = table[pl.ds(2 * layer, 1), :]
+            normalize_back(grad.shape[0], 64, values, sums, gain, gain_grad, write)
+
+    backward_work(width, grad, *refs)
+
+
+def backward_work(
     width,
     grad,
     n2,
@@ -1099,7 +1148,7 @@
         part_out[...] = total[...].astype(part_out.dtype)
 
 
-def backward_ffn(grad, n2, gate, up, inner, w_gate, w_up, w_down):
+def backward_ffn(grad, n2, gate, up, inner, w_gate, w_up, w_down, layer=None):
     rows, model_width = n2.shape
     width = w_gate.shape[1]
     whole = pl.BlockSpec((rows, model_width), lambda j: (0, 0))
@@ -1107,28 +1156,41 @@
     units = pl.BlockSpec((rows, TILE), lambda j: (0, j))
     like = lambda size: jax.ShapeDtypeStruct((model_width, size), jnp.bfloat16)
     cut = DOWN_TILES * TILE
+    scratch = [
+        pltpu.VMEM((model_width, rows), jnp.bfloat16),
+        pltpu.VMEM((model_width, rows), jnp.bfloat16),
+        pltpu.VMEM((rows, model_width), jnp.float32),
+    ]
+    grads, given, made, made_shapes = [grad], [whole], [], []
+    if layer is not None:
+        grads = grad
+        table_block = pl.BlockSpec(grad[3].shape, lambda j: (0, 0))
+        given = [whole, whole, whole, table_block]
+        made = [whole, pl.BlockSpec((1, model_width), lambda j: (0, 0))]
+        made_shapes = [
+            jax.ShapeDtypeStruct((rows, model_width), jnp.float32),
+            jax.ShapeDtypeStruct((1, model_width), jnp.float32),
+        ]
+        scratch.append(pltpu.VMEM((rows, model_width), jnp.bfloat16))
     before = pl.BlockSpec((model_width, TILE), lambda j: (0, jnp.minimum(j, DOWN_TILES - 1)))
     behind = pl.BlockSpec((model_width, TILE), lambda j: (0, jnp.maximum(j - DOWN_TILES, 0)))
     return pl.pallas_call(
-        functools.partial(backward_tile, width),
+        functools.partial(backward_tile, width, layer),
         grid=(pl.cdiv(width, TILE),),
-        in_specs=[whole, whole, units, units, units, weight, weight, weight],
-        out_specs=[before, behind, weight, weight, whole],
+        in_specs=given + [whole, units, units, units, weight, weight, weight],
+        out_specs=[before, behind, weight, weight, whole] + made,
         out_shape=[
             like(cut),
             like(width - cut),
             like(width),
             like(width),
             jax.ShapeDtypeStruct((rows, model_width), jnp.bfloat16),
-        ],
-        scratch_shapes=[
-            pltpu.VMEM((model_width, rows), jnp.bfloat16),
-            pltpu.VMEM((model_width, rows), jnp.bfloat16),
-            pltpu.VMEM((rows, model_width), jnp.float32),
-        ],
+        ]
+        + made_shapes,
+        scratch_shapes=scratch,
         compiler_params=pltpu.CompilerParams(vmem_limit_bytes=56 << 20),
         name="backward_ffn",
-    )(grad, n2, gate, up, inner, w_gate, w_up, w_down)
+    )(*grads, n2, gate, up, inner, w_gate, w_up, w_down)
 
 
 def rotate(values, cosine, sine):
@@ -1189,7 +1251,7 @@
     def move(**what):
         return transfer(sizes, next(numbers), **what)
 
-    down_shards = [down_weight[layer].T for layer in range(LAYERS)]
+    down_shards = down_weight.transpose(0, 2, 1)
 
     def after(array, *earlier):
         return lax.optimization_barrier((array, *earlier))[0]
@@ -1235,7 +1297,7 @@
         outputs = [
             jax.ShapeDtypeStruct((row_count, q_width), low),
             jax.ShapeDtypeStruct((ctxs, row_count, 2 * HD), low),
-            jax.ShapeDtypeStruct((row_count, HD), wide),
+            jax.ShapeDtypeStruct((-(-heads_here // 8) * 8, row_count), wide),
             jax.ShapeDtypeStruct((row_count, q_width), low),
             jax.ShapeDtypeStruct((row_count, model_width), low),
         ]
@@ -1253,6 +1315,7 @@
                 [
                     pltpu.VMEM((n, *own_table.shape), wide),
                     pltpu.VMEM(attention_shard.shape, low),
+                    pltpu.VMEM((row_count, HD), wide),
                 ],
                 n + gather_sems(sizes) + ctxs,
                 jax.ShapeDtypeStruct((row_count, model_width), low),
@@ -1260,7 +1323,7 @@
                 whole_plane=True,
             )
             total, *moved = move(
-                work=work, gathers=[down_shards[0]], plan=((8, 14), (12, 18), (14, 99))
+                work=work, gathers=[(down_shards, 0)], plan=((8, 14), (12, 18), (14, 99))
             )
             w_gate, w_up, down_weights = moved[:3]
             queries, pairs, log_total, mixed_low, normed, w_attention, table = moved[3:10]
@@ -1271,13 +1334,13 @@
                 functools.partial(attend, layer, seq_count),
                 [middle, total, table, w_attention, *sides],
                 outputs,
-                [],
+                [pltpu.VMEM((row_count, HD), wide)],
                 ctxs,
                 jax.ShapeDtypeStruct((row_count, model_width), low),
             )
             total, w_gate, w_up, queries, pairs, log_total, mixed_low, normed, hidden = move(
                 work=work,
-                gathers=later_shards[3 * layer - 2 : 3 * layer],
+                gathers=[(shard[None], 0) for shard in later_shards[3 * layer - 2 : 3 * layer]],
                 plan=((8, 14), (12, 18)),
             )
         w_gate, w_up, w_down = [
@@ -1308,7 +1371,7 @@
         if layer + 1 < LAYERS:
             total, w_attention, down_weights = move(
                 z_sums=[part],
-                gathers=[later_shards[3 * layer], down_shards[layer + 1]],
+                gathers=[(later_shards[3 * layer][None], 0), (down_shards, layer + 1)],
                 plan=((8, 15), (13, 18)),
             )
         else:
@@ -1317,7 +1380,8 @@
     def split(gradient):
         return gradient.astype(low).reshape(n, shard_rows, gradient.shape[1])
 
-    grad_hidden = out_grad.astype(wide).reshape(row_count, model_width)
+    grad_hidden = out_grad.reshape(row_count, model_width)
+    total = None
     done = [{} for _ in range(LAYERS)]
     small_grads = [None] * LAYERS
     for layer in reversed(range(LAYERS)):
@@ -1338,21 +1402,27 @@
             w_up,
             w_down,
         ) = stored[layer]
-        grad_low = grad_hidden.astype(low)
-        *ffn_grads, part = backward_ffn(
-            grad_low, normed_two, gate, up, inner_low, w_gate, w_up, w_down
-        )
+        if layer + 1 == LAYERS:
+            *ffn_grads, part = backward_ffn(
+                grad_hidden, normed_two, gate, up, inner_low, w_gate, w_up, w_down
+            )
+        else:
+            above = (grad_middle, above_input, total, table)
+            *ffn_grads, part, grad_hidden, gain_grad = backward_ffn(
+                above, normed_two, gate, up, inner_low, w_gate, w_up, w_down, layer + 1
+            )
+            small_grads[layer + 1].insert(0, gain_grad[0])
         down_first, down_rest, grad_gate_w, grad_up_w = (split(grad) for grad in ffn_grads)
         total, done[layer]["gate"], done[layer]["down_first"] = move(
             z_sums=[part], scatters=[grad_gate_w, down_first], plan=((2, 9), (3, 11))
         )
-        back_two, grad_gain_two = norm_back(middle, table[2 * layer + 1], total.astype(wide))
-        grad_middle = grad_hidden + back_two
-        grad_mid_low = grad_middle.astype(low)
         work = Work(
-            functools.partial(attend_back, seq_count),
+            functools.partial(attend_back, layer, seq_count),
             [
-                grad_mid_low,
+                total,
+                middle,
+                grad_hidden,
+                table,
                 normed,
                 w_attention,
                 cos_wide,
@@ -1364,7 +1434,11 @@
                 log_total,
                 mixed_low,
             ],
-            [jax.ShapeDtypeStruct((row_count, q_width + 2 * HD), low)],
+            [
+                jax.ShapeDtypeStruct((row_count, q_width + 2 * HD), low),
+                jax.ShapeDtypeStruct((row_count, model_width), wide),
+                jax.ShapeDtypeStruct((1, model_width), wide),
+            ],
             [
                 pltpu.VMEM((row_count, q_width), low),
                 pltpu.VMEM((ctxs, row_count, 2 * HD), low),
@@ -1373,32 +1447,31 @@
             ctxs,
             jax.ShapeDtypeStruct((row_count, model_width), low),
             [
+                jax.ShapeDtypeStruct((n, shard_rows, q_width), low),
                 jax.ShapeDtypeStruct((n, shard_rows, q_width + 2 * HD), low),
-                jax.ShapeDtypeStruct((n, shard_rows, q_width), low),
             ],
         )
         extra = [kv_part] if layer + 1 < LAYERS else []
-        total, *results, grad_lin = move(
+        total, *results, grad_lin, grad_middle, gain_grad = move(
             work=work,
             line_pieces=extra,
             scatters=[grad_up_w, down_rest],
-            plan=((-1, 4), (-1, 6), (6, 10), (6, 10)),
+            plan=((-1, 2), (-1, 4), (3, 13), (3, 13)),
         )
-        for name, result in zip(("up", "down_rest", "in", "out"), results):
+        for name, result in zip(("up", "down_rest", "out", "in"), results):
             done[layer][name] = result
         done[layer]["lin"] = grad_lin
         kv_part = done[layer]["in"][:, q_width:].astype(low)
         if extra:
             done[layer + 1]["kv"] = results[-1]
-        back_one, grad_gain_one = norm_back(
-            layer_input.astype(wide), table[2 * layer], total.astype(wide)
-        )
-        small_grads[layer] = [grad_gain_one, grad_gain_two]
-        grad_hidden = grad_middle + back_one
+        small_grads[layer] = [gain_grad[0]]
+        above_input = layer_input
         if layer + 1 == LAYERS:
-            half = row_count // 2
-            last_totals = [lax.psum(after(last_part[:half], total), "tensor")]
-
+            last_total = lax.psum(after(last_part, total), "tensor")
+
+    back_one, grad_gain_one = norm_back(above_input.astype(wide), table[0], total.astype(wide))
+    small_grads[0].insert(0, grad_gain_one)
+    grad_hidden = grad_middle + back_one
     sums, kv_parts = finish(
         sizes,
         next(numbers),
@@ -1408,8 +1481,7 @@
     )
     done[0]["kv"] = kv_parts
     cut = lambda a, size: lax.dynamic_slice_in_dim(a, shard * size, size, a.ndim - 1)
-    last_totals.append(lax.psum(after(last_part[half:], sums), "tensor"))
-    last_total = jnp.concatenate([after(last_totals[0], sums), last_totals[1]])
+    last_total = after(last_total, sums)
     block_out = (stored[-1][6] + last_total.astype(wide)).astype(low)
     block_out = block_out.reshape(seq_count, local_len, model_width)
     input_grad = grad_hidden.reshape(seq_count, local_len, model_width)

time: 840 us -> 785 us (0.935)
  other arithmetic: 63.6 us -> 32.5 us
  waiting for transfers between devices: 19.3 us -> 0.02 us
    psum x1, waiting for transfers between devices: 19.3 us -> 0.01 us  [local(): last_total = lax.psum(after(last_part, total), 'tensor')]
    convert_element_type x3 -> x0, other arithmetic: 14 us -> none  [the longest x2 8.94 us: local(): grad_mid_low = grad_middle.astype(low)]
    reduce_sum x3 -> x0, other arithmetic: 10.4 us -> none  [norm_back(): return (grad_values, jnp.sum(grad_rows * values * norm_scale, axis=0))]
  transfers between devices with their start and end apart: 1 -> 1, of which waited for: 1 -> 0; matrix products, arithmetic and copies ran while one was open for 3% -> 3% of each run, Pallas kernels for 3% -> 30%
where the time goes in v5:
time: 785 us; the launch traced here: 775 us
  Pallas kernels  718 us (91%)
  other arithmetic  32.5 us (4%)
  between operations  15.2 us (2%)
  local copies, waits for them, and re-layouts  9.49 us (1%)
    pallas_call x7, Pallas kernels, transfer(): pl.pallas_call(functools.partial(transfer_kernel, sizes, counts, layers,...  551 us
    pallas_call x2, Pallas kernels, backward_ffn(): pl.pallas_call(functools.partial(backward_tile, width, layer), grid=(pl.c...  81.3 us
    pallas_call x2, Pallas kernels, forward_ffn(): pl.pallas_call(functools.partial(forward_tile, width, layer), grid=(pl.cd...  49.6 us
    pallas_call x1, Pallas kernels, pair_adam(): pl.pallas_call(functools.partial(pair_adam_block, step_rate), grid=(layer...  24.7 us
  transfers between devices with their start and end apart: 1, of which 0 were waited for; matrix products, arithmetic and copies ran while one was open for 3% of the time, Pallas kernels for 30%

profile of v5, /device:TPU:0, one launch (start us, length us, event | category | flops | bytes accessed | tf_op | source)
XLA Modules:
  0.0 775.3 jit_solution(15381894284687567924)
XLA Ops:
  7.3 0.7 constant_dynamic-slice_fusion.3.refs_10_.refs_11_
  8.0 0.7 fusion.40
  9.3 0.7 copy_convert_fusion
  10.1 0.7 convert_element_type.93
  11.0 1.0 convert_reduce_fusion
  12.1 0.9 copy.75.refs_5_.refs_8_
  12.9 1.7 copy.77.refs_11_.refs_12_
  14.6 1.0 fusion.22
  16.5 1.0 pad_maximum_fusion.3
  17.5 124.6 %transfer1.1 = (bf16[512,1536]{1,0:T(8,128)(2,1)}, bf16[8,192,2240]{2,1,0:T(8,128)(2,1)}, bf16[8,192,2240]{2,1,0:T(8,128)(2,1)}, bf16[8,192,2240]{2,1,0:T(8,128)...) custom-call(bf16[2,192,2240]{2,1,0:T(8,128)(2,1)} %bitcast.81, ...), custom_call_target="tpu_custom_call" | custom-call | flops 30000001024 | bytes 150000000 | tf_op jit(solution)/shard_map/transfer1/pallas_call | solution.py:607
  142.0 24.7 %forward_ffn.2 = (f32[512,1536]{1,0:T(8,128)}, bf16[512,1536]{1,0:T(8,128)(2,1)}, f32[512,2240]{1,0:T(8,128)}, f32[512,2240]{1,0:T(8,128)}, bf16[512,2240]{1,0:T(8,128)(2,1)}, /*index=5*/bf16[512,1536]{1,0:T(8,128)(2,1)}) custom-call(bf16[512,1536]{1,0:T(8,128)(2,1)} %bitcast.80, bf16[512,1536]{1,0:T(8,128)(2,1)} %get-tuple-element.117.sums, ...), custom_call_target="tpu_custom_call" | custom-call | tf_op jit(solution)/shard_map/forward_ffn/pallas_call | solution.py:1049
  166.8 53.1 %transfer2.1 = (bf16[512,1536]{1,0:T(8,128)(2,1)}, bf16[8,192,1024]{2,1,0:T(8,128)(2,1)}, bf16[8,192,2240]{2,1,0:T(8,128)(2,1)}) custom-call(bf16[512,1536]{1,0:T(8,128)(2,1)} %get-tuple-element.123.refs_0_, bf16[1,192,1024]{2,1,0:T(8,128)(2,1)} %bitcast.107, bf16[2,192,2240]{2,1,0:T(8,128)(2,1)} %bitcast.82), custom_call_target="tpu_custom_call" | custom-call | flops 30000001024 | bytes 150000000 | tf_op jit(solution)/shard_map/transfer2/pallas_call | solution.py:607
  219.9 77.9 %transfer3.1 = (bf16[512,1536]{1,0:T(8,128)(2,1)}, bf16[8,192,2240]{2,1,0:T(8,128)(2,1)}, bf16[8,192,2240]{2,1,0:T(8,128)(2,1)}, bf16[512,384]{1,0:T(8,128)(2,1)...) custom-call(bf16[1,192,2240]{2,1,0:T(8,128)(2,1)} %bitcast.105, ...), custom_call_target="tpu_custom_call" | custom-call | flops 30000001024 | bytes 150000000 | tf_op jit(solution)/shard_map/transfer3/pallas_call | solution.py:607
  297.8 24.9 %forward_ffn.3 = (f32[512,1536]{1,0:T(8,128)}, bf16[512,1536]{1,0:T(8,128)(2,1)}, f32[512,2240]{1,0:T(8,128)}, f32[512,2240]{1,0:T(8,128)}, bf16[512,2240]{1,0:T(8,128)(2,1)}, /*index=5*/bf16[512,1536]{1,0:T(8,128)(2,1)}) custom-call(f32[512,1536]{1,0:T(8,128)} %get-tuple-element.127.x_in.refs_1_, bf16[512,1536]{1,0:T(8,128)(2,1)} %get-tuple-element.128.sums, ...), custom_call_target="tpu_custom_call" | custom-call | tf_op jit(solution)/shard_map/forward_ffn/pallas_call | solution.py:1049
  322.7 38.0 %backward_ffn.2 = (bf16[1536,1536]{1,0:T(8,128)(2,1)}, bf16[1536,704]{1,0:T(8,128)(2,1)}, bf16[1536,2240]{1,0:T(8,128)(2,1)}, bf16[1536,2240]{1,0:T(8,128)(2,1)}, bf16[512,1536]{1,0:T(8,128)(2,1)}) custom-call(bf16[512,1536]{1,0:T(8,128)(2,1)} %bitcast.83, bf16[512,1536]{1,0:T(8,128)(2,1)} %get-tuple-element.134.refs_1_, ...), custom_call_target="tpu_custom_call" | custom-call | tf_op jit(solution)/shard_map/backward_ffn/pallas_call | solution.py:1177
  360.7 61.9 %transfer4.1 = (bf16[512,1536]{1,0:T(8,128)(2,1)}, f32[192,2240]{1,0:T(8,128)}, f32[192,1536]{1,0:T(8,128)}) custom-call(bf16[512,1536]{1,0:T(8,128)(2,1)} %get-tuple-element.140.refs_0_, bf16[8,192,2240]{2,1,0:T(8,128)(2,1)} %bitcast.100, bf16[8,192,1536]{2,1,0:T(8,128)(2,1)} %bitcast.102), custom_call_target="tpu_custom_call" | custom-call | flops 30000001024 | bytes 150000000 | tf_op jit(solution)/shard_map/transfer4/pallas_call | solution.py:607
  422.6 77.6 %transfer5.1 = (bf16[512,1536]{1,0:T(8,128)(2,1)}, f32[192,2240]{1,0:T(8,128)}, f32[192,704]{1,0:T(8,128)}, f32[192,384]{1,0:T(8,128)}, f32[192,640]{1,0:T(8,128...) custom-call(bf16[8,192,2240]{2,1,0:T(8,128)(2,1)} %bitcast.98, ...), custom_call_target="tpu_custom_call" | custom-call | flops 30000001024 | bytes 150000000 | tf_op jit(solution)/shard_map/transfer5/pallas_call | solution.py:607
  500.3 0.9 slice_reduce_fusion
  502.2 43.2 %backward_ffn.3 = (bf16[1536,1536]{1,0:T(8,128)(2,1)}, bf16[1536,704]{1,0:T(8,128)(2,1)}, bf16[1536,2240]{1,0:T(8,128)(2,1)}, bf16[1536,2240]{1,0:T(8,128)(2,1)}...) custom-call(f32[512,1536]{1,0:T(8,128)} %get-tuple-element.151.refs_0_, ...), custom_call_target="tpu_custom_call" | custom-call | tf_op jit(solution)/shard_map/backward_ffn/pallas_call | solution.py:1177
  545.5 77.3 %transfer6.1 = (bf16[512,1536]{1,0:T(8,128)(2,1)}, f32[192,2240]{1,0:T(8,128)}, f32[192,1536]{1,0:T(8,128)}) custom-call(bf16[512,1536]{1,0:T(8,128)(2,1)} %get-tuple-element.159.refs_0_, bf16[8,192,2240]{2,1,0:T(8,128)(2,1)} %bitcast.99, bf16[8,192,1536]{2,1,0:T(8,128)(2,1)} %bitcast.101), custom_call_target="tpu_custom_call" | custom-call | flops 30000001024 | bytes 150000000 | tf_op jit(solution)/shard_map/transfer6/pallas_call | solution.py:607
  622.8 78.2 %transfer7.1 = (bf16[512,1536]{1,0:T(8,128)(2,1)}, f32[192,2240]{1,0:T(8,128)}, f32[192,704]{1,0:T(8,128)}, f32[192,384]{1,0:T(8,128)}, f32[192,640]{1,0:T(8,128...) custom-call(bf16[8,192,2240]{2,1,0:T(8,128)(2,1)} %bitcast.97, ...), custom_call_target="tpu_custom_call" | custom-call | flops 30000001024 | bytes 150000000 | tf_op jit(solution)/shard_map/transfer7/pallas_call | solution.py:607
  701.0 2.6 fusion.11
  703.8 12.0 %finish.1 = (f32[8,1536]{1,0:T(8,128)S(1)}, bf16[4,192,256]{2,1,0:T(8,128)(2,1)S(1)}) custom-call(f32[1,1536]{1,0:T(1,128)S(1)} %broadcast_in_dim.34.refs_0_, f32[1,1536]{1,0:T(1,128)S(1)} %copy-done.5, f32[1,1536]{1,0:T(1,128)S(1)} %copy-done.4, f32[1,1536]{1,0:T(1,128)S(1)} %copy-done.3, bf16[512,640]{1,0:T(8,128)(2,1)S(1)} %copy-done.2, ...), custom_call_target="tpu_custom_call" | custom-call | tf_op jit(solution)/shard_map/finish/pallas_call | solution.py:928
  716.0 1.2 add_bitcast_fusion.1
  717.3 0.7 copy-done.9
  718.1 4.1 fusion.6
  723.0 1.6 convert_subtract_fusion.3
  724.7 1.9 convert_subtract_fusion.1
  726.9 1.5 convert_subtract_fusion.2
  731.4 24.7 %pair_adam.1 = (f32[2,192,2,2240]{3,2,1,0:T(2,128)}, f32[2,192,2,2240]{3,2,1,0:T(2,128)}, f32[2,192,2,2240]{3,2,1,0:T(2,128)}, f32[2,192,2,2240]{3,2,1,0:T(2,128)}) custom-call(bf16[2,192,2,2240]{3,2,1,0:T(2,128)(2,1)} %weight.1, f32[2,192,2,2240]{3,2,1,0:T(2,128)} %first.1, f32[2,192,2,2240]{3,2,1,0:T(2,128)} %second.1, ...), custom_call_target="tpu_custom_call" | custom-call | tf_op jit(solution)/shard_map/pair_adam/pallas_call | solution.py:985
  756.1 8.0 %convert_subtract_fusion = (f32[2,2240,192]{1,2,0:T(8,128)}, f32[2,2240,192]{1,2,0:T(8,128)}, f32[2,2240,192]{1,2,0:T(8,128)}, f32[2,2240,192]{1,2,0:T(8,128)}) fusion(bf16[2,2240,192]{1,2,0:T(8,128)(2,1)} %param.37, f32[2,2240,192]{1,2,0:T(8,128)S(1)} %copy-done.7, f32[2,2240,192]{1,2,0:T(8,128)S(1)} %copy-done.8, f32[1,192,704]{2,1,0:T(8,128)} %bitcast.87, ...), kind=kLoop, calls=%fused_computation.5 | loop fusion | flops 16343040 | bytes 25804800 | tf_op jit(solution)/shard_map/sub | solution.py:954
  764.1 4.0 fusion.12
  (109 shorter events, 7.2 us)
Async XLA Ops:
  7.2 756.9 %all-reduce.4.cloned.1.call-start = ((), (), s32[]{:S(2)}) async-start(), calls=%async_computation | async-start | bytes 3145728 | tf_op jit(solution)/shard_map/psum | solution.py:1470
  8.0 134.1 %copy-start.24 = (s32[1,512]{1,0:T(1,128)}, s32[1,512]{1,0:T(1,128)S(1)}, u32[]{:S(2)}) copy-start(s32[1,512]{1,0:T(1,128)S(1)} %constant_dynamic-slice_fusion.3.refs_10_.refs_11_) | copy-start | bytes 6148
  422.6 78.6 %copy-start.6 = (bf16[1,512,1536]{2,1,0:T(8,128)(2,1)S(1)}, bf16[1,512,1536]{2,1,0:T(8,128)(2,1)}, u32[]{:S(2)}) copy-start(bf16[1,512,1536]{2,1,0:T(8,128)(2,1)} %param.27) | copy-start | bytes 4718596
  701.0 2.7 copy-start
  701.0 2.7 copy-start.1
  701.0 2.7 copy-start.2
  701.0 2.7 copy-start.3
  701.0 2.7 copy-start.4
  701.0 2.7 copy-start.5
  716.0 6.4 copy-start.23
  716.0 2.1 copy-start.9
  718.0 4.2 copy-start.26
  718.0 4.2 copy-start.29
  718.0 4.2 copy-start.30
  718.1 4.3 copy-start.25
  718.1 4.3 copy-start.27
  718.1 4.3 copy-start.28
  718.1 4.9 copy-start.13
  718.1 4.9 copy-start.14
  718.1 4.9 copy-start.19
  722.2 2.4 copy-start.11
  722.2 2.4 copy-start.12
  722.2 2.4 copy-start.17
  724.7 2.0 copy-start.15
  724.7 2.0 copy-start.16
  724.7 2.0 copy-start.20
  724.7 2.0 copy-start.21
  724.7 2.1 copy-start.22
  726.7 1.7 copy-start.33
  731.4 24.7 %copy-start.7 = (f32[2,2240,192]{1,2,0:T(8,128)S(1)}, f32[2,2240,192]{1,2,0:T(8,128)}, u32[]{:S(2)}) copy-start(f32[2,2240,192]{1,2,0:T(8,128)} %param.53) | copy-start | bytes 10321924
  731.4 24.7 %copy-start.8 = (f32[2,2240,192]{1,2,0:T(8,128)S(1)}, f32[2,2240,192]{1,2,0:T(8,128)}, u32[]{:S(2)}) copy-start(f32[2,2240,192]{1,2,0:T(8,128)} %param.45) | copy-start | bytes 10321924
  731.4 24.7 %copy-start.10 = (f32[192,1536]{1,0:T(8,128)S(1)}, f32[192,1536]{1,0:T(8,128)}, u32[]{:S(2)}) copy-start(f32[192,1536]{1,0:T(8,128)} %get-tuple-element.190) | copy-start | bytes 3538948
  (3 other events, 4.8 us)
Sparse Core Ops, SparseCore 0:
  500.4 81.1 all-reduce.3

commit v6 on v5

--- a/solution.py
+++ b/solution.py
@@ -1375,7 +1375,8 @@
                 plan=((8, 15), (13, 18)),
             )
         else:
-            last_part = part
+            last_part, half = part, row_count // 2
+            last_first = lax.psum(last_part[:half], "tensor")
 
     def split(gradient):
         return gradient.astype(low).reshape(n, shard_rows, gradient.shape[1])
@@ -1416,6 +1417,8 @@
         total, done[layer]["gate"], done[layer]["down_first"] = move(
             z_sums=[part], scatters=[grad_gate_w, down_first], plan=((2, 9), (3, 11))
         )
+        if layer + 2 >= LAYERS:
+            normed = after(normed, last_first if layer + 1 == LAYERS else last_rest)
         work = Work(
             functools.partial(attend_back, layer, seq_count),
             [
@@ -1467,7 +1470,7 @@
         small_grads[layer] = [gain_grad[0]]
         above_input = layer_input
         if layer + 1 == LAYERS:
-            last_total = lax.psum(after(last_part, total), "tensor")
+            last_rest = lax.psum(after(last_part[half:], total), "tensor")
 
     back_one, grad_gain_one = norm_back(above_input.astype(wide), table[0], total.astype(wide))
     small_grads[0].insert(0, grad_gain_one)
@@ -1481,7 +1484,7 @@
     )
     done[0]["kv"] = kv_parts
     cut = lambda a, size: lax.dynamic_slice_in_dim(a, shard * size, size, a.ndim - 1)
-    last_total = after(last_total, sums)
+    last_total = after(jnp.concatenate([last_first, last_rest]), sums)
     block_out = (stored[-1][6] + last_total.astype(wide)).astype(low)
     block_out = block_out.reshape(seq_count, local_len, model_width)
     input_grad = grad_hidden.reshape(seq_count, local_len, model_width)

time: 785 us -> 767 us (0.977)
  Pallas kernels: 718 us -> 701 us
    pallas_call x7, Pallas kernels: 551 us -> 534 us  [transfer(): pl.pallas_call(functools.partial(transfer_kernel, sizes, counts, layers,...]
  transfers between devices with their start and end apart: 1 -> 2, of which waited for: 0 -> 0; matrix products, arithmetic and copies ran while one was open for 3% -> 1% of each run, Pallas kernels for 30% -> 27%
where the time goes in v6:
time: 767 us; the launch traced here: 758 us
  Pallas kernels  701 us (91%)
  other arithmetic  29.2 us (4%)
  between operations  15 us (2%)
  local copies, waits for them, and re-layouts  12.6 us (2%)
    pallas_call x7, Pallas kernels, transfer(): pl.pallas_call(functools.partial(transfer_kernel, sizes, counts, layers,...  534 us
    pallas_call x2, Pallas kernels, backward_ffn(): pl.pallas_call(functools.partial(backward_tile, width, layer), grid=(pl.c...  81.1 us
    pallas_call x2, Pallas kernels, forward_ffn(): pl.pallas_call(functools.partial(forward_tile, width, layer), grid=(pl.cd...  49.6 us
    pallas_call x1, Pallas kernels, pair_adam(): pl.pallas_call(functools.partial(pair_adam_block, step_rate), grid=(layer...  24.7 us
  transfers between devices with their start and end apart: 2, of which 0 were waited for; matrix products, arithmetic and copies ran while one was open for 1% of the time, Pallas kernels for 27%

profile of v6, /device:TPU:0, one launch (start us, length us, event | category | flops | bytes accessed | tf_op | source)
XLA Modules:
  0.0 757.9 jit_solution(877855906396454354)
XLA Ops:
  7.3 0.7 constant_dynamic-slice_fusion.3.refs_10_.refs_11_
  8.0 0.7 fusion.41
  10.1 0.7 convert_element_type.93
  11.0 1.0 convert_reduce_fusion
  12.1 0.9 copy.75.refs_5_.refs_8_
  12.9 1.0 fusion.22
  14.8 1.0 pad_maximum_fusion.4
  15.8 124.6 %transfer1.1 = (bf16[512,1536]{1,0:T(8,128)(2,1)}, bf16[8,192,2240]{2,1,0:T(8,128)(2,1)}, bf16[8,192,2240]{2,1,0:T(8,128)(2,1)}, bf16[8,192,2240]{2,1,0:T(8,128)...) custom-call(bf16[2,192,2240]{2,1,0:T(8,128)(2,1)} %bitcast.81, ...), custom_call_target="tpu_custom_call" | custom-call | flops 30000001024 | bytes 150000000 | tf_op jit(solution)/shard_map/transfer1/pallas_call | solution.py:607
  140.3 24.7 %forward_ffn.2 = (f32[512,1536]{1,0:T(8,128)}, bf16[512,1536]{1,0:T(8,128)(2,1)}, f32[512,2240]{1,0:T(8,128)}, f32[512,2240]{1,0:T(8,128)}, bf16[512,2240]{1,0:T(8,128)(2,1)}, /*index=5*/bf16[512,1536]{1,0:T(8,128)(2,1)}) custom-call(bf16[512,1536]{1,0:T(8,128)(2,1)} %bitcast.80, bf16[512,1536]{1,0:T(8,128)(2,1)} %get-tuple-element.119.sums, ...), custom_call_target="tpu_custom_call" | custom-call | tf_op jit(solution)/shard_map/forward_ffn/pallas_call | solution.py:1049
  165.0 53.1 %transfer2.1 = (bf16[512,1536]{1,0:T(8,128)(2,1)}, bf16[8,192,1024]{2,1,0:T(8,128)(2,1)}, bf16[8,192,2240]{2,1,0:T(8,128)(2,1)}) custom-call(bf16[512,1536]{1,0:T(8,128)(2,1)} %get-tuple-element.125.refs_0_, bf16[1,192,1024]{2,1,0:T(8,128)(2,1)} %bitcast.107, bf16[2,192,2240]{2,1,0:T(8,128)(2,1)} %bitcast.82), custom_call_target="tpu_custom_call" | custom-call | flops 30000001024 | bytes 150000000 | tf_op jit(solution)/shard_map/transfer2/pallas_call | solution.py:607
  218.2 78.0 %transfer3.1 = (bf16[512,1536]{1,0:T(8,128)(2,1)}, bf16[8,192,2240]{2,1,0:T(8,128)(2,1)}, bf16[8,192,2240]{2,1,0:T(8,128)(2,1)}, bf16[512,384]{1,0:T(8,128)(2,1)...) custom-call(bf16[1,192,2240]{2,1,0:T(8,128)(2,1)} %bitcast.105, ...), custom_call_target="tpu_custom_call" | custom-call | flops 30000001024 | bytes 150000000 | tf_op jit(solution)/shard_map/transfer3/pallas_call | solution.py:607
  296.1 24.9 %forward_ffn.3 = (f32[512,1536]{1,0:T(8,128)}, bf16[512,1536]{1,0:T(8,128)(2,1)}, f32[512,2240]{1,0:T(8,128)}, f32[512,2240]{1,0:T(8,128)}, bf16[512,2240]{1,0:T(8,128)(2,1)}, /*index=5*/bf16[512,1536]{1,0:T(8,128)(2,1)}) custom-call(f32[512,1536]{1,0:T(8,128)} %get-tuple-element.129.x_in.refs_1_, bf16[512,1536]{1,0:T(8,128)(2,1)} %get-tuple-element.130.sums, ...), custom_call_target="tpu_custom_call" | custom-call | tf_op jit(solution)/shard_map/forward_ffn/pallas_call | solution.py:1049
  321.0 2.6 fusion.36
  323.7 38.0 %backward_ffn.2 = (bf16[1536,1536]{1,0:T(8,128)(2,1)}, bf16[1536,704]{1,0:T(8,128)(2,1)}, bf16[1536,2240]{1,0:T(8,128)(2,1)}, bf16[1536,2240]{1,0:T(8,128)(2,1)}, bf16[512,1536]{1,0:T(8,128)(2,1)}) custom-call(bf16[512,1536]{1,0:T(8,128)(2,1)} %bitcast.83, bf16[512,1536]{1,0:T(8,128)(2,1)} %get-tuple-element.136.refs_1_, ...), custom_call_target="tpu_custom_call" | custom-call | tf_op jit(solution)/shard_map/backward_ffn/pallas_call | solution.py:1177
  361.7 62.1 %transfer4.1 = (bf16[512,1536]{1,0:T(8,128)(2,1)}, f32[192,2240]{1,0:T(8,128)}, f32[192,1536]{1,0:T(8,128)}) custom-call(bf16[512,1536]{1,0:T(8,128)(2,1)} %get-tuple-element.142.refs_0_, bf16[8,192,2240]{2,1,0:T(8,128)(2,1)} %bitcast.100, bf16[8,192,1536]{2,1,0:T(8,128)(2,1)} %bitcast.102), custom_call_target="tpu_custom_call" | custom-call | flops 30000001024 | bytes 150000000 | tf_op jit(solution)/shard_map/transfer4/pallas_call | solution.py:607
  423.8 1.0 copy.77.refs_11_.refs_12_
  424.9 0.8 slice_reduce_fusion
  426.1 77.5 %transfer5.1 = (bf16[512,1536]{1,0:T(8,128)(2,1)}, f32[192,2240]{1,0:T(8,128)}, f32[192,704]{1,0:T(8,128)}, f32[192,384]{1,0:T(8,128)}, f32[192,640]{1,0:T(8,128...) custom-call(bf16[8,192,2240]{2,1,0:T(8,128)(2,1)} %bitcast.98, ...), custom_call_target="tpu_custom_call" | custom-call | flops 30000001024 | bytes 150000000 | tf_op jit(solution)/shard_map/transfer5/pallas_call | solution.py:607
  503.7 43.1 %backward_ffn.3 = (bf16[1536,1536]{1,0:T(8,128)(2,1)}, bf16[1536,704]{1,0:T(8,128)(2,1)}, bf16[1536,2240]{1,0:T(8,128)(2,1)}, bf16[1536,2240]{1,0:T(8,128)(2,1)}...) custom-call(f32[512,1536]{1,0:T(8,128)} %get-tuple-element.154.refs_0_, ...), custom_call_target="tpu_custom_call" | custom-call | tf_op jit(solution)/shard_map/backward_ffn/pallas_call | solution.py:1177
  546.8 60.8 %transfer6.1 = (bf16[512,1536]{1,0:T(8,128)(2,1)}, f32[192,2240]{1,0:T(8,128)}, f32[192,1536]{1,0:T(8,128)}) custom-call(bf16[512,1536]{1,0:T(8,128)(2,1)} %get-tuple-element.162.refs_0_, bf16[8,192,2240]{2,1,0:T(8,128)(2,1)} %bitcast.99, bf16[8,192,1536]{2,1,0:T(8,128)(2,1)} %bitcast.101), custom_call_target="tpu_custom_call" | custom-call | flops 30000001024 | bytes 150000000 | tf_op jit(solution)/shard_map/transfer6/pallas_call | solution.py:607
  607.6 1.6 slice.122.refs_2_
  609.2 1.0 slice_bitcast_fusion
  610.2 77.7 %transfer7.1 = (bf16[512,1536]{1,0:T(8,128)(2,1)}, f32[192,2240]{1,0:T(8,128)}, f32[192,704]{1,0:T(8,128)}, f32[192,384]{1,0:T(8,128)}, f32[192,640]{1,0:T(8,128...) custom-call(bf16[8,192,2240]{2,1,0:T(8,128)(2,1)} %bitcast.97, ...), custom_call_target="tpu_custom_call" | custom-call | flops 30000001024 | bytes 150000000 | tf_op jit(solution)/shard_map/transfer7/pallas_call | solution.py:607
  688.0 2.7 fusion.11
  690.8 11.8 %finish.1 = (f32[8,1536]{1,0:T(8,128)S(1)}, bf16[4,192,256]{2,1,0:T(8,128)(2,1)S(1)}) custom-call(f32[1,1536]{1,0:T(1,128)S(1)} %broadcast_in_dim.34.refs_0_, f32[1,1536]{1,0:T(1,128)S(1)} %copy-done.5, f32[1,1536]{1,0:T(1,128)S(1)} %copy-done.4, f32[1,1536]{1,0:T(1,128)S(1)} %copy-done.3, bf16[512,640]{1,0:T(8,128)(2,1)S(1)} %copy-done.2, ...), custom_call_target="tpu_custom_call" | custom-call | tf_op jit(solution)/shard_map/finish/pallas_call | solution.py:928
  702.8 1.7 fusion.12
  707.3 4.1 fusion.6
  712.8 1.6 convert_subtract_fusion.3
  714.5 1.9 convert_subtract_fusion.1
  716.7 1.5 convert_subtract_fusion.2
  718.2 24.7 %pair_adam.1 = (f32[2,192,2,2240]{3,2,1,0:T(2,128)}, f32[2,192,2,2240]{3,2,1,0:T(2,128)}, f32[2,192,2,2240]{3,2,1,0:T(2,128)}, f32[2,192,2,2240]{3,2,1,0:T(2,128)}) custom-call(bf16[2,192,2,2240]{3,2,1,0:T(2,128)(2,1)} %weight.1, f32[2,192,2,2240]{3,2,1,0:T(2,128)} %first.1, f32[2,192,2,2240]{3,2,1,0:T(2,128)} %second.1, ...), custom_call_target="tpu_custom_call" | custom-call | tf_op jit(solution)/shard_map/pair_adam/pallas_call | solution.py:985
  742.9 8.0 %convert_subtract_fusion = (f32[2,2240,192]{1,2,0:T(8,128)}, f32[2,2240,192]{1,2,0:T(8,128)}, f32[2,2240,192]{1,2,0:T(8,128)}, f32[2,2240,192]{1,2,0:T(8,128)}) fusion(bf16[2,2240,192]{1,2,0:T(8,128)(2,1)} %param.37, f32[2,2240,192]{1,2,0:T(8,128)S(1)} %copy-done.7, f32[2,2240,192]{1,2,0:T(8,128)S(1)} %copy-done.8, f32[1,192,704]{2,1,0:T(8,128)} %bitcast.87, ...), kind=kLoop, calls=%fused_computation.5 | loop fusion | flops 16343040 | bytes 25804800 | tf_op jit(solution)/shard_map/sub | solution.py:954
  (122 shorter events, 7.6 us)
Async XLA Ops:
  7.2 418.9 %all-reduce.5.cloned.1.call-start = ((), (), s32[]{:S(2)}) async-start(), calls=%async_computation | async-start | bytes 1572864 | tf_op jit(solution)/shard_map/psum | solution.py:1379
  8.0 5.0 copy-start.28
  323.6 286.6 %all-reduce.7.cloned.1.call-start = ((), (), s32[]{:S(2)}) async-start(), calls=%async_computation.1 | async-start | bytes 1572864 | tf_op jit(solution)/shard_map/psum | solution.py:1473
  361.7 62.1 %copy-start.26 = (s32[1,1024]{1,0:T(1,128)S(1)}, s32[1,1024]{1,0:T(1,128)}, u32[]{:S(2)}) copy-start(s32[1,1024]{1,0:T(1,128)} %refs_9_.1) | copy-start | bytes 12292
  361.7 64.0 %copy-start.6 = (bf16[1,512,1536]{2,1,0:T(8,128)(2,1)S(1)}, bf16[1,512,1536]{2,1,0:T(8,128)(2,1)}, u32[]{:S(2)}) copy-start(bf16[1,512,1536]{2,1,0:T(8,128)(2,1)} %param.27) | copy-start | bytes 4718596
  687.9 2.8 copy-start
  687.9 2.8 copy-start.1
  687.9 2.8 copy-start.2
  687.9 2.8 copy-start.3
  688.0 2.8 copy-start.4
  688.0 2.8 copy-start.5
  688.0 14.6 %copy-start.12 = (bf16[256,1536]{1,0:T(8,128)(2,1)S(1)}, bf16[256,1536]{1,0:T(8,128)(2,1)}, u32[]{:S(2)}) copy-start(bf16[256,1536]{1,0:T(8,128)(2,1)} %all-reduce.5.cloned.1.call-done) | copy-start | bytes 2359300
  688.0 14.6 %copy-start.13 = (bf16[256,1536]{1,0:T(8,128)(2,1)S(1)}, bf16[256,1536]{1,0:T(8,128)(2,1)}, u32[]{:S(2)}) copy-start(bf16[256,1536]{1,0:T(8,128)(2,1)} %all-reduce.7.cloned.1.call-done) | copy-start | bytes 2359300
  690.7 12.1 %copy-start.9 = (f32[512,1536]{1,0:T(8,128)S(1)}, f32[512,1536]{1,0:T(8,128)}, u32[]{:S(2)}) copy-start(f32[512,1536]{1,0:T(8,128)} %get-tuple-element.134.refs_3_) | copy-start | bytes 9437188
  702.8 2.6 copy-start.21
  704.6 7.5 copy-start.27
  704.6 2.6 copy-start.10
  707.3 4.2 copy-start.35
  707.3 4.2 copy-start.36
  707.3 4.2 copy-start.37
  707.3 4.9 copy-start.29
  707.3 4.9 copy-start.31
  707.3 4.9 copy-start.32
  707.3 5.5 copy-start.16
  707.3 5.5 copy-start.17
  707.3 5.5 copy-start.22
  711.4 3.0 copy-start.14
  711.4 3.0 copy-start.15
  711.5 3.0 copy-start.20
  718.2 24.7 %copy-start.7 = (f32[2,2240,192]{1,2,0:T(8,128)S(1)}, f32[2,2240,192]{1,2,0:T(8,128)}, u32[]{:S(2)}) copy-start(f32[2,2240,192]{1,2,0:T(8,128)} %param.53) | copy-start | bytes 10321924
  718.2 24.7 %copy-start.8 = (f32[2,2240,192]{1,2,0:T(8,128)S(1)}, f32[2,2240,192]{1,2,0:T(8,128)}, u32[]{:S(2)}) copy-start(f32[2,2240,192]{1,2,0:T(8,128)} %param.45) | copy-start | bytes 10321924
  718.2 24.7 %copy-start.11 = (f32[192,1536]{1,0:T(8,128)S(1)}, f32[192,1536]{1,0:T(8,128)}, u32[]{:S(2)}) copy-start(f32[192,1536]{1,0:T(8,128)} %get-tuple-element.194) | copy-start | bytes 3538948
  (8 other events, 15.7 us)
Sparse Core Ops, SparseCore 0:
  323.7 42.6 all-reduce.4
  503.8 42.3 all-reduce.6
